TPU v7x, 512 devices: a whole 4x4x16 slice. The times are simulated.
512 devices in a mesh: row: 32 (over z, core), col: 16 (over x, y).
Axes of the slice: x: 4, y: 4, z: 16, core: 2. Of those that a mesh axis runs over, the one named last changes fastest.
Arguments:
- covariance: float32 [2, 4096, 4, 2048], P(None, 'row', None, 'col'), may hold values from 0 to 3, as said below
Outputs:
- factored: float32 [2, 4096, 4, 2048], P(None, 'row', None, 'col')
Inputs may be any that keep to these rules, and one draw needn't show every extreme that they name: `covariance`: the matrix of order 8192 is symmetric positive definite; its diagonal entries lie in 1.5 to 3 and the others in 0 to 1.
All inputs are finite; a program needn't handle non-finite values.
Results may differ from a plain program's by a relative error of at most 0.00018.
Values sent between devices are 32-bit elements; how exact they have to be, the bound alone decides.
No kernel may reach another device: no remote copies, remote signals or barrier semaphores. Data moves between devices by JAX's collectives and lax.ppermute only.
A program may use at most 64 MiB of HBM per device.

v0:
```python
import jax
import jax.numpy as jnp
from jax import lax
from jax.sharding import PartitionSpec as P


def from_root(block, axis, owner):
    block = jnp.where(lax.axis_index(axis) == owner, block, jnp.zeros_like(block))
    return lax.psum(block, axis)


def factor_panel(local, index, row_id, col_id, row_count, col_count):
    tile_rows = local.shape[0]
    block_size = local.shape[1]
    diag_tile = from_root(
        local[index // row_count, :, index // col_count, :], "row", index % row_count
    )
    identity = jnp.eye(block_size, dtype=jnp.float32)
    diag_tile = jnp.where(col_id == index % col_count, diag_tile, identity)
    lower_tile = jnp.linalg.cholesky(diag_tile)
    column = local[:, :, index // col_count, :]
    stacked = jnp.transpose(column, (2, 0, 1)).reshape(block_size, tile_rows * block_size)
    solved = jax.scipy.linalg.solve_triangular(lower_tile, stacked, lower=True)
    panel = jnp.transpose(solved.reshape(block_size, tile_rows, block_size), (1, 2, 0))
    global_rows = jnp.arange(tile_rows) * row_count + row_id
    panel = jnp.where(
        (global_rows > index)[:, None, None],
        panel,
        jnp.where((global_rows == index)[:, None, None], lower_tile[None], jnp.float32(0.0)),
    )
    return from_root(panel, "col", index % col_count)


def place(local, index, panel, row_id, col_id, row_count, col_count, global_cols):
    col_slot = index // col_count
    current = local[:, :, col_slot, :]
    local = local.at[:, :, col_slot, :].set(jnp.where(col_id == index % col_count, panel, current))
    row_slot = index // row_count
    current = local[row_slot]
    wipe = (row_id == index % row_count) & (global_cols > index)[None, :, None]
    return local.at[row_slot].set(jnp.where(wipe, jnp.float32(0.0), current))


def per_device(covariance):
    row_count = lax.axis_size("row")
    col_count = lax.axis_size("col")
    row_id = lax.axis_index("row")
    col_id = lax.axis_index("col")
    ratio = row_count // col_count
    local = covariance
    tile_rows = local.shape[0]
    block_size = local.shape[1]
    tile_cols = local.shape[2]
    global_rows = jnp.arange(tile_rows) * row_count + row_id
    global_cols = jnp.arange(tile_cols) * col_count + col_id
    for index in range(2):
        panel = factor_panel(local, index, row_id, col_id, row_count, col_count)
        pieces = [from_root(panel, "row", col_id + offset * col_count) for offset in range(ratio)]
        across = jnp.stack(pieces, axis=1).reshape(tile_cols, block_size, block_size)
        row_part = jnp.where((global_rows > index)[:, None, None], panel, jnp.float32(0.0))
        col_part = jnp.where((global_cols > index)[:, None, None], across, jnp.float32(0.0))
        local = local - jnp.einsum(
            "lab,mcb->lamc", row_part, col_part, precision=lax.Precision.HIGHEST
        )
        local = place(local, index, panel, row_id, col_id, row_count, col_count, global_cols)
    return local


def solution(mesh):
    in_specs = (P(None, "row", None, "col"),)
    out_specs = P(None, "row", None, "col")
    return jax.shard_map(
        per_device, mesh=mesh, in_specs=in_specs, out_specs=out_specs, check_vma=False
    )
```

profile of v0, /device:TPU:1, one launch (start us, length us, event | category | flops | bytes accessed | tf_op | source)
XLA Modules:
  0.0 1075.4 jit_solution(401243265090646494)
XLA Ops:
  6.5 1.0 slice.133
  8.4 190.0 %all-reduce.9.cloned.1.call-done = f32[128,128]{0,1:T(8,128)} async-done(((f32[128,128]{0,1:T(8,128)}), f32[128,128]{0,1:T(8,128)}) %all-reduce.9.cloned.1.call-update) | async-done | bytes 65552 | tf_op jit(solution)/shard_map/psum | solution.py:9
  198.4 0.9 convert_select_fusion.1
  199.4 0.7 copy-done.3
  200.1 11.7 %cholesky.44 = f32[128,128]{1,0:T(8,128)S(1)} custom-call(f32[128,128]{1,0:T(8,128)S(1)} %fusion.21), custom_call_target="Cholesky" | custom-call | tf_op jit(solution)/shard_map/jit(cholesky)/cholesky | solution.py:20
  213.2 9.8 custom-call.6
  223.5 0.7 fusion.12
  224.3 103.7 %all-reduce.11.cloned.1.call-done = f32[2,128,128]{1,2,0:T(8,128)} async-done(((f32[2,128,128]{1,2,0:T(8,128)}), f32[2,128,128]{1,2,0:T(8,128)}) %all-reduce.11.cloned.1.call-update) | async-done | bytes 131088 | tf_op jit(solution)/shard_map/psum | solution.py:9
  328.0 1.6 select_bitcast_fusion.3
  330.0 208.2 %all-reduce.19.cloned.1.call-done = (f32[2,1,128,128]{2,3,0,1:T(8,128)}, f32[2,1,128,128]{2,3,0,1:T(8,128)}) async-done(((f32[2,1,128,128]{2,3,0,1:T(8,128)}, f32[2,1,128,128]{2,3,0,1:T(8,128)}), (f32[2,1,128,128]{2,3,0,1:T(8,128)}, f32[2,1,128,128]{2,3,0,1:T(8,128)})) %all-reduce.19.cloned.1.call-update) | async-done | bytes 262160 | tf_op jit(solution)/shard_map/psum | solution.py:9
  538.2 1.0 pad_maximum_fusion
  539.5 0.8 copy-done
  542.1 182.9 %all-reduce.13.cloned.1.call-done = f32[128,128]{0,1:T(8,128)} async-done(((f32[128,128]{0,1:T(8,128)}), f32[128,128]{0,1:T(8,128)}) %all-reduce.13.cloned.1.call-update) | async-done | bytes 65552 | tf_op jit(solution)/shard_map/psum | solution.py:9
  725.1 0.7 copy-done.4
  725.9 11.7 %cholesky.55 = f32[128,128]{1,0:T(8,128)S(1)} custom-call(f32[128,128]{1,0:T(8,128)S(1)} %fusion.18), custom_call_target="Cholesky" | custom-call | tf_op jit(solution)/shard_map/jit(cholesky)/cholesky | solution.py:20
  738.3 0.7 select_bitcast_fusion.4
  738.9 9.8 custom-call.7
  749.2 0.7 fusion.10
  750.1 104.5 %all-reduce.15.cloned.1.call-done = f32[2,128,128]{1,2,0:T(8,128)} async-done(((f32[2,128,128]{1,2,0:T(8,128)}), f32[2,128,128]{1,2,0:T(8,128)}) %all-reduce.15.cloned.1.call-update) | async-done | bytes 131088 | tf_op jit(solution)/shard_map/psum | solution.py:9
  854.6 1.6 select_bitcast_fusion.1
  856.2 208.5 %all-reduce.17.cloned.1.call-done = (f32[2,1,128,128]{2,3,0,1:T(8,128)}, f32[2,1,128,128]{2,3,0,1:T(8,128)}) async-done(((f32[2,1,128,128]{2,3,0,1:T(8,128)}, f32[2,1,128,128]{2,3,0,1:T(8,128)}), (f32[2,1,128,128]{2,3,0,1:T(8,128)}, f32[2,1,128,128]{2,3,0,1:T(8,128)})) %all-reduce.17.cloned.1.call-update) | async-done | bytes 262160 | tf_op jit(solution)/shard_map/psum | solution.py:9
  1064.7 1.0 pad_maximum_fusion.1
  1066.0 0.8 copy-done.1
  1067.6 1.0 copy.36
  (59 shorter events, 7.4 us)
Async XLA Ops:
  6.5 191.9 %all-reduce.9.cloned.1.call-start = ((), (), s32[]{:S(2)}) async-start(), calls=%async_computation | async-start | bytes 131072 | tf_op jit(solution)/shard_map/psum | solution.py:9
  8.3 319.7 %all-reduce.11.cloned.1.call-start = ((), (), s32[]{:S(2)}) async-start(), calls=%async_computation.1 | async-start | bytes 262144 | tf_op jit(solution)/shard_map/psum | solution.py:9
  199.3 0.8 copy-start.3
  211.8 11.2 %slice-start = ((f32[2,128,4,128]{3,2,1,0:T(4,128)}), f32[2,128,1,128]{3,2,1,0:T(1,128)S(1)}, s32[]{:S(2)}) async-start(f32[2,128,4,128]{3,2,1,0:T(4,128)} %param.12), calls=%async_computation.6 | async-start | bytes 262144 | tf_op jit(solution)/shard_map/slice | solution.py:21
  223.5 106.3 %copy-start.2 = (f32[2,128,4,128]{3,2,1,0:T(4,128)S(1)}, f32[2,128,4,128]{3,2,1,0:T(4,128)}, u32[]{:S(2)}) copy-start(f32[2,128,4,128]{3,2,1,0:T(4,128)} %param.12) | copy-start | bytes 1572868
  224.3 314.0 %all-reduce.19.cloned.1.call-start = ((), (), s32[]{:S(2)}) async-start(), calls=%async_computation.5 | async-start | bytes 524288 | tf_op jit(solution)/shard_map/psum | solution.py:9
  329.7 395.3 %all-reduce.13.cloned.1.call-start = ((), (), s32[]{:S(2)}) async-start(), calls=%async_computation.2 | async-start | bytes 131072 | tf_op jit(solution)/shard_map/psum | solution.py:9
  539.4 0.9 copy-start
  541.8 312.8 %all-reduce.15.cloned.1.call-start = ((), (), s32[]{:S(2)}) async-start(), calls=%async_computation.3 | async-start | bytes 262144 | tf_op jit(solution)/shard_map/psum | solution.py:9
  725.0 0.8 copy-start.4
  750.0 314.7 %all-reduce.17.cloned.1.call-start = ((), (), s32[]{:S(2)}) async-start(), calls=%async_computation.4 | async-start | bytes 524288 | tf_op jit(solution)/shard_map/psum | solution.py:9
  1065.9 0.9 copy-start.1
Sparse Core Ops, SparseCore 0:
  9.7 188.6 all-reduce.8
  224.4 103.6 all-reduce.10
  330.4 207.7 all-reduce.18
  541.9 183.0 all-reduce.12
  750.1 104.4 all-reduce.14
  856.9 207.7 all-reduce.16
where the time goes:
time: 1080 us
  waiting for transfers between devices  998 us (92%)
  other arithmetic  55.1 us (5%)
  between operations  13.8 us (1%)
    psum x6, waiting for transfers between devices, from_root(): return lax.psum(block, axis)  998 us
    another operation x6, other arithmetic, factor_panel(): lower_tile = jnp.linalg.cholesky(diag_tile)  24.8 us
  transfers between devices with their start and end apart: 6, of which 6 were waited for; matrix products, arithmetic and copies ran while one was open for 0% of the time, Pallas kernels for 0%

commit v1 on v0

v1 whole, which is shorter than its diff:
```python
import jax
import jax.numpy as jnp
from jax import lax
from jax.experimental import pallas as pl
from jax.experimental.pallas import tpu as pltpu
from jax.sharding import PartitionSpec as P

NB = 128
ROWS = 32
COLS = 16
F32 = jnp.float32
VMEM = pl.BlockSpec(memory_space=pltpu.VMEM)
SMEM = pl.BlockSpec(memory_space=pltpu.SMEM)


def dot(a, b, dims):
    return lax.dot_general(
        a, b, (dims, ((), ())), precision=lax.Precision.HIGHEST, preferred_element_type=F32
    )


def move(value, pairs):
    flat = [(sp * COLS + sq, dp * COLS + dq) for (sp, sq), (dp, dq) in pairs]
    return lax.ppermute(value, ("row", "col"), flat)


def eliminate(s_ref, e_ref, u_ref, w_ref):
    sub = lax.broadcasted_iota(jnp.int32, (8, NB), 0)

    def spread(x, j):
        return jnp.broadcast_to(x[j : j + 1, :], (8, NB))

    def splat(x, j):
        return jnp.broadcast_to(x[:, j : j + 1], (8, NB))

    def total(terms):
        while len(terms) > 1:
            terms = [terms[i] + terms[i + 1] for i in range(0, len(terms), 2)]
        return terms[0]

    for k in range(NB // 8):
        here = slice(8 * k, 8 * k + 8)
        s = s_ref[here, :]
        e = e_ref[here, :]
        v = [splat(s, 8 * k + j) for j in range(8)]
        for t in range(8):
            pivot = spread(v[t], t)
            inverse = 1.0 / pivot
            root = lax.rsqrt(pivot)
            me = sub == t
            factor = v[t] * inverse

            def step(x):
                row = spread(x, t)
                return row, jnp.where(me, row * inverse, x - factor * row)

            for j in range(t + 1, 8):
                _, v[j] = step(v[j])
            s_row, s = step(s)
            e_row, e = step(e)
            at = 8 * k + t
            u_ref[at : at + 1, :] = (s_row * root)[:1]
            w_ref[at : at + 1, :] = (e_row * root)[:1]
        zs = [spread(s, j) for j in range(8)]
        ze = [spread(e, j) for j in range(8)]
        for h in range(k + 1, NB // 8):
            there = slice(8 * h, 8 * h + 8)
            x = s_ref[there, :]
            y = e_ref[there, :]
            c = [splat(x, 8 * k + j) for j in range(8)]
            s_ref[there, :] = x - total([c[j] * zs[j] for j in range(8)])
            e_ref[there, :] = y - total([c[j] * ze[j] for j in range(8)])


def identity():
    i = lax.broadcasted_iota(jnp.int32, (NB, NB), 0)
    j = lax.broadcasted_iota(jnp.int32, (NB, NB), 1)
    return i, j, jnp.where(i == j, 1.0, 0.0).astype(F32)


def pick_body(place, x, tile, rows, cols):
    first = x[pl.ds(0, NB, stride=4), :]
    odd = (place[0] & 1) == 1
    tile[...] = jnp.where(odd, first.T, first)
    rows[0:NB, :] = first
    rows[NB:, :] = x[pl.ds(4 * NB, NB, stride=4), :]
    for m in range(4):
        cols[NB * m : NB * (m + 1), :] = x[pl.ds(m, NB, stride=4), :]


def factor_body(place, mine, other, u0, w0, m10, u1, w1, s, e):
    even = (place[0] & 1) == 0
    d00 = jnp.where(even, mine[0:NB, :], other[0:NB, :])
    d11 = jnp.where(even, other[0:NB, :], mine[0:NB, :])
    top = jnp.where(even, mine[NB:, :], other[NB:, :])
    bottom = jnp.where(even, other[NB:, :], mine[NB:, :])
    i, j, eye = identity()
    s[...] = d00
    e[...] = eye
    eliminate(s, e, u0, w0)
    u0[...] = jnp.where(i <= j, u0[...], 0.0)
    d01 = jnp.concatenate([top, bottom], axis=0)
    m = dot(w0[...], d01, ((1,), (0,)))
    m10[...] = m
    s[...] = d11 - dot(m, m, ((0,), (0,)))
    e[...] = eye
    eliminate(s, e, u1, w1)
    u1[...] = jnp.where(i <= j, u1[...], 0.0)


def finish_body(place, x, rows_a, rows_b, cols_a, cols_b, u0, w0, m10, u1, w1, out):
    p = place[0]
    q = place[1]
    even = (p & 1) == 0
    direct = (((q + 1) >> 1) & 1) == 0
    w0v = w0[...]
    w1v = w1[...]
    m = m10[...]
    r0 = jnp.where(direct, rows_a[...], rows_b[...])
    r1 = jnp.where(direct, rows_b[...], rows_a[...])
    y0 = dot(r0, w0v, ((1,), (1,)))
    y1 = dot(r1 - dot(y0, m, ((1,), (0,))), w1v, ((1,), (1,)))
    y = jnp.concatenate([y0, y1], axis=1)
    g0 = u0[...].T
    g1 = u1[...].T
    for t in range(4):
        at = slice(NB * t, NB * (t + 1))
        ca = cols_a[at, :]
        cb = cols_b[at, :]
        c0 = jnp.where(even, ca, cb)
        c1 = jnp.where(even, cb, ca)
        x0 = dot(w0v, c0, ((1,), (0,)))
        x1 = dot(w1v, c1 - dot(m, x0, ((0,), (0,))), ((1,), (0,)))
        xx = jnp.concatenate([x0, x1], axis=0)
        change = dot(y, xx, ((1,), (0,)))
        for l in range(2):
            here = pl.ds(4 * NB * l + t, NB, stride=4)
            rs = slice(NB * l, NB * (l + 1))
            new = x[here, :] - change[rs]
            if t == 0:
                new = jnp.where(q == 0, y0[rs], jnp.where(q == 1, y1[rs], new))
            if l == 0:
                if t == 0:
                    new = jnp.where(
                        p == 0,
                        jnp.where(q == 0, g0, 0.0),
                        jnp.where(
                            p == 1,
                            jnp.where(q == 0, y0[rs], jnp.where(q == 1, g1, 0.0)),
                            new,
                        ),
                    )
                else:
                    new = jnp.where(p < 2, 0.0, new)
            out[here, :] = new


def tile_of(*rows):
    return [jax.ShapeDtypeStruct((r, NB), F32) for r in rows]


def per_device(covariance):
    p = lax.axis_index("row")
    q = lax.axis_index("col")
    z = p >> 1
    x = q >> 2
    y = q & 3
    odd = (p & 1) == 1
    place = jnp.stack([p, q]).astype(jnp.int32)
    local = covariance.reshape(2 * NB * 4, NB)
    tile, rows, cols = pl.pallas_call(
        pick_body,
        out_shape=tile_of(NB, 2 * NB, 4 * NB),
        in_specs=[SMEM, VMEM],
        out_specs=[VMEM] * 3,
    )(place, local)

    cores = (0, 1)
    planes = range(16)
    squares = range(4)

    r1 = move(tile, [((c, a), (c, b)) for c in cores for a, b in ((0, 2), (1, 3))])
    r2 = move(tile, [((c, a), (c, b)) for c in cores for a, b in ((0, 3), (1, 2))])
    r3 = move(tile, [((c, a), (c, b)) for c in cores for a, b in ((0, 1), (1, 0))])
    first = jnp.where(y == 0, tile, jnp.where(y == 1, r3, jnp.where(y == 2, r1, r2)))
    second = jnp.where(y == 0, r3, jnp.where(y == 1, tile, jnp.where(y == 2, r2, r1)))
    diag = jnp.concatenate(
        [
            jnp.where(odd, second, first),
            jnp.where(odd, first[NB // 2 :], second[: NB // 2]),
        ],
        axis=0,
    )
    got = [
        move(diag, [((c, a), (c, 4 * b + a)) for c in cores for a in squares]) for b in (2, 1, 3)
    ]
    diag = jnp.where(x == 0, diag, got[0] + got[1] + got[2])
    got = [
        move(diag, [((c, a), (2 * b + c, a)) for c in cores for a in range(COLS)]) for b in (8, 4, 12)
    ]
    diag = jnp.where(z == 0, diag, got[0] + got[1] + got[2])
    got = [
        move(
            diag,
            [
                ((2 * s + c, a), (2 * (s + b) + c, a))
                for c in cores
                for s in (0, 4, 8, 12)
                for a in range(COLS)
            ],
        )
        for b in (2, 1, 3)
    ]
    diag = jnp.where((z & 3) == 0, diag, got[0] + got[1] + got[2])
    swap = [((r, a), (r ^ 1, a)) for r in range(ROWS) for a in range(COLS)]
    other = move(diag, swap)

    got = move(rows, [((r, a), (r, b)) for r in range(ROWS) for a, b in ((0, 3), (1, 2))])
    rows = jnp.where(y >= 2, got, rows)
    got = move(rows, [((r, a), (r, 8 + a)) for r in range(ROWS) for a in squares])
    rows = jnp.where(x == 2, got, rows)
    got = move(
        rows, [((r, 4 * b + a), (r, 4 * b + 4 + a)) for r in range(ROWS) for b in (0, 2) for a in squares]
    )
    rows = jnp.where((x & 1) == 1, got, rows)
    rows_b = move(
        rows, [((r, a), (r, a ^ 1)) for r in range(ROWS) for a in range(COLS)]
    )

    for stride in (8, 4, 2, 1):
        pairs = []
        for s in range(0, 16, 2 * stride):
            for c in cores:
                d = (s + stride if c == 0 else s - stride) % 16
                pairs += [((2 * s + c, a), (2 * d + c, a)) for a in range(COLS)]
        got = move(cols, pairs)
        cols = jnp.where((z & (2 * stride - 1)) == stride, got, cols)
    cols_b = move(cols, swap)

    factors = pl.pallas_call(
        factor_body,
        out_shape=tile_of(*([NB] * 5)),
        in_specs=[SMEM, VMEM, VMEM],
        out_specs=[VMEM] * 5,
        scratch_shapes=[pltpu.VMEM((NB, NB), F32)] * 2,
        cost_estimate=pl.CostEstimate(flops=10_000_000, bytes_accessed=400_000, transcendentals=0),
    )(place, diag, other)
    out = pl.pallas_call(
        finish_body,
        out_shape=jax.ShapeDtypeStruct((2 * NB * 4, NB), F32),
        in_specs=[SMEM] + [VMEM] * 10,
        out_specs=VMEM,
    )(place, local, rows, rows_b, cols, cols_b, *factors)
    return out.reshape(covariance.shape)


def solution(mesh):
    spec = P(None, "row", None, "col")
    return jax.shard_map(
        per_device, mesh=mesh, in_specs=(spec,), out_specs=spec, check_vma=False
    )
```

time: 1080 us -> 88.4 us (0.08)
  waiting for transfers between devices: 998 us -> 5.01 us
  starting transfers between devices: 0.39 us -> 60.6 us
  other arithmetic: 55.1 us -> 1.86 us
  Pallas kernels: 0 us -> 18.3 us
  between operations: 13.8 us -> 0.53 us
    psum x6 -> x0, waiting for transfers between devices: 998 us -> none  [from_root(): return lax.psum(block, axis)]
    ppermute x0 -> x22, starting transfers between devices: none -> 60.6 us  [move(): return lax.ppermute(value, ('row', 'col'), flat)]
    another operation x14 -> x1, other arithmetic: 50.9 us -> 0.67 us  [per_device(): place = jnp.stack([p, q]).astype(jnp.int32)]
    pallas_call x0 -> x3, Pallas kernels: none -> 18.3 us  [the longest x1 11.3 us: per_device(): pl.pallas_call(factor_body, out_shape=tile_of(*[NB] * 5), in_specs=[SMEM,...]
  transfers between devices with their start and end apart: 6 -> 22, of which waited for: 6 -> 2; matrix products, arithmetic and copies ran while one was open for 0% -> 1% of each run, Pallas kernels for 0% -> 13%
where the time goes in v1:
time: 88.4 us; the launch traced here: 87.8 us
  starting transfers between devices  60.6 us (69%)
  Pallas kernels  18.3 us (21%)
  waiting for transfers between devices  5.01 us (6%)
  other arithmetic  1.86 us (2%)
  local copies, waits for them, and re-layouts  1.41 us (2%)
    ppermute x22, starting transfers between devices, move(): return lax.ppermute(value, ('row', 'col'), flat)  60.6 us
    pallas_call x1, Pallas kernels, per_device(): pl.pallas_call(factor_body, out_shape=tile_of(*[NB] * 5), in_specs=[SMEM,...  11.3 us
    pallas_call x1, Pallas kernels, per_device(): pl.pallas_call(finish_body, out_shape=jax.ShapeDtypeStruct((2 * NB * 4, N...  5.17 us
    ppermute x22, waiting for transfers between devices, move(): return lax.ppermute(value, ('row', 'col'), flat)  5.01 us
    pallas_call x1, Pallas kernels, per_device(): pl.pallas_call(pick_body, out_shape=tile_of(NB, 2 * NB, 4 * NB), in_specs...  1.81 us
  transfers between devices with their start and end apart: 22, of which 2 were waited for; matrix products, arithmetic and copies ran while one was open for 1% of the time, Pallas kernels for 13%

profile of v1, /device:TPU:1, one launch (start us, length us, event | category | flops | bytes accessed | tf_op | source)
XLA Modules:
  0.0 87.8 jit_solution(8378784064038285939)
XLA Ops:
  0.7 1.8 %shard_map.17 = (f32[128,128]{1,0:T(8,128)}, f32[256,128]{1,0:T(8,128)}, f32[512,128]{1,0:T(8,128)}) custom-call(s32[2]{0:T(128)} %pad_add_fusion.place, f32[1024,128]{1,0:T(8,128)} %bitcast.4), custom_call_target="tpu_custom_call" | custom-call | tf_op jit(solution)/shard_map/pallas_call | solution.py:171
  2.5 5.6 %collective-permute-start.11 = (f32[128,128]{1,0:T(8,128)}, f32[128,128]{1,0:T(8,128)S(1)}, u32[]{:S(2)}, u32[]{:S(2)}) collective-permute-start(f32[128,128]{1,0:T(8,128)} %get-tuple-element.15), channel_id=1, source_target_pairs={{0,2},{1,3},{16,18},{17,19}} | collective-permute-start | bytes 196616 | tf_op jit(solution)/shard_map/ppermute | solution.py:24
  9.4 2.3 %collective-permute-start.9 = (f32[128,128]{1,0:T(8,128)}, f32[128,128]{1,0:T(8,128)S(1)}, u32[]{:S(2)}, u32[]{:S(2)}) collective-permute-start(f32[128,128]{1,0:T(8,128)} %get-tuple-element.15), channel_id=1, source_target_pairs={{0,1},{1,0},{16,17},{17,16}} | collective-permute-start | bytes 196616 | tf_op jit(solution)/shard_map/ppermute | solution.py:24
  11.7 1.3 %collective-permute-start = (f32[256,128]{1,0:T(8,128)}, f32[256,128]{1,0:T(8,128)S(1)}, u32[]{:S(2)}, u32[]{:S(2)}) collective-permute-start(f32[256,128]{1,0:T(8,128)} %get-tuple-element.13), channel_id=1, source_target_pairs={{0,3},{1,2},{16,19},{17,18},{32,35},{33,34},{48,51},{49,50},{64,67... | collective-permute-start | bytes 393224 | tf_op jit(solution)/shard_map/ppermute | solution.py:24
  13.0 12.4 %collective-permute-start.4 = (f32[512,128]{1,0:T(8,128)}, f32[512,128]{1,0:T(8,128)S(1)}, u32[]{:S(2)}, u32[]{:S(2)}) collective-permute-start(f32[512,128]{1,0:T(8,128)} %get-tuple-element.14), channel_id=1, source_target_pairs={{0,256},{1,257},{2,258},{3,259},{4,260},{5,261},{6,262},{7,263},{8... | collective-permute-start | bytes 786440 | tf_op jit(solution)/shard_map/ppermute | solution.py:24
  26.4 3.9 %collective-permute-done.4 = f32[512,128]{1,0:T(8,128)S(1)} collective-permute-done((f32[512,128]{1,0:T(8,128)}, f32[512,128]{1,0:T(8,128)S(1)}, u32[]{:S(2)}, u32[]{:S(2)}) %collective-permute-start.4) | collective-permute-done | bytes 262176 | tf_op jit(solution)/shard_map/ppermute | solution.py:24
  30.4 1.4 %collective-permute-start.5 = (f32[512,128]{1,0:T(8,128)S(1)}, f32[512,128]{1,0:T(8,128)S(1)}, u32[]{:S(2)}, u32[]{:S(2)}) collective-permute-start(f32[512,128]{1,0:T(8,128)S(1)} %broadcast_select_fusion), channel_id=1, source_target_pairs={{0,128},{1,129},{2,130},{3,131},{4,132},{5,133},{6,134},{7,135},{8... | collective-permute-start | bytes 786440 | tf_op jit(solution)/shard_map/ppermute | solution.py:24
  31.9 1.3 %collective-permute-start.14 = (f32[192,128]{1,0:T(8,128)S(1)}, f32[192,128]{1,0:T(8,128)S(1)}, u32[]{:S(2)}, u32[]{:S(2)}) collective-permute-start(f32[192,128]{1,0:T(8,128)S(1)} %pad_maximum_fusion), channel_id=1, source_target_pairs={{0,12},{1,13},{2,14},{3,15},{16,28},{17,29},{18,30},{19,31}} | collective-permute-start | bytes 294920 | tf_op jit(solution)/shard_map/ppermute | solution.py:24
  33.2 1.3 %collective-permute-start.13 = (f32[192,128]{1,0:T(8,128)S(1)}, f32[192,128]{1,0:T(8,128)S(1)}, u32[]{:S(2)}, u32[]{:S(2)}) collective-permute-start(f32[192,128]{1,0:T(8,128)S(1)} %pad_maximum_fusion), channel_id=1, source_target_pairs={{0,4},{1,5},{2,6},{3,7},{16,20},{17,21},{18,22},{19,23}} | collective-permute-start | bytes 294920 | tf_op jit(solution)/shard_map/ppermute | solution.py:24
  34.5 1.3 %collective-permute-start.12 = (f32[192,128]{1,0:T(8,128)S(1)}, f32[192,128]{1,0:T(8,128)S(1)}, u32[]{:S(2)}, u32[]{:S(2)}) collective-permute-start(f32[192,128]{1,0:T(8,128)S(1)} %pad_maximum_fusion), channel_id=1, source_target_pairs={{0,8},{1,9},{2,10},{3,11},{16,24},{17,25},{18,26},{19,27}} | collective-permute-start | bytes 294920 | tf_op jit(solution)/shard_map/ppermute | solution.py:24
  35.8 1.3 %collective-permute-start.1 = (f32[256,128]{1,0:T(8,128)S(1)}, f32[256,128]{1,0:T(8,128)S(1)}, u32[]{:S(2)}, u32[]{:S(2)}) collective-permute-start(f32[256,128]{1,0:T(8,128)S(1)} %broadcast_select_fusion.4), channel_id=1, source_target_pairs={{0,8},{1,9},{2,10},{3,11},{16,24},{17,25},{18,26},{19,27},{32,40},... | collective-permute-start | bytes 393224 | tf_op jit(solution)/shard_map/ppermute | solution.py:24
  37.2 1.3 %collective-permute-start.6 = (f32[512,128]{1,0:T(8,128)S(1)}, f32[512,128]{1,0:T(8,128)S(1)}, u32[]{:S(2)}, u32[]{:S(2)}) collective-permute-start(f32[512,128]{1,0:T(8,128)S(1)} %broadcast_select_fusion.1), channel_id=1, source_target_pairs={{0,64},{1,65},{2,66},{3,67},{4,68},{5,69},{6,70},{7,71},{8,72},{9,... | collective-permute-start | bytes 786440 | tf_op jit(solution)/shard_map/ppermute | solution.py:24
  38.6 5.7 %collective-permute-start.17 = (f32[192,128]{1,0:T(8,128)S(1)}, f32[192,128]{1,0:T(8,128)S(1)}, u32[]{:S(2)}, u32[]{:S(2)}) collective-permute-start(f32[192,128]{1,0:T(8,128)S(1)} %add_select_fusion.2), channel_id=1, source_target_pairs={{0,384},{1,385},{2,386},{3,387},{4,388},{5,389},{6,390},{7,391},{8... | collective-permute-start | bytes 294920 | tf_op jit(solution)/shard_map/ppermute | solution.py:24
  44.3 6.4 %collective-permute-start.16 = (f32[192,128]{1,0:T(8,128)S(1)}, f32[192,128]{1,0:T(8,128)S(1)}, u32[]{:S(2)}, u32[]{:S(2)}) collective-permute-start(f32[192,128]{1,0:T(8,128)S(1)} %add_select_fusion.2), channel_id=1, source_target_pairs={{0,128},{1,129},{2,130},{3,131},{4,132},{5,133},{6,134},{7,135},{8... | collective-permute-start | bytes 294920 | tf_op jit(solution)/shard_map/ppermute | solution.py:24
  50.7 1.3 %collective-permute-start.15 = (f32[192,128]{1,0:T(8,128)S(1)}, f32[192,128]{1,0:T(8,128)S(1)}, u32[]{:S(2)}, u32[]{:S(2)}) collective-permute-start(f32[192,128]{1,0:T(8,128)S(1)} %add_select_fusion.2), channel_id=1, source_target_pairs={{0,256},{1,257},{2,258},{3,259},{4,260},{5,261},{6,262},{7,263},{8... | collective-permute-start | bytes 294920 | tf_op jit(solution)/shard_map/ppermute | solution.py:24
  52.0 1.3 %collective-permute-start.2 = (f32[256,128]{1,0:T(8,128)S(1)}, f32[256,128]{1,0:T(8,128)S(1)}, u32[]{:S(2)}, u32[]{:S(2)}) collective-permute-start(f32[256,128]{1,0:T(8,128)S(1)} %broadcast_select_fusion.5), channel_id=1, source_target_pairs={{0,4},{1,5},{2,6},{3,7},{8,12},{9,13},{10,14},{11,15},{16,20},{17,... | collective-permute-start | bytes 393224 | tf_op jit(solution)/shard_map/ppermute | solution.py:24
  53.4 1.3 %collective-permute-start.7 = (f32[512,128]{1,0:T(8,128)S(1)}, f32[512,128]{1,0:T(8,128)S(1)}, u32[]{:S(2)}, u32[]{:S(2)}) collective-permute-start(f32[512,128]{1,0:T(8,128)S(1)} %broadcast_select_fusion.2), channel_id=1, source_target_pairs={{0,32},{1,33},{2,34},{3,35},{4,36},{5,37},{6,38},{7,39},{8,40},{9,... | collective-permute-start | bytes 786440 | tf_op jit(solution)/shard_map/ppermute | solution.py:24
  54.8 1.3 %collective-permute-start.20 = (f32[192,128]{1,0:T(8,128)S(1)}, f32[192,128]{1,0:T(8,128)S(1)}, u32[]{:S(2)}, u32[]{:S(2)}) collective-permute-start(f32[192,128]{1,0:T(8,128)S(1)} %add_select_fusion.1), channel_id=1, source_target_pairs={{0,96},{1,97},{2,98},{3,99},{4,100},{5,101},{6,102},{7,103},{8,104... | collective-permute-start | bytes 294920 | tf_op jit(solution)/shard_map/ppermute | solution.py:24
  56.1 1.3 %collective-permute-start.19 = (f32[192,128]{1,0:T(8,128)S(1)}, f32[192,128]{1,0:T(8,128)S(1)}, u32[]{:S(2)}, u32[]{:S(2)}) collective-permute-start(f32[192,128]{1,0:T(8,128)S(1)} %add_select_fusion.1), channel_id=1, source_target_pairs={{0,32},{1,33},{2,34},{3,35},{4,36},{5,37},{6,38},{7,39},{8,40},{9,... | collective-permute-start | bytes 294920 | tf_op jit(solution)/shard_map/ppermute | solution.py:24
  58.7 1.9 %collective-permute-start.3 = (f32[256,128]{1,0:T(8,128)S(1)}, f32[256,128]{1,0:T(8,128)S(1)}, u32[]{:S(2)}, u32[]{:S(2)}) collective-permute-start(f32[256,128]{1,0:T(8,128)S(1)} %broadcast_select_fusion.6.rows_a), channel_id=1, source_target_pairs={{0,1},{1,0},{2,3},{3,2},{4,5},{5,4},{6,7},{7,6},{8,9},{9,8},{10,11... | collective-permute-start | bytes 393224 | tf_op jit(solution)/shard_map/ppermute | solution.py:24
  60.7 5.8 %collective-permute-start.8 = (f32[512,128]{1,0:T(8,128)S(1)}, f32[512,128]{1,0:T(8,128)S(1)}, u32[]{:S(2)}, u32[]{:S(2)}) collective-permute-start(f32[512,128]{1,0:T(8,128)S(1)} %broadcast_select_fusion.3.cols_a), channel_id=1, source_target_pairs={{0,16},{1,17},{2,18},{3,19},{4,20},{5,21},{6,22},{7,23},{8,24},{9,... | collective-permute-start | bytes 786440 | tf_op jit(solution)/shard_map/ppermute | solution.py:24
  66.6 2.2 %collective-permute-start.21 = (f32[192,128]{1,0:T(8,128)S(1)}, f32[192,128]{1,0:T(8,128)S(1)}, u32[]{:S(2)}, u32[]{:S(2)}) collective-permute-start(f32[192,128]{1,0:T(8,128)S(1)} %add_select_fusion.mine), channel_id=1, source_target_pairs={{0,16},{1,17},{2,18},{3,19},{4,20},{5,21},{6,22},{7,23},{8,24},{9,... | collective-permute-start | bytes 294920 | tf_op jit(solution)/shard_map/ppermute | solution.py:24
  70.5 11.3 %shard_map.18 = (f32[128,128]{1,0:T(8,128)}, f32[128,128]{1,0:T(8,128)}, f32[128,128]{1,0:T(8,128)}, f32[128,128]{1,0:T(8,128)}, f32[128,128]{1,0:T(8,128)}) custom-call(s32[2]{0:T(128)} %pad_add_fusion.place, f32[192,128]{1,0:T(8,128)} %copy-done.2, f32[192,128]{1,0:T(8,128)} %copy-done.7), custom_call_target="tpu_custom_call" | custom-call | flops 10000000 | bytes 400000 | tf_op jit(solution)/shard_map/pallas_call | solution.py:240
  82.6 5.2 %shard_map.19 = f32[1024,128]{1,0:T(8,128)} custom-call(s32[2]{0:T(128)} %pad_add_fusion.place, f32[1024,128]{1,0:T(8,128)} %bitcast.5, f32[256,128]{1,0:T(8,128)} %copy-done.1, f32[256,128]{1,0:T(8,128)} %copy-done.5, f32[512,128]{1,0:T(8,128)} %copy-done, f32[512,128]{1,0:T(8,128)} %copy-done.3, f32[128,128]{1,0:T(8,128)} %get-tuple-element.16.u0, ...), custom_call_target="tpu_custom_call" | custom-call | tf_op jit(solution)/shard_map/pallas_call | solution.py:248
  (53 shorter events, 6.9 us)
Async XLA Ops:
  2.5 23.0 %collective-permute-start.11 = (f32[128,128]{1,0:T(8,128)}, f32[128,128]{1,0:T(8,128)S(1)}, u32[]{:S(2)}, u32[]{:S(2)}) collective-permute-start(f32[128,128]{1,0:T(8,128)} %get-tuple-element.15), channel_id=1, source_target_pairs={{0,2},{1,3},{16,18},{17,19}} | collective-permute-start | bytes 196616 | tf_op jit(solution)/shard_map/ppermute | solution.py:24
  8.1 17.4 %collective-permute-start.10 = (f32[128,128]{1,0:T(8,128)}, f32[128,128]{1,0:T(8,128)S(1)}, u32[]{:S(2)}, u32[]{:S(2)}) collective-permute-start(f32[128,128]{1,0:T(8,128)} %get-tuple-element.15), channel_id=1, source_target_pairs={{0,3},{1,2},{16,19},{17,18}} | collective-permute-start | bytes 196616 | tf_op jit(solution)/shard_map/ppermute | solution.py:24
  9.4 16.1 %collective-permute-start.9 = (f32[128,128]{1,0:T(8,128)}, f32[128,128]{1,0:T(8,128)S(1)}, u32[]{:S(2)}, u32[]{:S(2)}) collective-permute-start(f32[128,128]{1,0:T(8,128)} %get-tuple-element.15), channel_id=1, source_target_pairs={{0,1},{1,0},{16,17},{17,16}} | collective-permute-start | bytes 196616 | tf_op jit(solution)/shard_map/ppermute | solution.py:24
  11.7 24.1 %collective-permute-start = (f32[256,128]{1,0:T(8,128)}, f32[256,128]{1,0:T(8,128)S(1)}, u32[]{:S(2)}, u32[]{:S(2)}) collective-permute-start(f32[256,128]{1,0:T(8,128)} %get-tuple-element.13), channel_id=1, source_target_pairs={{0,3},{1,2},{16,19},{17,18},{32,35},{33,34},{48,51},{49,50},{64,67... | collective-permute-start | bytes 393224 | tf_op jit(solution)/shard_map/ppermute | solution.py:24
  13.0 17.3 %collective-permute-start.4 = (f32[512,128]{1,0:T(8,128)}, f32[512,128]{1,0:T(8,128)S(1)}, u32[]{:S(2)}, u32[]{:S(2)}) collective-permute-start(f32[512,128]{1,0:T(8,128)} %get-tuple-element.14), channel_id=1, source_target_pairs={{0,256},{1,257},{2,258},{3,259},{4,260},{5,261},{6,262},{7,263},{8... | collective-permute-start | bytes 786440 | tf_op jit(solution)/shard_map/ppermute | solution.py:24
  30.4 5.4 %copy-start.6 = (f32[256,128]{1,0:T(8,128)S(1)}, f32[256,128]{1,0:T(8,128)}, u32[]{:S(2)}) copy-start(f32[256,128]{1,0:T(8,128)} %get-tuple-element.13) | copy-start | bytes 393220
  30.4 6.7 %collective-permute-start.5 = (f32[512,128]{1,0:T(8,128)S(1)}, f32[512,128]{1,0:T(8,128)S(1)}, u32[]{:S(2)}, u32[]{:S(2)}) collective-permute-start(f32[512,128]{1,0:T(8,128)S(1)} %broadcast_select_fusion), channel_id=1, source_target_pairs={{0,128},{1,129},{2,130},{3,131},{4,132},{5,133},{6,134},{7,135},{8... | collective-permute-start | bytes 786440 | tf_op jit(solution)/shard_map/ppermute | solution.py:24
  31.9 6.6 %collective-permute-start.14 = (f32[192,128]{1,0:T(8,128)S(1)}, f32[192,128]{1,0:T(8,128)S(1)}, u32[]{:S(2)}, u32[]{:S(2)}) collective-permute-start(f32[192,128]{1,0:T(8,128)S(1)} %pad_maximum_fusion), channel_id=1, source_target_pairs={{0,12},{1,13},{2,14},{3,15},{16,28},{17,29},{18,30},{19,31}} | collective-permute-start | bytes 294920 | tf_op jit(solution)/shard_map/ppermute | solution.py:24
  33.2 5.3 %collective-permute-start.13 = (f32[192,128]{1,0:T(8,128)S(1)}, f32[192,128]{1,0:T(8,128)S(1)}, u32[]{:S(2)}, u32[]{:S(2)}) collective-permute-start(f32[192,128]{1,0:T(8,128)S(1)} %pad_maximum_fusion), channel_id=1, source_target_pairs={{0,4},{1,5},{2,6},{3,7},{16,20},{17,21},{18,22},{19,23}} | collective-permute-start | bytes 294920 | tf_op jit(solution)/shard_map/ppermute | solution.py:24
  34.5 4.0 %collective-permute-start.12 = (f32[192,128]{1,0:T(8,128)S(1)}, f32[192,128]{1,0:T(8,128)S(1)}, u32[]{:S(2)}, u32[]{:S(2)}) collective-permute-start(f32[192,128]{1,0:T(8,128)S(1)} %pad_maximum_fusion), channel_id=1, source_target_pairs={{0,8},{1,9},{2,10},{3,11},{16,24},{17,25},{18,26},{19,27}} | collective-permute-start | bytes 294920 | tf_op jit(solution)/shard_map/ppermute | solution.py:24
  35.8 16.2 %collective-permute-start.1 = (f32[256,128]{1,0:T(8,128)S(1)}, f32[256,128]{1,0:T(8,128)S(1)}, u32[]{:S(2)}, u32[]{:S(2)}) collective-permute-start(f32[256,128]{1,0:T(8,128)S(1)} %broadcast_select_fusion.4), channel_id=1, source_target_pairs={{0,8},{1,9},{2,10},{3,11},{16,24},{17,25},{18,26},{19,27},{32,40},... | collective-permute-start | bytes 393224 | tf_op jit(solution)/shard_map/ppermute | solution.py:24
  37.2 16.1 %collective-permute-start.6 = (f32[512,128]{1,0:T(8,128)S(1)}, f32[512,128]{1,0:T(8,128)S(1)}, u32[]{:S(2)}, u32[]{:S(2)}) collective-permute-start(f32[512,128]{1,0:T(8,128)S(1)} %broadcast_select_fusion.1), channel_id=1, source_target_pairs={{0,64},{1,65},{2,66},{3,67},{4,68},{5,69},{6,70},{7,71},{8,72},{9,... | collective-permute-start | bytes 786440 | tf_op jit(solution)/shard_map/ppermute | solution.py:24
  38.6 16.1 %collective-permute-start.17 = (f32[192,128]{1,0:T(8,128)S(1)}, f32[192,128]{1,0:T(8,128)S(1)}, u32[]{:S(2)}, u32[]{:S(2)}) collective-permute-start(f32[192,128]{1,0:T(8,128)S(1)} %add_select_fusion.2), channel_id=1, source_target_pairs={{0,384},{1,385},{2,386},{3,387},{4,388},{5,389},{6,390},{7,391},{8... | collective-permute-start | bytes 294920 | tf_op jit(solution)/shard_map/ppermute | solution.py:24
  44.3 10.4 %collective-permute-start.16 = (f32[192,128]{1,0:T(8,128)S(1)}, f32[192,128]{1,0:T(8,128)S(1)}, u32[]{:S(2)}, u32[]{:S(2)}) collective-permute-start(f32[192,128]{1,0:T(8,128)S(1)} %add_select_fusion.2), channel_id=1, source_target_pairs={{0,128},{1,129},{2,130},{3,131},{4,132},{5,133},{6,134},{7,135},{8... | collective-permute-start | bytes 294920 | tf_op jit(solution)/shard_map/ppermute | solution.py:24
  50.7 4.0 %collective-permute-start.15 = (f32[192,128]{1,0:T(8,128)S(1)}, f32[192,128]{1,0:T(8,128)S(1)}, u32[]{:S(2)}, u32[]{:S(2)}) collective-permute-start(f32[192,128]{1,0:T(8,128)S(1)} %add_select_fusion.2), channel_id=1, source_target_pairs={{0,256},{1,257},{2,258},{3,259},{4,260},{5,261},{6,262},{7,263},{8... | collective-permute-start | bytes 294920 | tf_op jit(solution)/shard_map/ppermute | solution.py:24
  52.0 6.6 %collective-permute-start.2 = (f32[256,128]{1,0:T(8,128)S(1)}, f32[256,128]{1,0:T(8,128)S(1)}, u32[]{:S(2)}, u32[]{:S(2)}) collective-permute-start(f32[256,128]{1,0:T(8,128)S(1)} %broadcast_select_fusion.5), channel_id=1, source_target_pairs={{0,4},{1,5},{2,6},{3,7},{8,12},{9,13},{10,14},{11,15},{16,20},{17,... | collective-permute-start | bytes 393224 | tf_op jit(solution)/shard_map/ppermute | solution.py:24
  53.4 7.3 %collective-permute-start.7 = (f32[512,128]{1,0:T(8,128)S(1)}, f32[512,128]{1,0:T(8,128)S(1)}, u32[]{:S(2)}, u32[]{:S(2)}) collective-permute-start(f32[512,128]{1,0:T(8,128)S(1)} %broadcast_select_fusion.2), channel_id=1, source_target_pairs={{0,32},{1,33},{2,34},{3,35},{4,36},{5,37},{6,38},{7,39},{8,40},{9,... | collective-permute-start | bytes 786440 | tf_op jit(solution)/shard_map/ppermute | solution.py:24
  54.8 11.8 %collective-permute-start.20 = (f32[192,128]{1,0:T(8,128)S(1)}, f32[192,128]{1,0:T(8,128)S(1)}, u32[]{:S(2)}, u32[]{:S(2)}) collective-permute-start(f32[192,128]{1,0:T(8,128)S(1)} %add_select_fusion.1), channel_id=1, source_target_pairs={{0,96},{1,97},{2,98},{3,99},{4,100},{5,101},{6,102},{7,103},{8,104... | collective-permute-start | bytes 294920 | tf_op jit(solution)/shard_map/ppermute | solution.py:24
  56.1 10.5 %collective-permute-start.19 = (f32[192,128]{1,0:T(8,128)S(1)}, f32[192,128]{1,0:T(8,128)S(1)}, u32[]{:S(2)}, u32[]{:S(2)}) collective-permute-start(f32[192,128]{1,0:T(8,128)S(1)} %add_select_fusion.1), channel_id=1, source_target_pairs={{0,32},{1,33},{2,34},{3,35},{4,36},{5,37},{6,38},{7,39},{8,40},{9,... | collective-permute-start | bytes 294920 | tf_op jit(solution)/shard_map/ppermute | solution.py:24
  57.4 9.2 %collective-permute-start.18 = (f32[192,128]{1,0:T(8,128)S(1)}, f32[192,128]{1,0:T(8,128)S(1)}, u32[]{:S(2)}, u32[]{:S(2)}) collective-permute-start(f32[192,128]{1,0:T(8,128)S(1)} %add_select_fusion.1), channel_id=1, source_target_pairs={{0,64},{1,65},{2,66},{3,67},{4,68},{5,69},{6,70},{7,71},{8,72},{9,... | collective-permute-start | bytes 294920 | tf_op jit(solution)/shard_map/ppermute | solution.py:24
  58.7 23.1 %collective-permute-start.3 = (f32[256,128]{1,0:T(8,128)S(1)}, f32[256,128]{1,0:T(8,128)S(1)}, u32[]{:S(2)}, u32[]{:S(2)}) collective-permute-start(f32[256,128]{1,0:T(8,128)S(1)} %broadcast_select_fusion.6.rows_a), channel_id=1, source_target_pairs={{0,1},{1,0},{2,3},{3,2},{4,5},{5,4},{6,7},{7,6},{8,9},{9,8},{10,11... | collective-permute-start | bytes 393224 | tf_op jit(solution)/shard_map/ppermute | solution.py:24
  60.7 21.1 %copy-start = (f32[512,128]{1,0:T(8,128)}, f32[512,128]{1,0:T(8,128)S(1)}, u32[]{:S(2)}) copy-start(f32[512,128]{1,0:T(8,128)S(1)} %broadcast_select_fusion.3.cols_a) | copy-start | bytes 786436
  60.7 21.1 %collective-permute-start.8 = (f32[512,128]{1,0:T(8,128)S(1)}, f32[512,128]{1,0:T(8,128)S(1)}, u32[]{:S(2)}, u32[]{:S(2)}) collective-permute-start(f32[512,128]{1,0:T(8,128)S(1)} %broadcast_select_fusion.3.cols_a), channel_id=1, source_target_pairs={{0,16},{1,17},{2,18},{3,19},{4,20},{5,21},{6,22},{7,23},{8,24},{9,... | collective-permute-start | bytes 786440 | tf_op jit(solution)/shard_map/ppermute | solution.py:24
  66.6 3.2 %collective-permute-start.21 = (f32[192,128]{1,0:T(8,128)S(1)}, f32[192,128]{1,0:T(8,128)S(1)}, u32[]{:S(2)}, u32[]{:S(2)}) collective-permute-start(f32[192,128]{1,0:T(8,128)S(1)} %add_select_fusion.mine), channel_id=1, source_target_pairs={{0,16},{1,17},{2,18},{3,19},{4,20},{5,21},{6,22},{7,23},{8,24},{9,... | collective-permute-start | bytes 294920 | tf_op jit(solution)/shard_map/ppermute | solution.py:24
  (6 other events, 12.2 us)

commit v2 on v1

--- a/solution.py
+++ b/solution.py
@@ -10,7 +10,7 @@
 COLS = 16
 F32 = jnp.float32
 VMEM = pl.BlockSpec(memory_space=pltpu.VMEM)
-SMEM = pl.BlockSpec(memory_space=pltpu.SMEM)
+PARAMS = pltpu.CompilerParams(vmem_limit_bytes=8 * 2**20)
 
 
 def dot(a, b, dims):
@@ -22,6 +22,10 @@
 def move(value, pairs):
     flat = [(sp * COLS + sq, dp * COLS + dq) for (sp, sq), (dp, dq) in pairs]
     return lax.ppermute(value, ("row", "col"), flat)
+
+
+def after(value, earlier):
+    return lax.optimization_barrier((value, earlier))[0]
 
 
 def eliminate(s_ref, e_ref, u_ref, w_ref):
@@ -78,9 +82,9 @@
     return i, j, jnp.where(i == j, 1.0, 0.0).astype(F32)
 
 
-def pick_body(place, x, tile, rows, cols):
+def pick_body(x, tile, rows, cols):
     first = x[pl.ds(0, NB, stride=4), :]
-    odd = (place[0] & 1) == 1
+    odd = (lax.axis_index("row") & 1) == 1
     tile[...] = jnp.where(odd, first.T, first)
     rows[0:NB, :] = first
     rows[NB:, :] = x[pl.ds(4 * NB, NB, stride=4), :]
@@ -88,8 +92,8 @@
         cols[NB * m : NB * (m + 1), :] = x[pl.ds(m, NB, stride=4), :]
 
 
-def factor_body(place, mine, other, u0, w0, m10, u1, w1, s, e):
-    even = (place[0] & 1) == 0
+def first_body(mine, other, u0, w0, m10, s11, s, e):
+    even = (lax.axis_index("row") & 1) == 0
     d00 = jnp.where(even, mine[0:NB, :], other[0:NB, :])
     d11 = jnp.where(even, other[0:NB, :], mine[0:NB, :])
     top = jnp.where(even, mine[NB:, :], other[NB:, :])
@@ -102,15 +106,20 @@
     d01 = jnp.concatenate([top, bottom], axis=0)
     m = dot(w0[...], d01, ((1,), (0,)))
     m10[...] = m
-    s[...] = d11 - dot(m, m, ((0,), (0,)))
+    s11[...] = d11 - dot(m, m, ((0,), (0,)))
+
+
+def second_body(s11, u1, w1, s, e):
+    i, j, eye = identity()
+    s[...] = s11[...]
     e[...] = eye
     eliminate(s, e, u1, w1)
     u1[...] = jnp.where(i <= j, u1[...], 0.0)
 
 
-def finish_body(place, x, rows_a, rows_b, cols_a, cols_b, u0, w0, m10, u1, w1, out):
-    p = place[0]
-    q = place[1]
+def finish_body(x, rows_a, rows_b, cols_a, cols_b, u0, w0, m10, u1, w1, out):
+    p = lax.axis_index("row")
+    q = lax.axis_index("col")
     even = (p & 1) == 0
     direct = (((q + 1) >> 1) & 1) == 0
     w0v = w0[...]
@@ -159,6 +168,17 @@
     return [jax.ShapeDtypeStruct((r, NB), F32) for r in rows]
 
 
+def call(body, shapes, scratch, *args):
+    return pl.pallas_call(
+        body,
+        out_shape=shapes,
+        in_specs=[VMEM] * len(args),
+        out_specs=[VMEM] * len(shapes),
+        scratch_shapes=[pltpu.VMEM((NB, NB), F32)] * scratch,
+        compiler_params=PARAMS,
+    )(*args)
+
+
 def per_device(covariance):
     p = lax.axis_index("row")
     q = lax.axis_index("col")
@@ -166,18 +186,22 @@
     x = q >> 2
     y = q & 3
     odd = (p & 1) == 1
-    place = jnp.stack([p, q]).astype(jnp.int32)
     local = covariance.reshape(2 * NB * 4, NB)
-    tile, rows, cols = pl.pallas_call(
-        pick_body,
-        out_shape=tile_of(NB, 2 * NB, 4 * NB),
-        in_specs=[SMEM, VMEM],
-        out_specs=[VMEM] * 3,
-    )(place, local)
+    tile, rows, cols = call(pick_body, tile_of(NB, 2 * NB, 4 * NB), 0, local)
 
     cores = (0, 1)
-    planes = range(16)
+    every = range(COLS)
     squares = range(4)
+    swap = [((r, a), (r ^ 1, a)) for r in range(ROWS) for a in every]
+
+    def climb(cols, stride):
+        pairs = []
+        for s in range(0, 16, 2 * stride):
+            for c in cores:
+                d = (s + stride if c == 0 else s - stride) % 16
+                pairs += [((2 * s + c, a), (2 * d + c, a)) for a in every]
+        got = move(cols, pairs)
+        return jnp.where((z & (2 * stride - 1)) == stride, got, cols)
 
     r1 = move(tile, [((c, a), (c, b)) for c in cores for a, b in ((0, 2), (1, 3))])
     r2 = move(tile, [((c, a), (c, b)) for c in cores for a, b in ((0, 3), (1, 2))])
@@ -191,14 +215,29 @@
         ],
         axis=0,
     )
+    got = move(rows, [((r, a), (r, b)) for r in range(ROWS) for a, b in ((0, 3), (1, 2))])
+    rows = jnp.where(y >= 2, got, rows)
+
     got = [
         move(diag, [((c, a), (c, 4 * b + a)) for c in cores for a in squares]) for b in (2, 1, 3)
     ]
+    cols = climb(after(cols, diag), 8)
+    rows = after(rows, diag)
+    rows_got = move(rows, [((r, a), (r, 8 + a)) for r in range(ROWS) for a in squares])
     diag = jnp.where(x == 0, diag, got[0] + got[1] + got[2])
+    rows = jnp.where(x == 2, rows_got, rows)
+
     got = [
-        move(diag, [((c, a), (2 * b + c, a)) for c in cores for a in range(COLS)]) for b in (8, 4, 12)
+        move(diag, [((c, a), (2 * b + c, a)) for c in cores for a in every]) for b in (8, 4, 12)
     ]
+    cols = climb(after(cols, diag), 4)
+    rows = after(rows, diag)
+    rows_got = move(
+        rows, [((r, 4 * b + a), (r, 4 * b + 4 + a)) for r in range(ROWS) for b in (0, 2) for a in squares]
+    )
     diag = jnp.where(z == 0, diag, got[0] + got[1] + got[2])
+    rows = jnp.where((x & 1) == 1, rows_got, rows)
+
     got = [
         move(
             diag,
@@ -206,51 +245,24 @@
                 ((2 * s + c, a), (2 * (s + b) + c, a))
                 for c in cores
                 for s in (0, 4, 8, 12)
-                for a in range(COLS)
+                for a in every
             ],
         )
         for b in (2, 1, 3)
     ]
+    cols = climb(after(cols, diag), 2)
     diag = jnp.where((z & 3) == 0, diag, got[0] + got[1] + got[2])
-    swap = [((r, a), (r ^ 1, a)) for r in range(ROWS) for a in range(COLS)]
+
     other = move(diag, swap)
-
-    got = move(rows, [((r, a), (r, b)) for r in range(ROWS) for a, b in ((0, 3), (1, 2))])
-    rows = jnp.where(y >= 2, got, rows)
-    got = move(rows, [((r, a), (r, 8 + a)) for r in range(ROWS) for a in squares])
-    rows = jnp.where(x == 2, got, rows)
-    got = move(
-        rows, [((r, 4 * b + a), (r, 4 * b + 4 + a)) for r in range(ROWS) for b in (0, 2) for a in squares]
-    )
-    rows = jnp.where((x & 1) == 1, got, rows)
-    rows_b = move(
-        rows, [((r, a), (r, a ^ 1)) for r in range(ROWS) for a in range(COLS)]
-    )
-
-    for stride in (8, 4, 2, 1):
-        pairs = []
-        for s in range(0, 16, 2 * stride):
-            for c in cores:
-                d = (s + stride if c == 0 else s - stride) % 16
-                pairs += [((2 * s + c, a), (2 * d + c, a)) for a in range(COLS)]
-        got = move(cols, pairs)
-        cols = jnp.where((z & (2 * stride - 1)) == stride, got, cols)
-    cols_b = move(cols, swap)
-
-    factors = pl.pallas_call(
-        factor_body,
-        out_shape=tile_of(*([NB] * 5)),
-        in_specs=[SMEM, VMEM, VMEM],
-        out_specs=[VMEM] * 5,
-        scratch_shapes=[pltpu.VMEM((NB, NB), F32)] * 2,
-        cost_estimate=pl.CostEstimate(flops=10_000_000, bytes_accessed=400_000, transcendentals=0),
-    )(place, diag, other)
-    out = pl.pallas_call(
-        finish_body,
-        out_shape=jax.ShapeDtypeStruct((2 * NB * 4, NB), F32),
-        in_specs=[SMEM] + [VMEM] * 10,
-        out_specs=VMEM,
-    )(place, local, rows, rows_b, cols, cols_b, *factors)
+    cols = climb(after(cols, diag), 1)
+    rows_b = move(after(rows, diag), [((r, a), (r, a ^ 1)) for r in range(ROWS) for a in every])
+
+    u0, w0, m10, s11 = call(first_body, tile_of(*[NB] * 4), 2, diag, other)
+    cols_b = move(after(cols, s11), swap)
+    u1, w1 = call(second_body, tile_of(*[NB] * 2), 2, s11)
+    (out,) = call(
+        finish_body, tile_of(8 * NB), 0, local, rows, rows_b, cols, cols_b, u0, w0, m10, u1, w1
+    )
     return out.reshape(covariance.shape)
 
 

time: 88.4 us -> 71.2 us (0.81)
  the two profiles are of different devices: /device:TPU:1 before, /device:TPU:65 now
where the time goes in v2:
time: 71.2 us; the launch traced here: 70.6 us
  starting transfers between devices  29.7 us (42%)
  waiting for transfers between devices  25.4 us (36%)
  Pallas kernels  13.6 us (19%)
  local copies, waits for them, and re-layouts  1.05 us (1%)
    ppermute x22, starting transfers between devices, move(): return lax.ppermute(value, ('row', 'col'), flat)  29.7 us
    ppermute x22, waiting for transfers between devices, move(): return lax.ppermute(value, ('row', 'col'), flat)  25.4 us
    pallas_call x4, Pallas kernels, call(): pl.pallas_call(body, out_shape=shapes, in_specs=[VMEM] * len(args), out_s...  13.6 us
  transfers between devices with their start and end apart: 22, of which 2 were waited for; matrix products, arithmetic and copies ran while one was open for 0% of the time, Pallas kernels for 14%

profile of v2, /device:TPU:65, one launch (start us, length us, event | category | flops | bytes accessed | tf_op | source)
XLA Modules:
  0.0 70.6 jit_solution(1191302131932483649)
XLA Ops:
  0.0 1.0 %copy-done = f32[2,128,4,128]{3,2,1,0:T(4,128)S(1)} copy-done((f32[2,128,4,128]{3,2,1,0:T(4,128)S(1)}, f32[2,128,4,128]{3,2,1,0:T(4,128)}, u32[]{:S(2)}) %copy-start) | copy-done | bytes 524312
  3.3 0.7 collective-permute-start.5
  4.0 0.7 collective-permute-start.6
  4.6 0.7 collective-permute-start.7
  5.3 0.7 collective-permute-start.16
  6.1 0.7 collective-permute-start.10
  6.7 0.7 collective-permute-start.11
  7.4 0.7 collective-permute-start.9
  8.1 0.7 collective-permute-start.17
  8.8 4.6 %collective-permute-start = (f32[256,128]{1,0:T(8,128)S(1)}, f32[256,128]{1,0:T(8,128)S(1)}, u32[]{:S(2)}, u32[]{:S(2)}) collective-permute-start(f32[256,128]{1,0:T(8,128)S(1)} %get-tuple-element.22), channel_id=1, source_target_pairs={{0,3},{1,2},{16,19},{17,18},{32,35},{33,34},{48,51},{49,50},{64,67... | collective-permute-start | bytes 393224 | tf_op jit(solution)/shard_map/ppermute | solution.py:24
  13.6 1.3 %collective-permute-start.12 = (f32[192,128]{1,0:T(8,128)S(1)}, f32[192,128]{1,0:T(8,128)S(1)}, u32[]{:S(2)}, u32[]{:S(2)}) collective-permute-start(f32[192,128]{1,0:T(8,128)S(1)} %add_select_fusion.1), channel_id=1, source_target_pairs={{0,64},{1,65},{2,66},{3,67},{4,68},{5,69},{6,70},{7,71},{8,72},{9,... | collective-permute-start | bytes 294920 | tf_op jit(solution)/shard_map/ppermute | solution.py:24
  14.9 0.7 collective-permute-start.13
  16.3 1.3 %collective-permute-start.18 = (f32[512,128]{1,0:T(8,128)S(1)}, f32[512,128]{1,0:T(8,128)S(1)}, u32[]{:S(2)}, u32[]{:S(2)}) collective-permute-start(f32[512,128]{1,0:T(8,128)S(1)} %broadcast_select_fusion.1), channel_id=1, source_target_pairs={{0,64},{1,65},{2,66},{3,67},{4,68},{5,69},{6,70},{7,71},{8,72},{9,... | collective-permute-start | bytes 786440 | tf_op jit(solution)/shard_map/ppermute | solution.py:24
  17.6 1.3 %collective-permute-start.4 = (f32[256,128]{1,0:T(8,128)S(1)}, f32[256,128]{1,0:T(8,128)S(1)}, u32[]{:S(2)}, u32[]{:S(2)}) collective-permute-start(f32[256,128]{1,0:T(8,128)S(1)} %broadcast_select_fusion.4), channel_id=1, source_target_pairs={{0,8},{1,9},{2,10},{3,11},{16,24},{17,25},{18,26},{19,27},{32,40},... | collective-permute-start | bytes 393224 | tf_op jit(solution)/shard_map/ppermute | solution.py:24
  18.9 15.8 %collective-permute-done.12 = f32[192,128]{1,0:T(8,128)S(1)} collective-permute-done((f32[192,128]{1,0:T(8,128)S(1)}, f32[192,128]{1,0:T(8,128)S(1)}, u32[]{:S(2)}, u32[]{:S(2)}) %collective-permute-start.12) | collective-permute-done | bytes 98336 | tf_op jit(solution)/shard_map/ppermute | solution.py:24
  34.8 9.6 %collective-permute-done.18 = f32[512,128]{1,0:T(8,128)S(1)} collective-permute-done((f32[512,128]{1,0:T(8,128)S(1)}, f32[512,128]{1,0:T(8,128)S(1)}, u32[]{:S(2)}, u32[]{:S(2)}) %collective-permute-start.18) | collective-permute-done | bytes 262176 | tf_op jit(solution)/shard_map/ppermute | solution.py:24
  44.4 1.3 %collective-permute-start.19 = (f32[512,128]{1,0:T(8,128)S(1)}, f32[512,128]{1,0:T(8,128)S(1)}, u32[]{:S(2)}, u32[]{:S(2)}) collective-permute-start(f32[512,128]{1,0:T(8,128)S(1)} %broadcast_select_fusion.2), channel_id=1, source_target_pairs={{0,32},{1,33},{2,34},{3,35},{4,36},{5,37},{6,38},{7,39},{8,40},{9,... | collective-permute-start | bytes 786440 | tf_op jit(solution)/shard_map/ppermute | solution.py:24
  45.7 1.9 %collective-permute-start.20 = (f32[192,128]{1,0:T(8,128)S(1)}, f32[192,128]{1,0:T(8,128)S(1)}, u32[]{:S(2)}, u32[]{:S(2)}) collective-permute-start(f32[192,128]{1,0:T(8,128)S(1)} %add_select_fusion.mine), channel_id=1, source_target_pairs={{0,16},{1,17},{2,18},{3,19},{4,20},{5,21},{6,22},{7,23},{8,24},{9,... | collective-permute-start | bytes 294920 | tf_op jit(solution)/shard_map/ppermute | solution.py:24
  47.6 3.2 %collective-permute-start.8 = (f32[256,128]{1,0:T(8,128)S(1)}, f32[256,128]{1,0:T(8,128)S(1)}, u32[]{:S(2)}, u32[]{:S(2)}) collective-permute-start(f32[256,128]{1,0:T(8,128)S(1)} %broadcast_select_fusion.5), channel_id=1, source_target_pairs={{0,4},{1,5},{2,6},{3,7},{8,12},{9,13},{10,14},{11,15},{16,20},{17,... | collective-permute-start | bytes 393224 | tf_op jit(solution)/shard_map/ppermute | solution.py:24
  50.9 5.3 %shard_map.18 = (f32[128,128]{1,0:T(8,128)S(1)}, f32[128,128]{1,0:T(8,128)S(1)}, f32[128,128]{1,0:T(8,128)S(1)}, f32[128,128]{1,0:T(8,128)S(1)}) custom-call(f32[192,128]{1,0:T(8,128)S(1)} %add_select_fusion.mine, f32[192,128]{1,0:T(8,128)S(1)} %collective-permute-done.20.other), custom_call_target="tpu_custom_call" | custom-call | tf_op jit(solution)/shard_map/pallas_call | solution.py:172
  56.2 2.8 %collective-permute-start.21 = (f32[512,128]{1,0:T(8,128)S(1)}, f32[512,128]{1,0:T(8,128)S(1)}, u32[]{:S(2)}, u32[]{:S(2)}) collective-permute-start(f32[512,128]{1,0:T(8,128)S(1)} %broadcast_select_fusion.3.cols_a), channel_id=1, source_target_pairs={{0,16},{1,17},{2,18},{3,19},{4,20},{5,21},{6,22},{7,23},{8,24},{9,... | collective-permute-start | bytes 786440 | tf_op jit(solution)/shard_map/ppermute | solution.py:24
  59.1 3.2 %collective-permute-start.15 = (f32[256,128]{1,0:T(8,128)S(1)}, f32[256,128]{1,0:T(8,128)S(1)}, u32[]{:S(2)}, u32[]{:S(2)}) collective-permute-start(f32[256,128]{1,0:T(8,128)S(1)} %broadcast_select_fusion.6.rows_a), channel_id=1, source_target_pairs={{0,1},{1,0},{2,3},{3,2},{4,5},{5,4},{6,7},{7,6},{8,9},{9,8},{10,11... | collective-permute-start | bytes 393224 | tf_op jit(solution)/shard_map/ppermute | solution.py:24
  62.3 4.5 %shard_map.19 = (f32[128,128]{1,0:T(8,128)S(1)}, f32[128,128]{1,0:T(8,128)S(1)}) custom-call(f32[128,128]{1,0:T(8,128)S(1)} %get-tuple-element.32.s11), custom_call_target="tpu_custom_call" | custom-call | tf_op jit(solution)/shard_map/pallas_call | solution.py:172
  66.8 3.8 %shard_map.20 = f32[1024,128]{1,0:T(8,128)} custom-call(f32[1024,128]{1,0:T(8,128)S(1)} %bitcast.3, f32[256,128]{1,0:T(8,128)S(1)} %broadcast_select_fusion.6.rows_a, f32[256,128]{1,0:T(8,128)S(1)} %collective-permute-done.15.rows_b, f32[512,128]{1,0:T(8,128)S(1)} %broadcast_select_fusion.3.cols_a, f32[512,128]{1,0:T(8,128)S(1)} %collective-permute-done.21.cols_b, ...), custom_call_target="tpu_custom_call" | custom-call | tf_op jit(solution)/shard_map/pallas_call | solution.py:172
  (41 shorter events, 3.1 us)
Async XLA Ops:
  0.0 1.0 %copy-start = (f32[2,128,4,128]{3,2,1,0:T(4,128)S(1)}, f32[2,128,4,128]{3,2,1,0:T(4,128)}, u32[]{:S(2)}) copy-start(f32[2,128,4,128]{3,2,1,0:T(4,128)} %param.1) | copy-start | bytes 1572868
  1.2 2.0 %collective-permute-start.1 = (f32[128,128]{1,0:T(8,128)S(1)}, f32[128,128]{1,0:T(8,128)S(1)}, u32[]{:S(2)}, u32[]{:S(2)}) collective-permute-start(f32[128,128]{1,0:T(8,128)S(1)} %get-tuple-element.23), channel_id=1, source_target_pairs={{0,1},{1,0},{16,17},{17,16}} | collective-permute-start | bytes 196616 | tf_op jit(solution)/shard_map/ppermute | solution.py:24
  1.8 1.4 %collective-permute-start.2 = (f32[128,128]{1,0:T(8,128)S(1)}, f32[128,128]{1,0:T(8,128)S(1)}, u32[]{:S(2)}, u32[]{:S(2)}) collective-permute-start(f32[128,128]{1,0:T(8,128)S(1)} %get-tuple-element.23), channel_id=1, source_target_pairs={{0,3},{1,2},{16,19},{17,18}} | collective-permute-start | bytes 196616 | tf_op jit(solution)/shard_map/ppermute | solution.py:24
  2.5 0.7 %collective-permute-start.3 = (f32[128,128]{1,0:T(8,128)S(1)}, f32[128,128]{1,0:T(8,128)S(1)}, u32[]{:S(2)}, u32[]{:S(2)}) collective-permute-start(f32[128,128]{1,0:T(8,128)S(1)} %get-tuple-element.23), channel_id=1, source_target_pairs={{0,2},{1,3},{16,18},{17,19}} | collective-permute-start | bytes 196616 | tf_op jit(solution)/shard_map/ppermute | solution.py:24
  3.3 2.7 %collective-permute-start.5 = (f32[192,128]{1,0:T(8,128)S(1)}, f32[192,128]{1,0:T(8,128)S(1)}, u32[]{:S(2)}, u32[]{:S(2)}) collective-permute-start(f32[192,128]{1,0:T(8,128)S(1)} %pad_maximum_fusion), channel_id=1, source_target_pairs={{0,8},{1,9},{2,10},{3,11},{16,24},{17,25},{18,26},{19,27}} | collective-permute-start | bytes 294920 | tf_op jit(solution)/shard_map/ppermute | solution.py:24
  4.0 2.1 %collective-permute-start.6 = (f32[192,128]{1,0:T(8,128)S(1)}, f32[192,128]{1,0:T(8,128)S(1)}, u32[]{:S(2)}, u32[]{:S(2)}) collective-permute-start(f32[192,128]{1,0:T(8,128)S(1)} %pad_maximum_fusion), channel_id=1, source_target_pairs={{0,4},{1,5},{2,6},{3,7},{16,20},{17,21},{18,22},{19,23}} | collective-permute-start | bytes 294920 | tf_op jit(solution)/shard_map/ppermute | solution.py:24
  4.6 1.4 %collective-permute-start.7 = (f32[192,128]{1,0:T(8,128)S(1)}, f32[192,128]{1,0:T(8,128)S(1)}, u32[]{:S(2)}, u32[]{:S(2)}) collective-permute-start(f32[192,128]{1,0:T(8,128)S(1)} %pad_maximum_fusion), channel_id=1, source_target_pairs={{0,12},{1,13},{2,14},{3,15},{16,28},{17,29},{18,30},{19,31}} | collective-permute-start | bytes 294920 | tf_op jit(solution)/shard_map/ppermute | solution.py:24
  5.3 2.8 %collective-permute-start.16 = (f32[512,128]{1,0:T(8,128)S(1)}, f32[512,128]{1,0:T(8,128)S(1)}, u32[]{:S(2)}, u32[]{:S(2)}) collective-permute-start(f32[512,128]{1,0:T(8,128)S(1)} %get-tuple-element.28), channel_id=1, source_target_pairs={{0,256},{1,257},{2,258},{3,259},{4,260},{5,261},{6,262},{7,263},{8... | collective-permute-start | bytes 786440 | tf_op jit(solution)/shard_map/ppermute | solution.py:24
  6.1 7.4 %collective-permute-start.10 = (f32[192,128]{1,0:T(8,128)S(1)}, f32[192,128]{1,0:T(8,128)S(1)}, u32[]{:S(2)}, u32[]{:S(2)}) collective-permute-start(f32[192,128]{1,0:T(8,128)S(1)} %add_select_fusion.2), channel_id=1, source_target_pairs={{0,128},{1,129},{2,130},{3,131},{4,132},{5,133},{6,134},{7,135},{8... | collective-permute-start | bytes 294920 | tf_op jit(solution)/shard_map/ppermute | solution.py:24
  6.7 6.8 %collective-permute-start.11 = (f32[192,128]{1,0:T(8,128)S(1)}, f32[192,128]{1,0:T(8,128)S(1)}, u32[]{:S(2)}, u32[]{:S(2)}) collective-permute-start(f32[192,128]{1,0:T(8,128)S(1)} %add_select_fusion.2), channel_id=1, source_target_pairs={{0,384},{1,385},{2,386},{3,387},{4,388},{5,389},{6,390},{7,391},{8... | collective-permute-start | bytes 294920 | tf_op jit(solution)/shard_map/ppermute | solution.py:24
  7.4 6.1 %collective-permute-start.9 = (f32[192,128]{1,0:T(8,128)S(1)}, f32[192,128]{1,0:T(8,128)S(1)}, u32[]{:S(2)}, u32[]{:S(2)}) collective-permute-start(f32[192,128]{1,0:T(8,128)S(1)} %add_select_fusion.2), channel_id=1, source_target_pairs={{0,256},{1,257},{2,258},{3,259},{4,260},{5,261},{6,262},{7,263},{8... | collective-permute-start | bytes 294920 | tf_op jit(solution)/shard_map/ppermute | solution.py:24
  8.1 8.1 %collective-permute-start.17 = (f32[512,128]{1,0:T(8,128)S(1)}, f32[512,128]{1,0:T(8,128)S(1)}, u32[]{:S(2)}, u32[]{:S(2)}) collective-permute-start(f32[512,128]{1,0:T(8,128)S(1)} %broadcast_select_fusion), channel_id=1, source_target_pairs={{0,128},{1,129},{2,130},{3,131},{4,132},{5,133},{6,134},{7,135},{8... | collective-permute-start | bytes 786440 | tf_op jit(solution)/shard_map/ppermute | solution.py:24
  8.8 8.7 %collective-permute-start = (f32[256,128]{1,0:T(8,128)S(1)}, f32[256,128]{1,0:T(8,128)S(1)}, u32[]{:S(2)}, u32[]{:S(2)}) collective-permute-start(f32[256,128]{1,0:T(8,128)S(1)} %get-tuple-element.22), channel_id=1, source_target_pairs={{0,3},{1,2},{16,19},{17,18},{32,35},{33,34},{48,51},{49,50},{64,67... | collective-permute-start | bytes 393224 | tf_op jit(solution)/shard_map/ppermute | solution.py:24
  13.6 21.2 %collective-permute-start.12 = (f32[192,128]{1,0:T(8,128)S(1)}, f32[192,128]{1,0:T(8,128)S(1)}, u32[]{:S(2)}, u32[]{:S(2)}) collective-permute-start(f32[192,128]{1,0:T(8,128)S(1)} %add_select_fusion.1), channel_id=1, source_target_pairs={{0,64},{1,65},{2,66},{3,67},{4,68},{5,69},{6,70},{7,71},{8,72},{9,... | collective-permute-start | bytes 294920 | tf_op jit(solution)/shard_map/ppermute | solution.py:24
  14.9 19.9 %collective-permute-start.13 = (f32[192,128]{1,0:T(8,128)S(1)}, f32[192,128]{1,0:T(8,128)S(1)}, u32[]{:S(2)}, u32[]{:S(2)}) collective-permute-start(f32[192,128]{1,0:T(8,128)S(1)} %add_select_fusion.1), channel_id=1, source_target_pairs={{0,32},{1,33},{2,34},{3,35},{4,36},{5,37},{6,38},{7,39},{8,40},{9,... | collective-permute-start | bytes 294920 | tf_op jit(solution)/shard_map/ppermute | solution.py:24
  15.5 19.2 %collective-permute-start.14 = (f32[192,128]{1,0:T(8,128)S(1)}, f32[192,128]{1,0:T(8,128)S(1)}, u32[]{:S(2)}, u32[]{:S(2)}) collective-permute-start(f32[192,128]{1,0:T(8,128)S(1)} %add_select_fusion.1), channel_id=1, source_target_pairs={{0,96},{1,97},{2,98},{3,99},{4,100},{5,101},{6,102},{7,103},{8,104... | collective-permute-start | bytes 294920 | tf_op jit(solution)/shard_map/ppermute | solution.py:24
  16.3 28.1 %collective-permute-start.18 = (f32[512,128]{1,0:T(8,128)S(1)}, f32[512,128]{1,0:T(8,128)S(1)}, u32[]{:S(2)}, u32[]{:S(2)}) collective-permute-start(f32[512,128]{1,0:T(8,128)S(1)} %broadcast_select_fusion.1), channel_id=1, source_target_pairs={{0,64},{1,65},{2,66},{3,67},{4,68},{5,69},{6,70},{7,71},{8,72},{9,... | collective-permute-start | bytes 786440 | tf_op jit(solution)/shard_map/ppermute | solution.py:24
  17.6 30.0 %collective-permute-start.4 = (f32[256,128]{1,0:T(8,128)S(1)}, f32[256,128]{1,0:T(8,128)S(1)}, u32[]{:S(2)}, u32[]{:S(2)}) collective-permute-start(f32[256,128]{1,0:T(8,128)S(1)} %broadcast_select_fusion.4), channel_id=1, source_target_pairs={{0,8},{1,9},{2,10},{3,11},{16,24},{17,25},{18,26},{19,27},{32,40},... | collective-permute-start | bytes 393224 | tf_op jit(solution)/shard_map/ppermute | solution.py:24
  44.4 11.8 %collective-permute-start.19 = (f32[512,128]{1,0:T(8,128)S(1)}, f32[512,128]{1,0:T(8,128)S(1)}, u32[]{:S(2)}, u32[]{:S(2)}) collective-permute-start(f32[512,128]{1,0:T(8,128)S(1)} %broadcast_select_fusion.2), channel_id=1, source_target_pairs={{0,32},{1,33},{2,34},{3,35},{4,36},{5,37},{6,38},{7,39},{8,40},{9,... | collective-permute-start | bytes 786440 | tf_op jit(solution)/shard_map/ppermute | solution.py:24
  45.7 5.2 %collective-permute-start.20 = (f32[192,128]{1,0:T(8,128)S(1)}, f32[192,128]{1,0:T(8,128)S(1)}, u32[]{:S(2)}, u32[]{:S(2)}) collective-permute-start(f32[192,128]{1,0:T(8,128)S(1)} %add_select_fusion.mine), channel_id=1, source_target_pairs={{0,16},{1,17},{2,18},{3,19},{4,20},{5,21},{6,22},{7,23},{8,24},{9,... | collective-permute-start | bytes 294920 | tf_op jit(solution)/shard_map/ppermute | solution.py:24
  47.6 11.4 %collective-permute-start.8 = (f32[256,128]{1,0:T(8,128)S(1)}, f32[256,128]{1,0:T(8,128)S(1)}, u32[]{:S(2)}, u32[]{:S(2)}) collective-permute-start(f32[256,128]{1,0:T(8,128)S(1)} %broadcast_select_fusion.5), channel_id=1, source_target_pairs={{0,4},{1,5},{2,6},{3,7},{8,12},{9,13},{10,14},{11,15},{16,20},{17,... | collective-permute-start | bytes 393224 | tf_op jit(solution)/shard_map/ppermute | solution.py:24
  56.1 10.6 %copy-start.1 = (f32[2,128,4,128]{3,2,1,0:T(4,128)S(1)}, f32[2,128,4,128]{3,2,1,0:T(4,128)}, u32[]{:S(2)}) copy-start(f32[2,128,4,128]{3,2,1,0:T(4,128)} %param.1) | copy-start | bytes 1572868
  56.2 10.6 %collective-permute-start.21 = (f32[512,128]{1,0:T(8,128)S(1)}, f32[512,128]{1,0:T(8,128)S(1)}, u32[]{:S(2)}, u32[]{:S(2)}) collective-permute-start(f32[512,128]{1,0:T(8,128)S(1)} %broadcast_select_fusion.3.cols_a), channel_id=1, source_target_pairs={{0,16},{1,17},{2,18},{3,19},{4,20},{5,21},{6,22},{7,23},{8,24},{9,... | collective-permute-start | bytes 786440 | tf_op jit(solution)/shard_map/ppermute | solution.py:24
  59.1 7.7 %collective-permute-start.15 = (f32[256,128]{1,0:T(8,128)S(1)}, f32[256,128]{1,0:T(8,128)S(1)}, u32[]{:S(2)}, u32[]{:S(2)}) collective-permute-start(f32[256,128]{1,0:T(8,128)S(1)} %broadcast_select_fusion.6.rows_a), channel_id=1, source_target_pairs={{0,1},{1,0},{2,3},{3,2},{4,5},{5,4},{6,7},{7,6},{8,9},{9,8},{10,11... | collective-permute-start | bytes 393224 | tf_op jit(solution)/shard_map/ppermute | solution.py:24

commit v3 on v2

v3 whole, which is shorter than its diff:
```python
import jax
import jax.numpy as jnp
from jax import lax
from jax.experimental import pallas as pl
from jax.experimental.pallas import tpu as pltpu
from jax.sharding import PartitionSpec as P

NB = 128
ROWS = 32
COLS = 16
F32 = jnp.float32
VMEM = pl.BlockSpec(memory_space=pltpu.VMEM)
COST = 10**9
PARAMS = pltpu.CompilerParams(vmem_limit_bytes=8 * 2**20)


def dot(a, b, dims):
    return lax.dot_general(
        a, b, (dims, ((), ())), precision=lax.Precision.HIGHEST, preferred_element_type=F32
    )


def move(value, pairs):
    flat = [(sp * COLS + sq, dp * COLS + dq) for (sp, sq), (dp, dq) in pairs]
    return lax.ppermute(value, ("row", "col"), flat)


def after(value, earlier):
    return lax.optimization_barrier((value, earlier))[0]


def invert_factor(x_ref, w_ref):
    sub = lax.broadcasted_iota(jnp.int32, (8, NB), 0)
    lane = lax.broadcasted_iota(jnp.int32, (8, NB), 1)

    def spread(x, j):
        return jnp.broadcast_to(x[j : j + 1, :], (8, NB))

    def splat(x, j):
        return jnp.broadcast_to(x[:, j : j + 1], (8, NB))

    for k in range(NB // 8):
        here = x_ref[8 * k : 8 * k + 8, :]
        v = [splat(here, 8 * k + j) for j in range(8)]
        mine = (lane >= 8 * k) & (lane < 8 * k + 8)
        rest = jnp.where(mine, jnp.where(lane == sub + 8 * k, 1.0, 0.0), here)
        for t in range(0, 8, 2):
            a = spread(v[t], t)
            b = spread(v[t], t + 1)
            c = spread(v[t + 1], t + 1)
            det = a * c - b * b
            scale = 1.0 / det
            i00 = c * scale
            i01 = b * scale
            i11 = a * scale
            f0 = jnp.where(
                sub == t, 1.0 - i00, jnp.where(sub == t + 1, i01, v[t] * i00 - v[t + 1] * i01)
            )
            f1 = jnp.where(
                sub == t, i01, jnp.where(sub == t + 1, 1.0 - i11, v[t + 1] * i11 - v[t] * i01)
            )
            for j in range(t + 2, 8):
                v[j] = v[j] - f0 * spread(v[j], t) - f1 * spread(v[j], t + 1)
            r0 = spread(rest, t)
            r1 = spread(rest, t + 1)
            over = 1.0 / a
            at = 8 * k + t
            w_ref[at : at + 1, :] = (r0 * lax.rsqrt(a))[:1]
            w_ref[at + 1 : at + 2, :] = ((r1 - (b * over) * r0) * lax.rsqrt(det * over))[:1]
            rest = rest - f0 * r0 - f1 * r1
        z = [spread(rest, j) for j in range(8)]
        for h in range(k + 1, NB // 8):
            there = slice(8 * h, 8 * h + 8)
            x = x_ref[there, :]
            terms = [splat(x, 8 * k + j) * z[j] for j in range(8)]
            while len(terms) > 1:
                terms = [terms[i] + terms[i + 1] for i in range(0, len(terms), 2)]
            x_ref[there, :] = jnp.where(mine, 0.0, x) - terms[0]


def indices():
    i = lax.broadcasted_iota(jnp.int32, (NB, NB), 0)
    return i, lax.broadcasted_iota(jnp.int32, (NB, NB), 1)


def pick_body(x, tile, rows, cols):
    first = x[pl.ds(0, NB, stride=4), :]
    odd = (lax.axis_index("row") & 1) == 1
    tile[...] = jnp.where(odd, first.T, first)
    rows[0:NB, :] = first
    rows[NB:, :] = x[pl.ds(4 * NB, NB, stride=4), :]
    for m in range(4):
        cols[NB * m : NB * (m + 1), :] = x[pl.ds(m, NB, stride=4), :]


def token_body(*refs):
    out = refs[-1]
    total = refs[0][...]
    for ref in refs[1:-1]:
        total = total + ref[...]
    out[...] = total


def first_body(mine, other, w0, m10, s11, x):
    even = (lax.axis_index("row") & 1) == 0
    i, j = indices()
    x[...] = jnp.where(even, mine[0:NB, :], other[0:NB, :])
    invert_factor(x, w0)
    w = jnp.where(i >= j, w0[...], 0.0)
    w0[...] = w
    top = jnp.where(even, mine[NB:, :], other[NB:, :])
    bottom = jnp.where(even, other[NB:, :], mine[NB:, :])
    m = dot(w, jnp.concatenate([top, bottom], axis=0), ((1,), (0,)))
    m10[...] = m
    s11[...] = jnp.where(even, other[0:NB, :], mine[0:NB, :]) - dot(m, m, ((0,), (0,)))


def second_body(s11, mark, w1, x):
    i, j = indices()
    x[...] = s11[...]
    invert_factor(x, w1)
    w1[...] = jnp.where(i >= j, w1[...], 0.0)


def finish_body(x, rows_a, rows_b, cols_a, cols_b, w0, m10, w1, out):
    p = lax.axis_index("row")
    q = lax.axis_index("col")
    even = (p & 1) == 0
    direct = (((q + 1) >> 1) & 1) == 0
    i, j = indices()
    low = i >= j
    w0v = w0[...]
    w1v = w1[...]
    m = m10[...]
    r0 = jnp.where(direct, rows_a[...], rows_b[...])
    r1 = jnp.where(direct, rows_b[...], rows_a[...])
    y0 = dot(r0, w0v, ((1,), (1,)))
    y1 = dot(r1 - dot(y0, m, ((1,), (0,))), w1v, ((1,), (1,)))
    y = jnp.concatenate([y0, y1], axis=1)
    for t in range(4):
        at = slice(NB * t, NB * (t + 1))
        ca = cols_a[at, :]
        cb = cols_b[at, :]
        x0 = dot(w0v, jnp.where(even, ca, cb), ((1,), (0,)))
        x1 = dot(w1v, jnp.where(even, cb, ca) - dot(m, x0, ((0,), (0,))), ((1,), (0,)))
        change = dot(y, jnp.concatenate([x0, x1], axis=0), ((1,), (0,)))
        for l in range(2):
            here = pl.ds(4 * NB * l + t, NB, stride=4)
            rs = slice(NB * l, NB * (l + 1))
            new = x[here, :] - change[rs]
            if t == 0:
                panel = jnp.where(q == 0, y0[rs], y1[rs])
                if l == 0:
                    panel = jnp.where((p != q) | low, panel, 0.0)
                    panel = jnp.where((p == 0) & (q == 1), 0.0, panel)
                new = jnp.where(q < 2, panel, new)
                if l == 0:
                    new = jnp.where((p < 2) & (q >= 2), 0.0, new)
            elif l == 0:
                new = jnp.where(p < 2, 0.0, new)
            out[here, :] = new


def tile_of(*rows):
    return [jax.ShapeDtypeStruct((r, NB), F32) for r in rows]


LONG = pl.CostEstimate(flops=COST, bytes_accessed=COST, transcendentals=0)


def call(body, shapes, scratch, *args, cost=None):
    return pl.pallas_call(
        body,
        out_shape=shapes,
        in_specs=[VMEM] * len(args),
        out_specs=[VMEM] * len(shapes),
        scratch_shapes=[pltpu.VMEM((NB, NB), F32)] * scratch,
        compiler_params=PARAMS,
        cost_estimate=cost,
    )(*args)


def token(*xs):
    block = pl.BlockSpec((8, NB), lambda i: (0, 0))
    return pl.pallas_call(
        token_body,
        grid=(1,),
        out_shape=jax.ShapeDtypeStruct((8, NB), F32),
        in_specs=[block] * len(xs),
        out_specs=block,
        compiler_params=PARAMS,
        cost_estimate=LONG,
    )(*xs)


def per_device(covariance):
    p = lax.axis_index("row")
    q = lax.axis_index("col")
    z = p >> 1
    x = q >> 2
    y = q & 3
    odd = (p & 1) == 1
    local = covariance.reshape(2 * NB * 4, NB)
    tile, rows, cols = call(pick_body, tile_of(NB, 2 * NB, 4 * NB), 0, local)

    cores = (0, 1)
    every = range(COLS)
    squares = range(4)
    tied = lax.optimization_barrier

    def in_row(value, pairs):
        return move(value, [((r, a), (r, b)) for r in range(ROWS) for a, b in pairs])

    def along_x(s, d):
        return [(4 * s + a, 4 * d + a) for a in squares]

    def along_z(value, sends, on=cores):
        return move(
            value, [((2 * s + c, a), (2 * d + c, a)) for s, d in sends for c in on for a in every]
        )

    def among(h, members):
        hit = h == members[0]
        for m in members[1:]:
            hit = hit | (h == m)
        return hit

    def take(old, h, got, sends):
        for value, each in zip(got, sends):
            old = jnp.where(among(h, [d for _, d in each]), value, old)
        return old

    swap = [((r, a), (r ^ 1, a)) for r in range(ROWS) for a in every]

    def lift(value, sends):
        return [along_z(value, each) for each in sends]

    r3 = move(tile, [((c, a), (c, b)) for c in cores for a, b in ((0, 1), (1, 0))])
    r1 = move(tile, [((c, a), (c, b)) for c in cores for a, b in ((0, 2), (1, 3))])
    r2 = move(tile, [((c, a), (c, b)) for c in cores for a, b in ((0, 3), (1, 2))])
    for sends in ([(0, 1)], [(1, 5)]):
        cols = take(cols, z, lift(cols, [sends]), [sends])
    c_sends = [[(1, 13), (5, 9)]]
    c_got = lift(cols, c_sends)
    first = jnp.where(y == 0, tile, jnp.where(y == 1, r3, jnp.where(y == 2, r1, r2)))
    second = jnp.where(y == 0, r3, jnp.where(y == 1, tile, jnp.where(y == 2, r2, r1)))
    diag = jnp.concatenate(
        [
            jnp.where(odd, second, first),
            jnp.where(odd, first[NB // 2 :], second[: NB // 2]),
        ],
        axis=0,
    )

    got = [move(diag, [((c, a), (c, b)) for c in cores for a, b in along_x(0, d)]) for d in (2, 1, 3)]
    cols = take(cols, z, c_got, c_sends)
    cols = tied((cols, diag))[0]
    q_sends = [[(1, 2), (5, 4), (13, 12), (9, 8)]]
    q_got = lift(cols, q_sends)
    r_got = in_row(tied((rows, diag))[0], [(0, 3), (1, 2)])
    rows = jnp.where((y >= 2) & (x == 0), r_got, rows)
    far = in_row(tied((rows, diag))[0], along_x(0, 2))
    diag = take(diag, x, got, [[(0, 2)], [(0, 1)], [(0, 3)]])
    diag, mark = tied((diag, token(diag, diag, r_got)))

    d_sends = [[(0, 4)], [(0, 12)], [(0, 2)]]
    got = lift(diag, d_sends)
    rows = jnp.where(x == 2, far, rows)
    r_got = in_row(tied((rows, mark))[0], along_x(0, 1) + along_x(2, 3))
    diag = take(diag, z, got, d_sends)
    diag, mark = tied((diag, token(diag, mark)))

    d_sends = [
        [(0, 13), (2, 5), (4, 8), (12, 9)],
        [(0, 14), (2, 3), (4, 7), (12, 10)],
        [(0, 15), (2, 1), (4, 6), (12, 11)],
    ]
    got = lift(diag, d_sends)
    late_sends = [[(1, 3), (5, 6), (9, 10), (13, 14)], [(5, 7), (9, 11), (13, 15)]]
    late_got = [along_z(tied((cols, mark))[0], each) for each in late_sends]
    diag = take(diag, z, got, d_sends)
    diag, mark = tied((diag, token(diag, mark, *late_got)))

    other = move(diag, swap)
    rows = jnp.where((x & 1) == 1, r_got, rows)
    rows_b = in_row(tied((rows, mark))[0], [(a, a ^ 1) for a in every])
    w0, m10, s11 = call(first_body, tile_of(NB, NB, NB), 1, diag, other)
    cols = take(cols, z, q_got + late_got, q_sends + late_sends)
    cols_b = move(tied((cols, s11))[0], swap)
    (w1,) = call(second_body, tile_of(NB), 1, s11, w0[:8], cost=LONG)
    (out,) = call(
        finish_body, tile_of(8 * NB), 0, local, rows, rows_b, cols, cols_b, w0, m10, w1
    )
    return out.reshape(covariance.shape)


def solution(mesh):
    spec = P(None, "row", None, "col")
    return jax.shard_map(
        per_device, mesh=mesh, in_specs=(spec,), out_specs=spec, check_vma=False
    )
```

time: 71.2 us -> 65.4 us (0.919)
  the two profiles are of different devices: /device:TPU:65 before, /device:TPU:33 now
where the time goes in v3:
time: 65.4 us; the launch traced here: 64.8 us
  starting transfers between devices  41.7 us (64%)
  Pallas kernels  12.9 us (20%)
  waiting for transfers between devices  8.26 us (13%)
  local copies, waits for them, and re-layouts  1.05 us (2%)
    ppermute x24, starting transfers between devices, move(): return lax.ppermute(value, ('row', 'col'), flat)  41.7 us
    pallas_call x4, Pallas kernels, call(): pl.pallas_call(body, out_shape=shapes, in_specs=[VMEM] * len(args), out_s...  12.9 us
    ppermute x24, waiting for transfers between devices, move(): return lax.ppermute(value, ('row', 'col'), flat)  8.26 us
  transfers between devices with their start and end apart: 24, of which 3 were waited for; matrix products, arithmetic and copies ran while one was open for 0% of the time, Pallas kernels for 14%

profile of v3, /device:TPU:33, one launch (start us, length us, event | category | flops | bytes accessed | tf_op | source)
XLA Modules:
  0.0 64.8 jit_solution(14808864237057768028)
XLA Ops:
  0.0 1.0 %copy-done = f32[2,128,4,128]{3,2,1,0:T(4,128)S(1)} copy-done((f32[2,128,4,128]{3,2,1,0:T(4,128)S(1)}, f32[2,128,4,128]{3,2,1,0:T(4,128)}, u32[]{:S(2)}) %copy-start) | copy-done | bytes 524312
  3.2 1.3 %collective-permute-start.7 = (f32[512,128]{1,0:T(8,128)S(1)}, f32[512,128]{1,0:T(8,128)S(1)}, u32[]{:S(2)}, u32[]{:S(2)}) collective-permute-start(f32[512,128]{1,0:T(8,128)S(1)} %get-tuple-element.19), channel_id=1, source_target_pairs={{0,32},{1,33},{2,34},{3,35},{4,36},{5,37},{6,38},{7,39},{8,40},{9,... | collective-permute-start | bytes 786440 | tf_op jit(solution)/shard_map/ppermute | solution.py:25
  4.6 0.7 %collective-permute-start.13 = (f32[192,128]{1,0:T(8,128)S(1)}, f32[192,128]{1,0:T(8,128)S(1)}, u32[]{:S(2)}, u32[]{:S(2)}) collective-permute-start(f32[192,128]{1,0:T(8,128)S(1)} %pad_maximum_fusion), channel_id=1, source_target_pairs={{0,12},{1,13},{2,14},{3,15},{16,28},{17,29},{18,30},{19,31}} | collective-permute-start | bytes 294920 | tf_op jit(solution)/shard_map/ppermute | solution.py:25
  5.3 0.7 %collective-permute-start.14 = (f32[192,128]{1,0:T(8,128)S(1)}, f32[192,128]{1,0:T(8,128)S(1)}, u32[]{:S(2)}, u32[]{:S(2)}) collective-permute-start(f32[192,128]{1,0:T(8,128)S(1)} %pad_maximum_fusion), channel_id=1, source_target_pairs={{0,4},{1,5},{2,6},{3,7},{16,20},{17,21},{18,22},{19,23}} | collective-permute-start | bytes 294920 | tf_op jit(solution)/shard_map/ppermute | solution.py:25
  5.9 0.7 %collective-permute-start.15 = (f32[192,128]{1,0:T(8,128)S(1)}, f32[192,128]{1,0:T(8,128)S(1)}, u32[]{:S(2)}, u32[]{:S(2)}) collective-permute-start(f32[192,128]{1,0:T(8,128)S(1)} %pad_maximum_fusion), channel_id=1, source_target_pairs={{0,8},{1,9},{2,10},{3,11},{16,24},{17,25},{18,26},{19,27}} | collective-permute-start | bytes 294920 | tf_op jit(solution)/shard_map/ppermute | solution.py:25
  6.6 6.2 %collective-permute-done.7 = f32[512,128]{1,0:T(8,128)S(1)} collective-permute-done((f32[512,128]{1,0:T(8,128)S(1)}, f32[512,128]{1,0:T(8,128)S(1)}, u32[]{:S(2)}, u32[]{:S(2)}) %collective-permute-start.7) | collective-permute-done | bytes 262176 | tf_op jit(solution)/shard_map/ppermute | solution.py:25
  12.9 2.0 %collective-permute-start.8 = (f32[512,128]{1,0:T(8,128)S(1)}, f32[512,128]{1,0:T(8,128)S(1)}, u32[]{:S(2)}, u32[]{:S(2)}) collective-permute-start(f32[512,128]{1,0:T(8,128)S(1)} %broadcast_select_fusion), channel_id=1, source_target_pairs={{32,160},{33,161},{34,162},{35,163},{36,164},{37,165},{38,166},{39... | collective-permute-start | bytes 786440 | tf_op jit(solution)/shard_map/ppermute | solution.py:25
  15.0 4.6 %collective-permute-start.3 = (f32[256,128]{1,0:T(8,128)S(1)}, f32[256,128]{1,0:T(8,128)S(1)}, u32[]{:S(2)}, u32[]{:S(2)}) collective-permute-start(f32[256,128]{1,0:T(8,128)S(1)} %get-tuple-element.17), channel_id=1, source_target_pairs={{0,3},{1,2},{16,19},{17,18},{32,35},{33,34},{48,51},{49,50},{64,67... | collective-permute-start | bytes 393224 | tf_op jit(solution)/shard_map/ppermute | solution.py:25
  19.7 0.7 %collective-permute-start.16 = (f32[192,128]{1,0:T(8,128)S(1)}, f32[192,128]{1,0:T(8,128)S(1)}, u32[]{:S(2)}, u32[]{:S(2)}) collective-permute-start(f32[192,128]{1,0:T(8,128)S(1)} %select_select_fusion.3), channel_id=1, source_target_pairs={{0,64},{1,65},{2,66},{3,67},{4,68},{5,69},{6,70},{7,71},{8,72},{9,... | collective-permute-start | bytes 294920 | tf_op jit(solution)/shard_map/ppermute | solution.py:25
  21.8 3.4 %collective-permute-start.9 = (f32[512,128]{1,0:T(8,128)S(1)}, f32[512,128]{1,0:T(8,128)S(1)}, u32[]{:S(2)}, u32[]{:S(2)}) collective-permute-start(f32[512,128]{1,0:T(8,128)S(1)} %broadcast_select_fusion.1), channel_id=1, source_target_pairs={{32,416},{33,417},{34,418},{35,419},{36,420},{37,421},{38,422},{39... | collective-permute-start | bytes 786440 | tf_op jit(solution)/shard_map/ppermute | solution.py:25
  25.2 1.7 %collective-permute-start.4 = (f32[256,128]{1,0:T(8,128)S(1)}, f32[256,128]{1,0:T(8,128)S(1)}, u32[]{:S(2)}, u32[]{:S(2)}) collective-permute-start(f32[256,128]{1,0:T(8,128)S(1)} %broadcast_select_fusion.3), channel_id=1, source_target_pairs={{0,8},{1,9},{2,10},{3,11},{16,24},{17,25},{18,26},{19,27},{32,40},... | collective-permute-start | bytes 393224 | tf_op jit(solution)/shard_map/ppermute | solution.py:25
  27.0 1.3 %collective-permute-start.19 = (f32[192,128]{1,0:T(8,128)S(1)}, f32[192,128]{1,0:T(8,128)S(1)}, u32[]{:S(2)}, u32[]{:S(2)}) collective-permute-start(f32[192,128]{1,0:T(8,128)S(1)} %select_select_fusion.2), channel_id=1, source_target_pairs={{0,480},{1,481},{2,482},{3,483},{4,484},{5,485},{6,486},{7,487},{8... | collective-permute-start | bytes 294920 | tf_op jit(solution)/shard_map/ppermute | solution.py:25
  29.0 0.7 %collective-permute-start.21 = (f32[192,128]{1,0:T(8,128)S(1)}, f32[192,128]{1,0:T(8,128)S(1)}, u32[]{:S(2)}, u32[]{:S(2)}) collective-permute-start(f32[192,128]{1,0:T(8,128)S(1)} %select_select_fusion.2), channel_id=1, source_target_pairs={{0,416},{1,417},{2,418},{3,419},{4,420},{5,421},{6,422},{7,423},{8... | collective-permute-start | bytes 294920 | tf_op jit(solution)/shard_map/ppermute | solution.py:25
  29.9 0.7 %collective-permute-start.10 = (f32[512,128]{1,0:T(8,128)S(1)}, f32[512,128]{1,0:T(8,128)S(1)}, u32[]{:S(2)}, u32[]{:S(2)}) collective-permute-start(f32[512,128]{1,0:T(8,128)S(1)} %broadcast_select_fusion.2), channel_id=1, source_target_pairs={{160,224},{161,225},{162,226},{163,227},{164,228},{165,229},{166,2... | collective-permute-start | bytes 786440 | tf_op jit(solution)/shard_map/ppermute | solution.py:25
  30.6 1.8 %collective-permute-done.19 = f32[192,128]{1,0:T(8,128)S(1)} collective-permute-done((f32[192,128]{1,0:T(8,128)S(1)}, f32[192,128]{1,0:T(8,128)S(1)}, u32[]{:S(2)}, u32[]{:S(2)}) %collective-permute-start.19) | collective-permute-done | bytes 98336 | tf_op jit(solution)/shard_map/ppermute | solution.py:25
  32.3 1.3 %collective-permute-start.11 = (f32[512,128]{1,0:T(8,128)S(1)}, f32[512,128]{1,0:T(8,128)S(1)}, u32[]{:S(2)}, u32[]{:S(2)}) collective-permute-start(f32[512,128]{1,0:T(8,128)S(1)} %broadcast_select_fusion.2), channel_id=1, source_target_pairs={{32,96},{33,97},{34,98},{35,99},{36,100},{37,101},{38,102},{39,103... | collective-permute-start | bytes 786440 | tf_op jit(solution)/shard_map/ppermute | solution.py:25
  33.7 6.3 %collective-permute-start.12 = (f32[512,128]{1,0:T(8,128)S(1)}, f32[512,128]{1,0:T(8,128)S(1)}, u32[]{:S(2)}, u32[]{:S(2)}) collective-permute-start(f32[512,128]{1,0:T(8,128)S(1)} %broadcast_select_fusion.2), channel_id=1, source_target_pairs={{32,64},{33,65},{34,66},{35,67},{36,68},{37,69},{38,70},{39,71},{4... | collective-permute-start | bytes 786440 | tf_op jit(solution)/shard_map/ppermute | solution.py:25
  40.1 4.3 %collective-permute-start.22 = (f32[192,128]{1,0:T(8,128)S(1)}, f32[192,128]{1,0:T(8,128)S(1)}, u32[]{:S(2)}, u32[]{:S(2)}) collective-permute-start(f32[192,128]{1,0:T(8,128)S(1)} %select_select_fusion.1.mine), channel_id=1, source_target_pairs={{0,16},{1,17},{2,18},{3,19},{4,20},{5,21},{6,22},{7,23},{8,24},{9,... | collective-permute-start | bytes 294920 | tf_op jit(solution)/shard_map/ppermute | solution.py:25
  44.4 1.3 %collective-permute-start.5 = (f32[256,128]{1,0:T(8,128)S(1)}, f32[256,128]{1,0:T(8,128)S(1)}, u32[]{:S(2)}, u32[]{:S(2)}) collective-permute-start(f32[256,128]{1,0:T(8,128)S(1)} %broadcast_select_fusion.4), channel_id=1, source_target_pairs={{0,4},{1,5},{2,6},{3,7},{8,12},{9,13},{10,14},{11,15},{16,20},{17,... | collective-permute-start | bytes 393224 | tf_op jit(solution)/shard_map/ppermute | solution.py:25
  45.7 5.0 %shard_map.18 = (f32[128,128]{1,0:T(8,128)S(1)}, f32[128,128]{1,0:T(8,128)S(1)}, f32[128,128]{1,0:T(8,128)S(1)}) custom-call(f32[192,128]{1,0:T(8,128)S(1)} %select_select_fusion.1.mine, f32[192,128]{1,0:T(8,128)S(1)} %collective-permute-done.22.other), custom_call_target="tpu_custom_call" | custom-call | tf_op jit(solution)/shard_map/pallas_call | solution.py:172
  50.8 1.9 %collective-permute-start.23 = (f32[512,128]{1,0:T(8,128)S(1)}, f32[512,128]{1,0:T(8,128)S(1)}, u32[]{:S(2)}, u32[]{:S(2)}) collective-permute-start(f32[512,128]{1,0:T(8,128)S(1)} %select_select_fusion.cols_a), channel_id=1, source_target_pairs={{0,16},{1,17},{2,18},{3,19},{4,20},{5,21},{6,22},{7,23},{8,24},{9,... | collective-permute-start | bytes 786440 | tf_op jit(solution)/shard_map/ppermute | solution.py:25
  52.8 4.2 %collective-permute-start.6 = (f32[256,128]{1,0:T(8,128)S(1)}, f32[256,128]{1,0:T(8,128)S(1)}, u32[]{:S(2)}, u32[]{:S(2)}) collective-permute-start(f32[256,128]{1,0:T(8,128)S(1)} %broadcast_select_fusion.5.rows_a), channel_id=1, source_target_pairs={{0,1},{1,0},{2,3},{3,2},{4,5},{5,4},{6,7},{7,6},{8,9},{9,8},{10,11... | collective-permute-start | bytes 393224 | tf_op jit(solution)/shard_map/ppermute | solution.py:25
  57.0 4.0 %shard_map.19.w1 = f32[128,128]{1,0:T(8,128)S(1)} custom-call(f32[128,128]{1,0:T(8,128)S(1)} %get-tuple-element.21.s11, f32[8,128]{1,0:T(8,128)S(1)} %slice.11.mark), custom_call_target="tpu_custom_call" | custom-call | flops 1000000000 | bytes 1000000000 | tf_op jit(solution)/shard_map/pallas_call | solution.py:172
  61.0 3.8 %shard_map.20 = f32[1024,128]{1,0:T(8,128)} custom-call(f32[1024,128]{1,0:T(8,128)S(1)} %bitcast.3, f32[256,128]{1,0:T(8,128)S(1)} %broadcast_select_fusion.5.rows_a, f32[256,128]{1,0:T(8,128)S(1)} %collective-permute-done.6.rows_b, f32[512,128]{1,0:T(8,128)S(1)} %select_select_fusion.cols_a, f32[512,128]{1,0:T(8,128)S(1)} %collective-permute-done.23.cols_b, ...), custom_call_target="tpu_custom_call" | custom-call | tf_op jit(solution)/shard_map/pallas_call | solution.py:172
  (46 shorter events, 4.7 us)
Async XLA Ops:
  1.2 3.3 %collective-permute-start = (f32[128,128]{1,0:T(8,128)S(1)}, f32[128,128]{1,0:T(8,128)S(1)}, u32[]{:S(2)}, u32[]{:S(2)}) collective-permute-start(f32[128,128]{1,0:T(8,128)S(1)} %get-tuple-element.16), channel_id=1, source_target_pairs={{0,1},{1,0},{16,17},{17,16}} | collective-permute-start | bytes 196616 | tf_op jit(solution)/shard_map/ppermute | solution.py:25
  1.8 2.7 %collective-permute-start.2 = (f32[128,128]{1,0:T(8,128)S(1)}, f32[128,128]{1,0:T(8,128)S(1)}, u32[]{:S(2)}, u32[]{:S(2)}) collective-permute-start(f32[128,128]{1,0:T(8,128)S(1)} %get-tuple-element.16), channel_id=1, source_target_pairs={{0,2},{1,3},{16,18},{17,19}} | collective-permute-start | bytes 196616 | tf_op jit(solution)/shard_map/ppermute | solution.py:25
  2.5 2.0 %collective-permute-start.1 = (f32[128,128]{1,0:T(8,128)S(1)}, f32[128,128]{1,0:T(8,128)S(1)}, u32[]{:S(2)}, u32[]{:S(2)}) collective-permute-start(f32[128,128]{1,0:T(8,128)S(1)} %get-tuple-element.16), channel_id=1, source_target_pairs={{0,3},{1,2},{16,19},{17,18}} | collective-permute-start | bytes 196616 | tf_op jit(solution)/shard_map/ppermute | solution.py:25
  3.2 9.7 %collective-permute-start.7 = (f32[512,128]{1,0:T(8,128)S(1)}, f32[512,128]{1,0:T(8,128)S(1)}, u32[]{:S(2)}, u32[]{:S(2)}) collective-permute-start(f32[512,128]{1,0:T(8,128)S(1)} %get-tuple-element.19), channel_id=1, source_target_pairs={{0,32},{1,33},{2,34},{3,35},{4,36},{5,37},{6,38},{7,39},{8,40},{9,... | collective-permute-start | bytes 786440 | tf_op jit(solution)/shard_map/ppermute | solution.py:25
  4.6 15.0 %collective-permute-start.13 = (f32[192,128]{1,0:T(8,128)S(1)}, f32[192,128]{1,0:T(8,128)S(1)}, u32[]{:S(2)}, u32[]{:S(2)}) collective-permute-start(f32[192,128]{1,0:T(8,128)S(1)} %pad_maximum_fusion), channel_id=1, source_target_pairs={{0,12},{1,13},{2,14},{3,15},{16,28},{17,29},{18,30},{19,31}} | collective-permute-start | bytes 294920 | tf_op jit(solution)/shard_map/ppermute | solution.py:25
  5.3 14.4 %collective-permute-start.14 = (f32[192,128]{1,0:T(8,128)S(1)}, f32[192,128]{1,0:T(8,128)S(1)}, u32[]{:S(2)}, u32[]{:S(2)}) collective-permute-start(f32[192,128]{1,0:T(8,128)S(1)} %pad_maximum_fusion), channel_id=1, source_target_pairs={{0,4},{1,5},{2,6},{3,7},{16,20},{17,21},{18,22},{19,23}} | collective-permute-start | bytes 294920 | tf_op jit(solution)/shard_map/ppermute | solution.py:25
  5.9 13.7 %collective-permute-start.15 = (f32[192,128]{1,0:T(8,128)S(1)}, f32[192,128]{1,0:T(8,128)S(1)}, u32[]{:S(2)}, u32[]{:S(2)}) collective-permute-start(f32[192,128]{1,0:T(8,128)S(1)} %pad_maximum_fusion), channel_id=1, source_target_pairs={{0,8},{1,9},{2,10},{3,11},{16,24},{17,25},{18,26},{19,27}} | collective-permute-start | bytes 294920 | tf_op jit(solution)/shard_map/ppermute | solution.py:25
  12.9 8.9 %collective-permute-start.8 = (f32[512,128]{1,0:T(8,128)S(1)}, f32[512,128]{1,0:T(8,128)S(1)}, u32[]{:S(2)}, u32[]{:S(2)}) collective-permute-start(f32[512,128]{1,0:T(8,128)S(1)} %broadcast_select_fusion), channel_id=1, source_target_pairs={{32,160},{33,161},{34,162},{35,163},{36,164},{37,165},{38,166},{39... | collective-permute-start | bytes 786440 | tf_op jit(solution)/shard_map/ppermute | solution.py:25
  15.0 10.2 %collective-permute-start.3 = (f32[256,128]{1,0:T(8,128)S(1)}, f32[256,128]{1,0:T(8,128)S(1)}, u32[]{:S(2)}, u32[]{:S(2)}) collective-permute-start(f32[256,128]{1,0:T(8,128)S(1)} %get-tuple-element.17), channel_id=1, source_target_pairs={{0,3},{1,2},{16,19},{17,18},{32,35},{33,34},{48,51},{49,50},{64,67... | collective-permute-start | bytes 393224 | tf_op jit(solution)/shard_map/ppermute | solution.py:25
  19.7 7.2 %collective-permute-start.16 = (f32[192,128]{1,0:T(8,128)S(1)}, f32[192,128]{1,0:T(8,128)S(1)}, u32[]{:S(2)}, u32[]{:S(2)}) collective-permute-start(f32[192,128]{1,0:T(8,128)S(1)} %select_select_fusion.3), channel_id=1, source_target_pairs={{0,64},{1,65},{2,66},{3,67},{4,68},{5,69},{6,70},{7,71},{8,72},{9,... | collective-permute-start | bytes 294920 | tf_op jit(solution)/shard_map/ppermute | solution.py:25
  20.4 6.6 %collective-permute-start.17 = (f32[192,128]{1,0:T(8,128)S(1)}, f32[192,128]{1,0:T(8,128)S(1)}, u32[]{:S(2)}, u32[]{:S(2)}) collective-permute-start(f32[192,128]{1,0:T(8,128)S(1)} %select_select_fusion.3), channel_id=1, source_target_pairs={{0,384},{1,385},{2,386},{3,387},{4,388},{5,389},{6,390},{7,391},{8... | collective-permute-start | bytes 294920 | tf_op jit(solution)/shard_map/ppermute | solution.py:25
  21.0 5.9 %collective-permute-start.18 = (f32[192,128]{1,0:T(8,128)S(1)}, f32[192,128]{1,0:T(8,128)S(1)}, u32[]{:S(2)}, u32[]{:S(2)}) collective-permute-start(f32[192,128]{1,0:T(8,128)S(1)} %select_select_fusion.3), channel_id=1, source_target_pairs={{0,128},{1,129},{2,130},{3,131},{4,132},{5,133},{6,134},{7,135},{8... | collective-permute-start | bytes 294920 | tf_op jit(solution)/shard_map/ppermute | solution.py:25
  21.8 8.1 %collective-permute-start.9 = (f32[512,128]{1,0:T(8,128)S(1)}, f32[512,128]{1,0:T(8,128)S(1)}, u32[]{:S(2)}, u32[]{:S(2)}) collective-permute-start(f32[512,128]{1,0:T(8,128)S(1)} %broadcast_select_fusion.1), channel_id=1, source_target_pairs={{32,416},{33,417},{34,418},{35,419},{36,420},{37,421},{38,422},{39... | collective-permute-start | bytes 786440 | tf_op jit(solution)/shard_map/ppermute | solution.py:25
  25.2 19.1 %collective-permute-start.4 = (f32[256,128]{1,0:T(8,128)S(1)}, f32[256,128]{1,0:T(8,128)S(1)}, u32[]{:S(2)}, u32[]{:S(2)}) collective-permute-start(f32[256,128]{1,0:T(8,128)S(1)} %broadcast_select_fusion.3), channel_id=1, source_target_pairs={{0,8},{1,9},{2,10},{3,11},{16,24},{17,25},{18,26},{19,27},{32,40},... | collective-permute-start | bytes 393224 | tf_op jit(solution)/shard_map/ppermute | solution.py:25
  27.0 5.4 %collective-permute-start.19 = (f32[192,128]{1,0:T(8,128)S(1)}, f32[192,128]{1,0:T(8,128)S(1)}, u32[]{:S(2)}, u32[]{:S(2)}) collective-permute-start(f32[192,128]{1,0:T(8,128)S(1)} %select_select_fusion.2), channel_id=1, source_target_pairs={{0,480},{1,481},{2,482},{3,483},{4,484},{5,485},{6,486},{7,487},{8... | collective-permute-start | bytes 294920 | tf_op jit(solution)/shard_map/ppermute | solution.py:25
  28.3 5.4 %collective-permute-start.20 = (f32[192,128]{1,0:T(8,128)S(1)}, f32[192,128]{1,0:T(8,128)S(1)}, u32[]{:S(2)}, u32[]{:S(2)}) collective-permute-start(f32[192,128]{1,0:T(8,128)S(1)} %select_select_fusion.2), channel_id=1, source_target_pairs={{0,448},{1,449},{2,450},{3,451},{4,452},{5,453},{6,454},{7,455},{8... | collective-permute-start | bytes 294920 | tf_op jit(solution)/shard_map/ppermute | solution.py:25
  29.0 11.1 %collective-permute-start.21 = (f32[192,128]{1,0:T(8,128)S(1)}, f32[192,128]{1,0:T(8,128)S(1)}, u32[]{:S(2)}, u32[]{:S(2)}) collective-permute-start(f32[192,128]{1,0:T(8,128)S(1)} %select_select_fusion.2), channel_id=1, source_target_pairs={{0,416},{1,417},{2,418},{3,419},{4,420},{5,421},{6,422},{7,423},{8... | collective-permute-start | bytes 294920 | tf_op jit(solution)/shard_map/ppermute | solution.py:25
  29.9 20.8 %collective-permute-start.10 = (f32[512,128]{1,0:T(8,128)S(1)}, f32[512,128]{1,0:T(8,128)S(1)}, u32[]{:S(2)}, u32[]{:S(2)}) collective-permute-start(f32[512,128]{1,0:T(8,128)S(1)} %broadcast_select_fusion.2), channel_id=1, source_target_pairs={{160,224},{161,225},{162,226},{163,227},{164,228},{165,229},{166,2... | collective-permute-start | bytes 786440 | tf_op jit(solution)/shard_map/ppermute | solution.py:25
  32.3 18.4 %collective-permute-start.11 = (f32[512,128]{1,0:T(8,128)S(1)}, f32[512,128]{1,0:T(8,128)S(1)}, u32[]{:S(2)}, u32[]{:S(2)}) collective-permute-start(f32[512,128]{1,0:T(8,128)S(1)} %broadcast_select_fusion.2), channel_id=1, source_target_pairs={{32,96},{33,97},{34,98},{35,99},{36,100},{37,101},{38,102},{39,103... | collective-permute-start | bytes 786440 | tf_op jit(solution)/shard_map/ppermute | solution.py:25
  33.7 17.1 %collective-permute-start.12 = (f32[512,128]{1,0:T(8,128)S(1)}, f32[512,128]{1,0:T(8,128)S(1)}, u32[]{:S(2)}, u32[]{:S(2)}) collective-permute-start(f32[512,128]{1,0:T(8,128)S(1)} %broadcast_select_fusion.2), channel_id=1, source_target_pairs={{32,64},{33,65},{34,66},{35,67},{36,68},{37,69},{38,70},{39,71},{4... | collective-permute-start | bytes 786440 | tf_op jit(solution)/shard_map/ppermute | solution.py:25
  40.1 5.6 %collective-permute-start.22 = (f32[192,128]{1,0:T(8,128)S(1)}, f32[192,128]{1,0:T(8,128)S(1)}, u32[]{:S(2)}, u32[]{:S(2)}) collective-permute-start(f32[192,128]{1,0:T(8,128)S(1)} %select_select_fusion.1.mine), channel_id=1, source_target_pairs={{0,16},{1,17},{2,18},{3,19},{4,20},{5,21},{6,22},{7,23},{8,24},{9,... | collective-permute-start | bytes 294920 | tf_op jit(solution)/shard_map/ppermute | solution.py:25
  44.4 8.3 %collective-permute-start.5 = (f32[256,128]{1,0:T(8,128)S(1)}, f32[256,128]{1,0:T(8,128)S(1)}, u32[]{:S(2)}, u32[]{:S(2)}) collective-permute-start(f32[256,128]{1,0:T(8,128)S(1)} %broadcast_select_fusion.4), channel_id=1, source_target_pairs={{0,4},{1,5},{2,6},{3,7},{8,12},{9,13},{10,14},{11,15},{16,20},{17,... | collective-permute-start | bytes 393224 | tf_op jit(solution)/shard_map/ppermute | solution.py:25
  50.8 10.2 %collective-permute-start.23 = (f32[512,128]{1,0:T(8,128)S(1)}, f32[512,128]{1,0:T(8,128)S(1)}, u32[]{:S(2)}, u32[]{:S(2)}) collective-permute-start(f32[512,128]{1,0:T(8,128)S(1)} %select_select_fusion.cols_a), channel_id=1, source_target_pairs={{0,16},{1,17},{2,18},{3,19},{4,20},{5,21},{6,22},{7,23},{8,24},{9,... | collective-permute-start | bytes 786440 | tf_op jit(solution)/shard_map/ppermute | solution.py:25
  52.8 8.2 %collective-permute-start.6 = (f32[256,128]{1,0:T(8,128)S(1)}, f32[256,128]{1,0:T(8,128)S(1)}, u32[]{:S(2)}, u32[]{:S(2)}) collective-permute-start(f32[256,128]{1,0:T(8,128)S(1)} %broadcast_select_fusion.5.rows_a), channel_id=1, source_target_pairs={{0,1},{1,0},{2,3},{3,2},{4,5},{5,4},{6,7},{7,6},{8,9},{9,8},{10,11... | collective-permute-start | bytes 393224 | tf_op jit(solution)/shard_map/ppermute | solution.py:25
  (2 other events, 5.1 us)

commit v4 on v3

--- a/solution.py
+++ b/solution.py
@@ -32,50 +32,71 @@
 def invert_factor(x_ref, w_ref):
     sub = lax.broadcasted_iota(jnp.int32, (8, NB), 0)
     lane = lax.broadcasted_iota(jnp.int32, (8, NB), 1)
+    wide = 16
+    groups = range(wide // 8)
 
     def spread(x, j):
-        return jnp.broadcast_to(x[j : j + 1, :], (8, NB))
+        return jnp.broadcast_to(x[j % 8 : j % 8 + 1, :], (8, NB))
 
     def splat(x, j):
         return jnp.broadcast_to(x[:, j : j + 1], (8, NB))
 
-    for k in range(NB // 8):
-        here = x_ref[8 * k : 8 * k + 8, :]
-        v = [splat(here, 8 * k + j) for j in range(8)]
-        mine = (lane >= 8 * k) & (lane < 8 * k + 8)
-        rest = jnp.where(mine, jnp.where(lane == sub + 8 * k, 1.0, 0.0), here)
-        for t in range(0, 8, 2):
-            a = spread(v[t], t)
-            b = spread(v[t], t + 1)
-            c = spread(v[t + 1], t + 1)
+    for start in range(0, NB, wide):
+        here = [x_ref[start + 8 * g : start + 8 * g + 8, :] for g in groups]
+        v = [[splat(here[g], start + j) for g in groups] for j in range(wide)]
+        mine = (lane >= start) & (lane < start + wide)
+        rest = [
+            jnp.where(mine, jnp.where(lane == sub + (start + 8 * g), 1.0, 0.0), here[g])
+            for g in groups
+        ]
+        for t in range(0, wide, 2):
+            home = t // 8
+            u = t % 8
+            a = spread(v[t][home], t)
+            b = spread(v[t][home], t + 1)
+            c = spread(v[t + 1][home], t + 1)
             det = a * c - b * b
             scale = 1.0 / det
             i00 = c * scale
             i01 = b * scale
             i11 = a * scale
-            f0 = jnp.where(
-                sub == t, 1.0 - i00, jnp.where(sub == t + 1, i01, v[t] * i00 - v[t + 1] * i01)
-            )
-            f1 = jnp.where(
-                sub == t, i01, jnp.where(sub == t + 1, 1.0 - i11, v[t + 1] * i11 - v[t] * i01)
-            )
-            for j in range(t + 2, 8):
-                v[j] = v[j] - f0 * spread(v[j], t) - f1 * spread(v[j], t + 1)
-            r0 = spread(rest, t)
-            r1 = spread(rest, t + 1)
+            f0 = []
+            f1 = []
+            for g in groups:
+                p0 = v[t][g] * i00 - v[t + 1][g] * i01
+                p1 = v[t + 1][g] * i11 - v[t][g] * i01
+                if g == home:
+                    p0 = jnp.where(sub == u, 1.0 - i00, jnp.where(sub == u + 1, i01, p0))
+                    p1 = jnp.where(sub == u, i01, jnp.where(sub == u + 1, 1.0 - i11, p1))
+                f0.append(p0)
+                f1.append(p1)
+            for j in range(t + 2, wide):
+                s0 = spread(v[j][home], t)
+                s1 = spread(v[j][home], t + 1)
+                v[j] = [v[j][g] - f0[g] * s0 - f1[g] * s1 for g in groups]
+            r0 = spread(rest[home], t)
+            r1 = spread(rest[home], t + 1)
             over = 1.0 / a
-            at = 8 * k + t
+            at = start + t
             w_ref[at : at + 1, :] = (r0 * lax.rsqrt(a))[:1]
             w_ref[at + 1 : at + 2, :] = ((r1 - (b * over) * r0) * lax.rsqrt(det * over))[:1]
-            rest = rest - f0 * r0 - f1 * r1
-        z = [spread(rest, j) for j in range(8)]
-        for h in range(k + 1, NB // 8):
-            there = slice(8 * h, 8 * h + 8)
-            x = x_ref[there, :]
-            terms = [splat(x, 8 * k + j) * z[j] for j in range(8)]
+            rest = [rest[g] - f0[g] * r0 - f1[g] * r1 for g in groups]
+        after = start + wide
+        below = after + wide
+        if below < NB:
+            pieces = [jnp.zeros((start, NB), F32)] if start else []
+            z = jnp.concatenate(pieces + rest + [jnp.zeros((NB - after, NB), F32)], axis=0)
+            far = x_ref[below:, :]
+            ours = jnp.broadcast_to(mine[:1], far.shape)
+            change = dot(jnp.where(ours, far, 0.0), z, ((1,), (0,)))
+            x_ref[below:, :] = jnp.where(ours, 0.0, far) - change
+        rows = [spread(rest[j // 8], j) for j in range(wide)]
+        for h in range(after, min(below, NB), 8):
+            x = x_ref[h : h + 8, :]
+            terms = [splat(x, start + j) * rows[j] for j in range(wide)]
             while len(terms) > 1:
                 terms = [terms[i] + terms[i + 1] for i in range(0, len(terms), 2)]
-            x_ref[there, :] = jnp.where(mine, 0.0, x) - terms[0]
+            x_ref[h : h + 8, :] = jnp.where(mine, 0.0, x) - terms[0]
 
 
 def indices():

time: 65.4 us -> 63.5 us (0.971)
  the two profiles are of different devices: /device:TPU:33 before, /device:TPU:40 now
where the time goes in v4:
time: 63.5 us; the launch traced here: 62.9 us
  starting transfers between devices  33.6 us (53%)
  waiting for transfers between devices  17.5 us (28%)
  Pallas kernels  9.81 us (15%)
  local copies, waits for them, and re-layouts  1.05 us (2%)
    ppermute x24, starting transfers between devices, move(): return lax.ppermute(value, ('row', 'col'), flat)  33.6 us
    ppermute x24, waiting for transfers between devices, move(): return lax.ppermute(value, ('row', 'col'), flat)  17.5 us
    pallas_call x4, Pallas kernels, call(): pl.pallas_call(body, out_shape=shapes, in_specs=[VMEM] * len(args), out_s...  9.81 us
  transfers between devices with their start and end apart: 24, of which 4 were waited for; matrix products, arithmetic and copies ran while one was open for 0% of the time, Pallas kernels for 9%

profile of v4, /device:TPU:40, one launch (start us, length us, event | category | flops | bytes accessed | tf_op | source)
XLA Modules:
  0.0 62.9 jit_solution(6412044899881378321)
XLA Ops:
  0.0 1.0 %copy-done = f32[2,128,4,128]{3,2,1,0:T(4,128)S(1)} copy-done((f32[2,128,4,128]{3,2,1,0:T(4,128)S(1)}, f32[2,128,4,128]{3,2,1,0:T(4,128)}, u32[]{:S(2)}) %copy-start) | copy-done | bytes 524312
  3.2 1.3 %collective-permute-start.7 = (f32[512,128]{1,0:T(8,128)S(1)}, f32[512,128]{1,0:T(8,128)S(1)}, u32[]{:S(2)}, u32[]{:S(2)}) collective-permute-start(f32[512,128]{1,0:T(8,128)S(1)} %get-tuple-element.19), channel_id=1, source_target_pairs={{0,32},{1,33},{2,34},{3,35},{4,36},{5,37},{6,38},{7,39},{8,40},{9,... | collective-permute-start | bytes 786440 | tf_op jit(solution)/shard_map/ppermute | solution.py:25
  4.6 0.7 %collective-permute-start.13 = (f32[192,128]{1,0:T(8,128)S(1)}, f32[192,128]{1,0:T(8,128)S(1)}, u32[]{:S(2)}, u32[]{:S(2)}) collective-permute-start(f32[192,128]{1,0:T(8,128)S(1)} %pad_maximum_fusion), channel_id=1, source_target_pairs={{0,12},{1,13},{2,14},{3,15},{16,28},{17,29},{18,30},{19,31}} | collective-permute-start | bytes 294920 | tf_op jit(solution)/shard_map/ppermute | solution.py:25
  5.3 0.7 %collective-permute-start.14 = (f32[192,128]{1,0:T(8,128)S(1)}, f32[192,128]{1,0:T(8,128)S(1)}, u32[]{:S(2)}, u32[]{:S(2)}) collective-permute-start(f32[192,128]{1,0:T(8,128)S(1)} %pad_maximum_fusion), channel_id=1, source_target_pairs={{0,4},{1,5},{2,6},{3,7},{16,20},{17,21},{18,22},{19,23}} | collective-permute-start | bytes 294920 | tf_op jit(solution)/shard_map/ppermute | solution.py:25
  5.9 0.7 %collective-permute-start.15 = (f32[192,128]{1,0:T(8,128)S(1)}, f32[192,128]{1,0:T(8,128)S(1)}, u32[]{:S(2)}, u32[]{:S(2)}) collective-permute-start(f32[192,128]{1,0:T(8,128)S(1)} %pad_maximum_fusion), channel_id=1, source_target_pairs={{0,8},{1,9},{2,10},{3,11},{16,24},{17,25},{18,26},{19,27}} | collective-permute-start | bytes 294920 | tf_op jit(solution)/shard_map/ppermute | solution.py:25
  6.6 10.6 %collective-permute-done.7 = f32[512,128]{1,0:T(8,128)S(1)} collective-permute-done((f32[512,128]{1,0:T(8,128)S(1)}, f32[512,128]{1,0:T(8,128)S(1)}, u32[]{:S(2)}, u32[]{:S(2)}) %collective-permute-start.7) | collective-permute-done | bytes 262176 | tf_op jit(solution)/shard_map/ppermute | solution.py:25
  17.3 1.3 %collective-permute-start.8 = (f32[512,128]{1,0:T(8,128)S(1)}, f32[512,128]{1,0:T(8,128)S(1)}, u32[]{:S(2)}, u32[]{:S(2)}) collective-permute-start(f32[512,128]{1,0:T(8,128)S(1)} %broadcast_select_fusion), channel_id=1, source_target_pairs={{32,160},{33,161},{34,162},{35,163},{36,164},{37,165},{38,166},{39... | collective-permute-start | bytes 786440 | tf_op jit(solution)/shard_map/ppermute | solution.py:25
  18.7 1.3 %collective-permute-start.3 = (f32[256,128]{1,0:T(8,128)S(1)}, f32[256,128]{1,0:T(8,128)S(1)}, u32[]{:S(2)}, u32[]{:S(2)}) collective-permute-start(f32[256,128]{1,0:T(8,128)S(1)} %get-tuple-element.17), channel_id=1, source_target_pairs={{0,3},{1,2},{16,19},{17,18},{32,35},{33,34},{48,51},{49,50},{64,67... | collective-permute-start | bytes 393224 | tf_op jit(solution)/shard_map/ppermute | solution.py:25
  22.1 0.8 %collective-permute-done.8 = f32[512,128]{1,0:T(8,128)S(1)} collective-permute-done((f32[512,128]{1,0:T(8,128)S(1)}, f32[512,128]{1,0:T(8,128)S(1)}, u32[]{:S(2)}, u32[]{:S(2)}) %collective-permute-start.8) | collective-permute-done | bytes 262176 | tf_op jit(solution)/shard_map/ppermute | solution.py:25
  22.9 1.4 %collective-permute-start.9 = (f32[512,128]{1,0:T(8,128)S(1)}, f32[512,128]{1,0:T(8,128)S(1)}, u32[]{:S(2)}, u32[]{:S(2)}) collective-permute-start(f32[512,128]{1,0:T(8,128)S(1)} %broadcast_select_fusion.1), channel_id=1, source_target_pairs={{32,416},{33,417},{34,418},{35,419},{36,420},{37,421},{38,422},{39... | collective-permute-start | bytes 786440 | tf_op jit(solution)/shard_map/ppermute | solution.py:25
  24.3 3.7 %collective-permute-start.4 = (f32[256,128]{1,0:T(8,128)S(1)}, f32[256,128]{1,0:T(8,128)S(1)}, u32[]{:S(2)}, u32[]{:S(2)}) collective-permute-start(f32[256,128]{1,0:T(8,128)S(1)} %broadcast_select_fusion.3), channel_id=1, source_target_pairs={{0,8},{1,9},{2,10},{3,11},{16,24},{17,25},{18,26},{19,27},{32,40},... | collective-permute-start | bytes 393224 | tf_op jit(solution)/shard_map/ppermute | solution.py:25
  28.1 1.3 %collective-permute-start.19 = (f32[192,128]{1,0:T(8,128)S(1)}, f32[192,128]{1,0:T(8,128)S(1)}, u32[]{:S(2)}, u32[]{:S(2)}) collective-permute-start(f32[192,128]{1,0:T(8,128)S(1)} %select_select_fusion.2), channel_id=1, source_target_pairs={{0,480},{1,481},{2,482},{3,483},{4,484},{5,485},{6,486},{7,487},{8... | collective-permute-start | bytes 294920 | tf_op jit(solution)/shard_map/ppermute | solution.py:25
  30.8 0.7 %collective-permute-start.10 = (f32[512,128]{1,0:T(8,128)S(1)}, f32[512,128]{1,0:T(8,128)S(1)}, u32[]{:S(2)}, u32[]{:S(2)}) collective-permute-start(f32[512,128]{1,0:T(8,128)S(1)} %broadcast_select_fusion.2), channel_id=1, source_target_pairs={{160,224},{161,225},{162,226},{163,227},{164,228},{165,229},{166,2... | collective-permute-start | bytes 786440 | tf_op jit(solution)/shard_map/ppermute | solution.py:25
  31.5 3.1 %collective-permute-done.19 = f32[192,128]{1,0:T(8,128)S(1)} collective-permute-done((f32[192,128]{1,0:T(8,128)S(1)}, f32[192,128]{1,0:T(8,128)S(1)}, u32[]{:S(2)}, u32[]{:S(2)}) %collective-permute-start.19) | collective-permute-done | bytes 98336 | tf_op jit(solution)/shard_map/ppermute | solution.py:25
  34.6 1.3 %collective-permute-start.11 = (f32[512,128]{1,0:T(8,128)S(1)}, f32[512,128]{1,0:T(8,128)S(1)}, u32[]{:S(2)}, u32[]{:S(2)}) collective-permute-start(f32[512,128]{1,0:T(8,128)S(1)} %broadcast_select_fusion.2), channel_id=1, source_target_pairs={{32,96},{33,97},{34,98},{35,99},{36,100},{37,101},{38,102},{39,103... | collective-permute-start | bytes 786440 | tf_op jit(solution)/shard_map/ppermute | solution.py:25
  36.0 5.8 %collective-permute-start.12 = (f32[512,128]{1,0:T(8,128)S(1)}, f32[512,128]{1,0:T(8,128)S(1)}, u32[]{:S(2)}, u32[]{:S(2)}) collective-permute-start(f32[512,128]{1,0:T(8,128)S(1)} %broadcast_select_fusion.2), channel_id=1, source_target_pairs={{32,64},{33,65},{34,66},{35,67},{36,68},{37,69},{38,70},{39,71},{4... | collective-permute-start | bytes 786440 | tf_op jit(solution)/shard_map/ppermute | solution.py:25
  41.8 1.9 %collective-permute-start.22 = (f32[192,128]{1,0:T(8,128)S(1)}, f32[192,128]{1,0:T(8,128)S(1)}, u32[]{:S(2)}, u32[]{:S(2)}) collective-permute-start(f32[192,128]{1,0:T(8,128)S(1)} %select_select_fusion.1.mine), channel_id=1, source_target_pairs={{0,16},{1,17},{2,18},{3,19},{4,20},{5,21},{6,22},{7,23},{8,24},{9,... | collective-permute-start | bytes 294920 | tf_op jit(solution)/shard_map/ppermute | solution.py:25
  43.7 2.3 %collective-permute-start.5 = (f32[256,128]{1,0:T(8,128)S(1)}, f32[256,128]{1,0:T(8,128)S(1)}, u32[]{:S(2)}, u32[]{:S(2)}) collective-permute-start(f32[256,128]{1,0:T(8,128)S(1)} %broadcast_select_fusion.4), channel_id=1, source_target_pairs={{0,4},{1,5},{2,6},{3,7},{8,12},{9,13},{10,14},{11,15},{16,20},{17,... | collective-permute-start | bytes 393224 | tf_op jit(solution)/shard_map/ppermute | solution.py:25
  46.0 3.2 %shard_map.18 = (f32[128,128]{1,0:T(8,128)S(1)}, f32[128,128]{1,0:T(8,128)S(1)}, f32[128,128]{1,0:T(8,128)S(1)}) custom-call(f32[192,128]{1,0:T(8,128)S(1)} %select_select_fusion.1.mine, f32[192,128]{1,0:T(8,128)S(1)} %collective-permute-done.22.other), custom_call_target="tpu_custom_call" | custom-call | tf_op jit(solution)/shard_map/pallas_call | solution.py:193
  49.3 2.1 %collective-permute-start.23 = (f32[512,128]{1,0:T(8,128)S(1)}, f32[512,128]{1,0:T(8,128)S(1)}, u32[]{:S(2)}, u32[]{:S(2)}) collective-permute-start(f32[512,128]{1,0:T(8,128)S(1)} %select_select_fusion.cols_a), channel_id=1, source_target_pairs={{0,16},{1,17},{2,18},{3,19},{4,20},{5,21},{6,22},{7,23},{8,24},{9,... | collective-permute-start | bytes 786440 | tf_op jit(solution)/shard_map/ppermute | solution.py:25
  51.5 1.9 %collective-permute-start.6 = (f32[256,128]{1,0:T(8,128)S(1)}, f32[256,128]{1,0:T(8,128)S(1)}, u32[]{:S(2)}, u32[]{:S(2)}) collective-permute-start(f32[256,128]{1,0:T(8,128)S(1)} %broadcast_select_fusion.5.rows_a), channel_id=1, source_target_pairs={{0,1},{1,0},{2,3},{3,2},{4,5},{5,4},{6,7},{7,6},{8,9},{9,8},{10,11... | collective-permute-start | bytes 393224 | tf_op jit(solution)/shard_map/ppermute | solution.py:25
  53.5 2.7 %shard_map.19.w1 = f32[128,128]{1,0:T(8,128)S(1)} custom-call(f32[128,128]{1,0:T(8,128)S(1)} %get-tuple-element.21.s11, f32[8,128]{1,0:T(8,128)S(1)} %slice.11.mark), custom_call_target="tpu_custom_call" | custom-call | flops 1000000000 | bytes 1000000000 | tf_op jit(solution)/shard_map/pallas_call | solution.py:193
  56.2 2.9 %collective-permute-done.6.rows_b = f32[256,128]{1,0:T(8,128)S(1)} collective-permute-done((f32[256,128]{1,0:T(8,128)S(1)}, f32[256,128]{1,0:T(8,128)S(1)}, u32[]{:S(2)}, u32[]{:S(2)}) %collective-permute-start.6) | collective-permute-done | bytes 131104 | tf_op jit(solution)/shard_map/ppermute | solution.py:25
  59.1 3.8 %shard_map.20 = f32[1024,128]{1,0:T(8,128)} custom-call(f32[1024,128]{1,0:T(8,128)S(1)} %bitcast.3, f32[256,128]{1,0:T(8,128)S(1)} %broadcast_select_fusion.5.rows_a, f32[256,128]{1,0:T(8,128)S(1)} %collective-permute-done.6.rows_b, f32[512,128]{1,0:T(8,128)S(1)} %select_select_fusion.cols_a, f32[512,128]{1,0:T(8,128)S(1)} %collective-permute-done.23.cols_b, ...), custom_call_target="tpu_custom_call" | custom-call | tf_op jit(solution)/shard_map/pallas_call | solution.py:193
  (46 shorter events, 5.8 us)
Async XLA Ops:
  1.2 3.3 %collective-permute-start = (f32[128,128]{1,0:T(8,128)S(1)}, f32[128,128]{1,0:T(8,128)S(1)}, u32[]{:S(2)}, u32[]{:S(2)}) collective-permute-start(f32[128,128]{1,0:T(8,128)S(1)} %get-tuple-element.16), channel_id=1, source_target_pairs={{0,1},{1,0},{16,17},{17,16}} | collective-permute-start | bytes 196616 | tf_op jit(solution)/shard_map/ppermute | solution.py:25
  1.8 2.7 %collective-permute-start.2 = (f32[128,128]{1,0:T(8,128)S(1)}, f32[128,128]{1,0:T(8,128)S(1)}, u32[]{:S(2)}, u32[]{:S(2)}) collective-permute-start(f32[128,128]{1,0:T(8,128)S(1)} %get-tuple-element.16), channel_id=1, source_target_pairs={{0,2},{1,3},{16,18},{17,19}} | collective-permute-start | bytes 196616 | tf_op jit(solution)/shard_map/ppermute | solution.py:25
  2.5 2.0 %collective-permute-start.1 = (f32[128,128]{1,0:T(8,128)S(1)}, f32[128,128]{1,0:T(8,128)S(1)}, u32[]{:S(2)}, u32[]{:S(2)}) collective-permute-start(f32[128,128]{1,0:T(8,128)S(1)} %get-tuple-element.16), channel_id=1, source_target_pairs={{0,3},{1,2},{16,19},{17,18}} | collective-permute-start | bytes 196616 | tf_op jit(solution)/shard_map/ppermute | solution.py:25
  3.2 14.1 %collective-permute-start.7 = (f32[512,128]{1,0:T(8,128)S(1)}, f32[512,128]{1,0:T(8,128)S(1)}, u32[]{:S(2)}, u32[]{:S(2)}) collective-permute-start(f32[512,128]{1,0:T(8,128)S(1)} %get-tuple-element.19), channel_id=1, source_target_pairs={{0,32},{1,33},{2,34},{3,35},{4,36},{5,37},{6,38},{7,39},{8,40},{9,... | collective-permute-start | bytes 786440 | tf_op jit(solution)/shard_map/ppermute | solution.py:25
  4.6 15.4 %collective-permute-start.13 = (f32[192,128]{1,0:T(8,128)S(1)}, f32[192,128]{1,0:T(8,128)S(1)}, u32[]{:S(2)}, u32[]{:S(2)}) collective-permute-start(f32[192,128]{1,0:T(8,128)S(1)} %pad_maximum_fusion), channel_id=1, source_target_pairs={{0,12},{1,13},{2,14},{3,15},{16,28},{17,29},{18,30},{19,31}} | collective-permute-start | bytes 294920 | tf_op jit(solution)/shard_map/ppermute | solution.py:25
  5.3 14.7 %collective-permute-start.14 = (f32[192,128]{1,0:T(8,128)S(1)}, f32[192,128]{1,0:T(8,128)S(1)}, u32[]{:S(2)}, u32[]{:S(2)}) collective-permute-start(f32[192,128]{1,0:T(8,128)S(1)} %pad_maximum_fusion), channel_id=1, source_target_pairs={{0,4},{1,5},{2,6},{3,7},{16,20},{17,21},{18,22},{19,23}} | collective-permute-start | bytes 294920 | tf_op jit(solution)/shard_map/ppermute | solution.py:25
  5.9 14.1 %collective-permute-start.15 = (f32[192,128]{1,0:T(8,128)S(1)}, f32[192,128]{1,0:T(8,128)S(1)}, u32[]{:S(2)}, u32[]{:S(2)}) collective-permute-start(f32[192,128]{1,0:T(8,128)S(1)} %pad_maximum_fusion), channel_id=1, source_target_pairs={{0,8},{1,9},{2,10},{3,11},{16,24},{17,25},{18,26},{19,27}} | collective-permute-start | bytes 294920 | tf_op jit(solution)/shard_map/ppermute | solution.py:25
  17.3 5.6 %collective-permute-start.8 = (f32[512,128]{1,0:T(8,128)S(1)}, f32[512,128]{1,0:T(8,128)S(1)}, u32[]{:S(2)}, u32[]{:S(2)}) collective-permute-start(f32[512,128]{1,0:T(8,128)S(1)} %broadcast_select_fusion), channel_id=1, source_target_pairs={{32,160},{33,161},{34,162},{35,163},{36,164},{37,165},{38,166},{39... | collective-permute-start | bytes 786440 | tf_op jit(solution)/shard_map/ppermute | solution.py:25
  18.7 5.6 %collective-permute-start.3 = (f32[256,128]{1,0:T(8,128)S(1)}, f32[256,128]{1,0:T(8,128)S(1)}, u32[]{:S(2)}, u32[]{:S(2)}) collective-permute-start(f32[256,128]{1,0:T(8,128)S(1)} %get-tuple-element.17), channel_id=1, source_target_pairs={{0,3},{1,2},{16,19},{17,18},{32,35},{33,34},{48,51},{49,50},{64,67... | collective-permute-start | bytes 393224 | tf_op jit(solution)/shard_map/ppermute | solution.py:25
  20.0 8.0 %collective-permute-start.16 = (f32[192,128]{1,0:T(8,128)S(1)}, f32[192,128]{1,0:T(8,128)S(1)}, u32[]{:S(2)}, u32[]{:S(2)}) collective-permute-start(f32[192,128]{1,0:T(8,128)S(1)} %select_select_fusion.3), channel_id=1, source_target_pairs={{0,64},{1,65},{2,66},{3,67},{4,68},{5,69},{6,70},{7,71},{8,72},{9,... | collective-permute-start | bytes 294920 | tf_op jit(solution)/shard_map/ppermute | solution.py:25
  20.7 7.4 %collective-permute-start.17 = (f32[192,128]{1,0:T(8,128)S(1)}, f32[192,128]{1,0:T(8,128)S(1)}, u32[]{:S(2)}, u32[]{:S(2)}) collective-permute-start(f32[192,128]{1,0:T(8,128)S(1)} %select_select_fusion.3), channel_id=1, source_target_pairs={{0,384},{1,385},{2,386},{3,387},{4,388},{5,389},{6,390},{7,391},{8... | collective-permute-start | bytes 294920 | tf_op jit(solution)/shard_map/ppermute | solution.py:25
  21.4 6.7 %collective-permute-start.18 = (f32[192,128]{1,0:T(8,128)S(1)}, f32[192,128]{1,0:T(8,128)S(1)}, u32[]{:S(2)}, u32[]{:S(2)}) collective-permute-start(f32[192,128]{1,0:T(8,128)S(1)} %select_select_fusion.3), channel_id=1, source_target_pairs={{0,128},{1,129},{2,130},{3,131},{4,132},{5,133},{6,134},{7,135},{8... | collective-permute-start | bytes 294920 | tf_op jit(solution)/shard_map/ppermute | solution.py:25
  22.9 7.9 %collective-permute-start.9 = (f32[512,128]{1,0:T(8,128)S(1)}, f32[512,128]{1,0:T(8,128)S(1)}, u32[]{:S(2)}, u32[]{:S(2)}) collective-permute-start(f32[512,128]{1,0:T(8,128)S(1)} %broadcast_select_fusion.1), channel_id=1, source_target_pairs={{32,416},{33,417},{34,418},{35,419},{36,420},{37,421},{38,422},{39... | collective-permute-start | bytes 786440 | tf_op jit(solution)/shard_map/ppermute | solution.py:25
  24.3 19.4 %collective-permute-start.4 = (f32[256,128]{1,0:T(8,128)S(1)}, f32[256,128]{1,0:T(8,128)S(1)}, u32[]{:S(2)}, u32[]{:S(2)}) collective-permute-start(f32[256,128]{1,0:T(8,128)S(1)} %broadcast_select_fusion.3), channel_id=1, source_target_pairs={{0,8},{1,9},{2,10},{3,11},{16,24},{17,25},{18,26},{19,27},{32,40},... | collective-permute-start | bytes 393224 | tf_op jit(solution)/shard_map/ppermute | solution.py:25
  28.1 6.5 %collective-permute-start.19 = (f32[192,128]{1,0:T(8,128)S(1)}, f32[192,128]{1,0:T(8,128)S(1)}, u32[]{:S(2)}, u32[]{:S(2)}) collective-permute-start(f32[192,128]{1,0:T(8,128)S(1)} %select_select_fusion.2), channel_id=1, source_target_pairs={{0,480},{1,481},{2,482},{3,483},{4,484},{5,485},{6,486},{7,487},{8... | collective-permute-start | bytes 294920 | tf_op jit(solution)/shard_map/ppermute | solution.py:25
  29.4 6.5 %collective-permute-start.20 = (f32[192,128]{1,0:T(8,128)S(1)}, f32[192,128]{1,0:T(8,128)S(1)}, u32[]{:S(2)}, u32[]{:S(2)}) collective-permute-start(f32[192,128]{1,0:T(8,128)S(1)} %select_select_fusion.2), channel_id=1, source_target_pairs={{0,448},{1,449},{2,450},{3,451},{4,452},{5,453},{6,454},{7,455},{8... | collective-permute-start | bytes 294920 | tf_op jit(solution)/shard_map/ppermute | solution.py:25
  30.1 11.6 %collective-permute-start.21 = (f32[192,128]{1,0:T(8,128)S(1)}, f32[192,128]{1,0:T(8,128)S(1)}, u32[]{:S(2)}, u32[]{:S(2)}) collective-permute-start(f32[192,128]{1,0:T(8,128)S(1)} %select_select_fusion.2), channel_id=1, source_target_pairs={{0,416},{1,417},{2,418},{3,419},{4,420},{5,421},{6,422},{7,423},{8... | collective-permute-start | bytes 294920 | tf_op jit(solution)/shard_map/ppermute | solution.py:25
  30.8 18.4 %collective-permute-start.10 = (f32[512,128]{1,0:T(8,128)S(1)}, f32[512,128]{1,0:T(8,128)S(1)}, u32[]{:S(2)}, u32[]{:S(2)}) collective-permute-start(f32[512,128]{1,0:T(8,128)S(1)} %broadcast_select_fusion.2), channel_id=1, source_target_pairs={{160,224},{161,225},{162,226},{163,227},{164,228},{165,229},{166,2... | collective-permute-start | bytes 786440 | tf_op jit(solution)/shard_map/ppermute | solution.py:25
  34.6 14.6 %collective-permute-start.11 = (f32[512,128]{1,0:T(8,128)S(1)}, f32[512,128]{1,0:T(8,128)S(1)}, u32[]{:S(2)}, u32[]{:S(2)}) collective-permute-start(f32[512,128]{1,0:T(8,128)S(1)} %broadcast_select_fusion.2), channel_id=1, source_target_pairs={{32,96},{33,97},{34,98},{35,99},{36,100},{37,101},{38,102},{39,103... | collective-permute-start | bytes 786440 | tf_op jit(solution)/shard_map/ppermute | solution.py:25
  36.0 13.3 %collective-permute-start.12 = (f32[512,128]{1,0:T(8,128)S(1)}, f32[512,128]{1,0:T(8,128)S(1)}, u32[]{:S(2)}, u32[]{:S(2)}) collective-permute-start(f32[512,128]{1,0:T(8,128)S(1)} %broadcast_select_fusion.2), channel_id=1, source_target_pairs={{32,64},{33,65},{34,66},{35,67},{36,68},{37,69},{38,70},{39,71},{4... | collective-permute-start | bytes 786440 | tf_op jit(solution)/shard_map/ppermute | solution.py:25
  41.8 4.3 %collective-permute-start.22 = (f32[192,128]{1,0:T(8,128)S(1)}, f32[192,128]{1,0:T(8,128)S(1)}, u32[]{:S(2)}, u32[]{:S(2)}) collective-permute-start(f32[192,128]{1,0:T(8,128)S(1)} %select_select_fusion.1.mine), channel_id=1, source_target_pairs={{0,16},{1,17},{2,18},{3,19},{4,20},{5,21},{6,22},{7,23},{8,24},{9,... | collective-permute-start | bytes 294920 | tf_op jit(solution)/shard_map/ppermute | solution.py:25
  43.7 7.8 %collective-permute-start.5 = (f32[256,128]{1,0:T(8,128)S(1)}, f32[256,128]{1,0:T(8,128)S(1)}, u32[]{:S(2)}, u32[]{:S(2)}) collective-permute-start(f32[256,128]{1,0:T(8,128)S(1)} %broadcast_select_fusion.4), channel_id=1, source_target_pairs={{0,4},{1,5},{2,6},{3,7},{8,12},{9,13},{10,14},{11,15},{16,20},{17,... | collective-permute-start | bytes 393224 | tf_op jit(solution)/shard_map/ppermute | solution.py:25
  49.3 9.8 %collective-permute-start.23 = (f32[512,128]{1,0:T(8,128)S(1)}, f32[512,128]{1,0:T(8,128)S(1)}, u32[]{:S(2)}, u32[]{:S(2)}) collective-permute-start(f32[512,128]{1,0:T(8,128)S(1)} %select_select_fusion.cols_a), channel_id=1, source_target_pairs={{0,16},{1,17},{2,18},{3,19},{4,20},{5,21},{6,22},{7,23},{8,24},{9,... | collective-permute-start | bytes 786440 | tf_op jit(solution)/shard_map/ppermute | solution.py:25
  51.5 7.6 %collective-permute-start.6 = (f32[256,128]{1,0:T(8,128)S(1)}, f32[256,128]{1,0:T(8,128)S(1)}, u32[]{:S(2)}, u32[]{:S(2)}) collective-permute-start(f32[256,128]{1,0:T(8,128)S(1)} %broadcast_select_fusion.5.rows_a), channel_id=1, source_target_pairs={{0,1},{1,0},{2,3},{3,2},{4,5},{5,4},{6,7},{7,6},{8,9},{9,8},{10,11... | collective-permute-start | bytes 393224 | tf_op jit(solution)/shard_map/ppermute | solution.py:25
  (2 other events, 6.7 us)

commit v5 on v4

--- a/solution.py
+++ b/solution.py
@@ -158,17 +158,19 @@
     y0 = dot(r0, w0v, ((1,), (1,)))
     y1 = dot(r1 - dot(y0, m, ((1,), (0,))), w1v, ((1,), (1,)))
     y = jnp.concatenate([y0, y1], axis=1)
+    def side(ref):
+        return jnp.concatenate([ref[NB * t : NB * (t + 1), :] for t in range(4)], axis=1)
+
+    ca = side(cols_a)
+    cb = side(cols_b)
+    x0 = dot(w0v, jnp.where(even, ca, cb), ((1,), (0,)))
+    x1 = dot(w1v, jnp.where(even, cb, ca) - dot(m, x0, ((0,), (0,))), ((1,), (0,)))
+    change = dot(y, jnp.concatenate([x0, x1], axis=0), ((1,), (0,)))
     for t in range(4):
-        at = slice(NB * t, NB * (t + 1))
-        ca = cols_a[at, :]
-        cb = cols_b[at, :]
-        x0 = dot(w0v, jnp.where(even, ca, cb), ((1,), (0,)))
-        x1 = dot(w1v, jnp.where(even, cb, ca) - dot(m, x0, ((0,), (0,))), ((1,), (0,)))
-        change = dot(y, jnp.concatenate([x0, x1], axis=0), ((1,), (0,)))
         for l in range(2):
             here = pl.ds(4 * NB * l + t, NB, stride=4)
             rs = slice(NB * l, NB * (l + 1))
-            new = x[here, :] - change[rs]
+            new = x[here, :] - change[rs, NB * t : NB * (t + 1)]
             if t == 0:
                 panel = jnp.where(q == 0, y0[rs], y1[rs])
                 if l == 0:

time: 63.5 us -> 62.7 us (0.987)
  Pallas kernels: 9.81 us -> 9.08 us
    pallas_call x4, Pallas kernels: 9.81 us -> 9.08 us  [call(): pl.pallas_call(body, out_shape=shapes, in_specs=[VMEM] * len(args), out_s...]
  transfers between devices with their start and end apart: 24 -> 24, of which waited for: 4 -> 4; matrix products, arithmetic and copies ran while one was open for 0% -> 1% of each run, Pallas kernels for 9% -> 10%
where the time goes in v5:
time: 62.7 us; the launch traced here: 62.2 us
  starting transfers between devices  33.6 us (54%)
  waiting for transfers between devices  17.5 us (28%)
  Pallas kernels  9.08 us (14%)
  local copies, waits for them, and re-layouts  1.05 us (2%)
    ppermute x24, starting transfers between devices, move(): return lax.ppermute(value, ('row', 'col'), flat)  33.6 us
    ppermute x24, waiting for transfers between devices, move(): return lax.ppermute(value, ('row', 'col'), flat)  17.5 us
    pallas_call x4, Pallas kernels, call(): pl.pallas_call(body, out_shape=shapes, in_specs=[VMEM] * len(args), out_s...  9.08 us
  transfers between devices with their start and end apart: 24, of which 4 were waited for; matrix products, arithmetic and copies ran while one was open for 1% of the time, Pallas kernels for 10%

profile of v5, /device:TPU:40, one launch (start us, length us, event | category | flops | bytes accessed | tf_op | source)
XLA Modules:
  0.0 62.2 jit_solution(8692952242762027360)
XLA Ops:
  0.0 1.0 %copy-done = f32[2,128,4,128]{3,2,1,0:T(4,128)S(1)} copy-done((f32[2,128,4,128]{3,2,1,0:T(4,128)S(1)}, f32[2,128,4,128]{3,2,1,0:T(4,128)}, u32[]{:S(2)}) %copy-start) | copy-done | bytes 524312
  3.2 1.3 %collective-permute-start.7 = (f32[512,128]{1,0:T(8,128)S(1)}, f32[512,128]{1,0:T(8,128)S(1)}, u32[]{:S(2)}, u32[]{:S(2)}) collective-permute-start(f32[512,128]{1,0:T(8,128)S(1)} %get-tuple-element.19), channel_id=1, source_target_pairs={{0,32},{1,33},{2,34},{3,35},{4,36},{5,37},{6,38},{7,39},{8,40},{9,... | collective-permute-start | bytes 786440 | tf_op jit(solution)/shard_map/ppermute | solution.py:25
  4.6 0.7 %collective-permute-start.13 = (f32[192,128]{1,0:T(8,128)S(1)}, f32[192,128]{1,0:T(8,128)S(1)}, u32[]{:S(2)}, u32[]{:S(2)}) collective-permute-start(f32[192,128]{1,0:T(8,128)S(1)} %pad_maximum_fusion), channel_id=1, source_target_pairs={{0,12},{1,13},{2,14},{3,15},{16,28},{17,29},{18,30},{19,31}} | collective-permute-start | bytes 294920 | tf_op jit(solution)/shard_map/ppermute | solution.py:25
  5.3 0.7 %collective-permute-start.14 = (f32[192,128]{1,0:T(8,128)S(1)}, f32[192,128]{1,0:T(8,128)S(1)}, u32[]{:S(2)}, u32[]{:S(2)}) collective-permute-start(f32[192,128]{1,0:T(8,128)S(1)} %pad_maximum_fusion), channel_id=1, source_target_pairs={{0,4},{1,5},{2,6},{3,7},{16,20},{17,21},{18,22},{19,23}} | collective-permute-start | bytes 294920 | tf_op jit(solution)/shard_map/ppermute | solution.py:25
  6.6 10.6 %collective-permute-done.7 = f32[512,128]{1,0:T(8,128)S(1)} collective-permute-done((f32[512,128]{1,0:T(8,128)S(1)}, f32[512,128]{1,0:T(8,128)S(1)}, u32[]{:S(2)}, u32[]{:S(2)}) %collective-permute-start.7) | collective-permute-done | bytes 262176 | tf_op jit(solution)/shard_map/ppermute | solution.py:25
  17.3 1.3 %collective-permute-start.8 = (f32[512,128]{1,0:T(8,128)S(1)}, f32[512,128]{1,0:T(8,128)S(1)}, u32[]{:S(2)}, u32[]{:S(2)}) collective-permute-start(f32[512,128]{1,0:T(8,128)S(1)} %broadcast_select_fusion), channel_id=1, source_target_pairs={{32,160},{33,161},{34,162},{35,163},{36,164},{37,165},{38,166},{39... | collective-permute-start | bytes 786440 | tf_op jit(solution)/shard_map/ppermute | solution.py:25
  18.7 1.3 %collective-permute-start.3 = (f32[256,128]{1,0:T(8,128)S(1)}, f32[256,128]{1,0:T(8,128)S(1)}, u32[]{:S(2)}, u32[]{:S(2)}) collective-permute-start(f32[256,128]{1,0:T(8,128)S(1)} %get-tuple-element.17), channel_id=1, source_target_pairs={{0,3},{1,2},{16,19},{17,18},{32,35},{33,34},{48,51},{49,50},{64,67... | collective-permute-start | bytes 393224 | tf_op jit(solution)/shard_map/ppermute | solution.py:25
  22.1 0.8 %collective-permute-done.8 = f32[512,128]{1,0:T(8,128)S(1)} collective-permute-done((f32[512,128]{1,0:T(8,128)S(1)}, f32[512,128]{1,0:T(8,128)S(1)}, u32[]{:S(2)}, u32[]{:S(2)}) %collective-permute-start.8) | collective-permute-done | bytes 262176 | tf_op jit(solution)/shard_map/ppermute | solution.py:25
  22.9 1.4 %collective-permute-start.9 = (f32[512,128]{1,0:T(8,128)S(1)}, f32[512,128]{1,0:T(8,128)S(1)}, u32[]{:S(2)}, u32[]{:S(2)}) collective-permute-start(f32[512,128]{1,0:T(8,128)S(1)} %broadcast_select_fusion.1), channel_id=1, source_target_pairs={{32,416},{33,417},{34,418},{35,419},{36,420},{37,421},{38,422},{39... | collective-permute-start | bytes 786440 | tf_op jit(solution)/shard_map/ppermute | solution.py:25
  24.3 3.7 %collective-permute-start.4 = (f32[256,128]{1,0:T(8,128)S(1)}, f32[256,128]{1,0:T(8,128)S(1)}, u32[]{:S(2)}, u32[]{:S(2)}) collective-permute-start(f32[256,128]{1,0:T(8,128)S(1)} %broadcast_select_fusion.3), channel_id=1, source_target_pairs={{0,8},{1,9},{2,10},{3,11},{16,24},{17,25},{18,26},{19,27},{32,40},... | collective-permute-start | bytes 393224 | tf_op jit(solution)/shard_map/ppermute | solution.py:25
  28.1 1.3 %collective-permute-start.19 = (f32[192,128]{1,0:T(8,128)S(1)}, f32[192,128]{1,0:T(8,128)S(1)}, u32[]{:S(2)}, u32[]{:S(2)}) collective-permute-start(f32[192,128]{1,0:T(8,128)S(1)} %select_select_fusion.2), channel_id=1, source_target_pairs={{0,480},{1,481},{2,482},{3,483},{4,484},{5,485},{6,486},{7,487},{8... | collective-permute-start | bytes 294920 | tf_op jit(solution)/shard_map/ppermute | solution.py:25
  29.4 0.7 %collective-permute-start.20 = (f32[192,128]{1,0:T(8,128)S(1)}, f32[192,128]{1,0:T(8,128)S(1)}, u32[]{:S(2)}, u32[]{:S(2)}) collective-permute-start(f32[192,128]{1,0:T(8,128)S(1)} %select_select_fusion.2), channel_id=1, source_target_pairs={{0,448},{1,449},{2,450},{3,451},{4,452},{5,453},{6,454},{7,455},{8... | collective-permute-start | bytes 294920 | tf_op jit(solution)/shard_map/ppermute | solution.py:25
  30.8 0.7 %collective-permute-start.10 = (f32[512,128]{1,0:T(8,128)S(1)}, f32[512,128]{1,0:T(8,128)S(1)}, u32[]{:S(2)}, u32[]{:S(2)}) collective-permute-start(f32[512,128]{1,0:T(8,128)S(1)} %broadcast_select_fusion.2), channel_id=1, source_target_pairs={{160,224},{161,225},{162,226},{163,227},{164,228},{165,229},{166,2... | collective-permute-start | bytes 786440 | tf_op jit(solution)/shard_map/ppermute | solution.py:25
  31.5 3.1 %collective-permute-done.19 = f32[192,128]{1,0:T(8,128)S(1)} collective-permute-done((f32[192,128]{1,0:T(8,128)S(1)}, f32[192,128]{1,0:T(8,128)S(1)}, u32[]{:S(2)}, u32[]{:S(2)}) %collective-permute-start.19) | collective-permute-done | bytes 98336 | tf_op jit(solution)/shard_map/ppermute | solution.py:25
  34.6 1.3 %collective-permute-start.11 = (f32[512,128]{1,0:T(8,128)S(1)}, f32[512,128]{1,0:T(8,128)S(1)}, u32[]{:S(2)}, u32[]{:S(2)}) collective-permute-start(f32[512,128]{1,0:T(8,128)S(1)} %broadcast_select_fusion.2), channel_id=1, source_target_pairs={{32,96},{33,97},{34,98},{35,99},{36,100},{37,101},{38,102},{39,103... | collective-permute-start | bytes 786440 | tf_op jit(solution)/shard_map/ppermute | solution.py:25
  36.0 5.8 %collective-permute-start.12 = (f32[512,128]{1,0:T(8,128)S(1)}, f32[512,128]{1,0:T(8,128)S(1)}, u32[]{:S(2)}, u32[]{:S(2)}) collective-permute-start(f32[512,128]{1,0:T(8,128)S(1)} %broadcast_select_fusion.2), channel_id=1, source_target_pairs={{32,64},{33,65},{34,66},{35,67},{36,68},{37,69},{38,70},{39,71},{4... | collective-permute-start | bytes 786440 | tf_op jit(solution)/shard_map/ppermute | solution.py:25
  41.8 1.9 %collective-permute-start.22 = (f32[192,128]{1,0:T(8,128)S(1)}, f32[192,128]{1,0:T(8,128)S(1)}, u32[]{:S(2)}, u32[]{:S(2)}) collective-permute-start(f32[192,128]{1,0:T(8,128)S(1)} %select_select_fusion.1.mine), channel_id=1, source_target_pairs={{0,16},{1,17},{2,18},{3,19},{4,20},{5,21},{6,22},{7,23},{8,24},{9,... | collective-permute-start | bytes 294920 | tf_op jit(solution)/shard_map/ppermute | solution.py:25
  43.7 2.3 %collective-permute-start.5 = (f32[256,128]{1,0:T(8,128)S(1)}, f32[256,128]{1,0:T(8,128)S(1)}, u32[]{:S(2)}, u32[]{:S(2)}) collective-permute-start(f32[256,128]{1,0:T(8,128)S(1)} %broadcast_select_fusion.4), channel_id=1, source_target_pairs={{0,4},{1,5},{2,6},{3,7},{8,12},{9,13},{10,14},{11,15},{16,20},{17,... | collective-permute-start | bytes 393224 | tf_op jit(solution)/shard_map/ppermute | solution.py:25
  46.0 3.2 %shard_map.18 = (f32[128,128]{1,0:T(8,128)S(1)}, f32[128,128]{1,0:T(8,128)S(1)}, f32[128,128]{1,0:T(8,128)S(1)}) custom-call(f32[192,128]{1,0:T(8,128)S(1)} %select_select_fusion.1.mine, f32[192,128]{1,0:T(8,128)S(1)} %collective-permute-done.22.other), custom_call_target="tpu_custom_call" | custom-call | tf_op jit(solution)/shard_map/pallas_call | solution.py:195
  49.3 2.1 %collective-permute-start.23 = (f32[512,128]{1,0:T(8,128)S(1)}, f32[512,128]{1,0:T(8,128)S(1)}, u32[]{:S(2)}, u32[]{:S(2)}) collective-permute-start(f32[512,128]{1,0:T(8,128)S(1)} %select_select_fusion.cols_a), channel_id=1, source_target_pairs={{0,16},{1,17},{2,18},{3,19},{4,20},{5,21},{6,22},{7,23},{8,24},{9,... | collective-permute-start | bytes 786440 | tf_op jit(solution)/shard_map/ppermute | solution.py:25
  51.5 1.9 %collective-permute-start.6 = (f32[256,128]{1,0:T(8,128)S(1)}, f32[256,128]{1,0:T(8,128)S(1)}, u32[]{:S(2)}, u32[]{:S(2)}) collective-permute-start(f32[256,128]{1,0:T(8,128)S(1)} %broadcast_select_fusion.5.rows_a), channel_id=1, source_target_pairs={{0,1},{1,0},{2,3},{3,2},{4,5},{5,4},{6,7},{7,6},{8,9},{9,8},{10,11... | collective-permute-start | bytes 393224 | tf_op jit(solution)/shard_map/ppermute | solution.py:25
  53.5 2.7 %shard_map.19.w1 = f32[128,128]{1,0:T(8,128)S(1)} custom-call(f32[128,128]{1,0:T(8,128)S(1)} %get-tuple-element.21.s11, f32[8,128]{1,0:T(8,128)S(1)} %slice.11.mark), custom_call_target="tpu_custom_call" | custom-call | flops 1000000000 | bytes 1000000000 | tf_op jit(solution)/shard_map/pallas_call | solution.py:195
  56.2 2.9 %collective-permute-done.6.rows_b = f32[256,128]{1,0:T(8,128)S(1)} collective-permute-done((f32[256,128]{1,0:T(8,128)S(1)}, f32[256,128]{1,0:T(8,128)S(1)}, u32[]{:S(2)}, u32[]{:S(2)}) %collective-permute-start.6) | collective-permute-done | bytes 131104 | tf_op jit(solution)/shard_map/ppermute | solution.py:25
  59.1 3.1 %shard_map.20 = f32[1024,128]{1,0:T(8,128)} custom-call(f32[1024,128]{1,0:T(8,128)S(1)} %bitcast.3, f32[256,128]{1,0:T(8,128)S(1)} %broadcast_select_fusion.5.rows_a, f32[256,128]{1,0:T(8,128)S(1)} %collective-permute-done.6.rows_b, f32[512,128]{1,0:T(8,128)S(1)} %select_select_fusion.cols_a, f32[512,128]{1,0:T(8,128)S(1)} %collective-permute-done.23.cols_b, ...), custom_call_target="tpu_custom_call" | custom-call | tf_op jit(solution)/shard_map/pallas_call | solution.py:195
  (46 shorter events, 5.8 us)
Async XLA Ops:
  1.2 3.3 %collective-permute-start = (f32[128,128]{1,0:T(8,128)S(1)}, f32[128,128]{1,0:T(8,128)S(1)}, u32[]{:S(2)}, u32[]{:S(2)}) collective-permute-start(f32[128,128]{1,0:T(8,128)S(1)} %get-tuple-element.16), channel_id=1, source_target_pairs={{0,1},{1,0},{16,17},{17,16}} | collective-permute-start | bytes 196616 | tf_op jit(solution)/shard_map/ppermute | solution.py:25
  1.8 2.7 %collective-permute-start.2 = (f32[128,128]{1,0:T(8,128)S(1)}, f32[128,128]{1,0:T(8,128)S(1)}, u32[]{:S(2)}, u32[]{:S(2)}) collective-permute-start(f32[128,128]{1,0:T(8,128)S(1)} %get-tuple-element.16), channel_id=1, source_target_pairs={{0,2},{1,3},{16,18},{17,19}} | collective-permute-start | bytes 196616 | tf_op jit(solution)/shard_map/ppermute | solution.py:25
  2.5 2.0 %collective-permute-start.1 = (f32[128,128]{1,0:T(8,128)S(1)}, f32[128,128]{1,0:T(8,128)S(1)}, u32[]{:S(2)}, u32[]{:S(2)}) collective-permute-start(f32[128,128]{1,0:T(8,128)S(1)} %get-tuple-element.16), channel_id=1, source_target_pairs={{0,3},{1,2},{16,19},{17,18}} | collective-permute-start | bytes 196616 | tf_op jit(solution)/shard_map/ppermute | solution.py:25
  3.2 14.1 %collective-permute-start.7 = (f32[512,128]{1,0:T(8,128)S(1)}, f32[512,128]{1,0:T(8,128)S(1)}, u32[]{:S(2)}, u32[]{:S(2)}) collective-permute-start(f32[512,128]{1,0:T(8,128)S(1)} %get-tuple-element.19), channel_id=1, source_target_pairs={{0,32},{1,33},{2,34},{3,35},{4,36},{5,37},{6,38},{7,39},{8,40},{9,... | collective-permute-start | bytes 786440 | tf_op jit(solution)/shard_map/ppermute | solution.py:25
  4.6 15.4 %collective-permute-start.13 = (f32[192,128]{1,0:T(8,128)S(1)}, f32[192,128]{1,0:T(8,128)S(1)}, u32[]{:S(2)}, u32[]{:S(2)}) collective-permute-start(f32[192,128]{1,0:T(8,128)S(1)} %pad_maximum_fusion), channel_id=1, source_target_pairs={{0,12},{1,13},{2,14},{3,15},{16,28},{17,29},{18,30},{19,31}} | collective-permute-start | bytes 294920 | tf_op jit(solution)/shard_map/ppermute | solution.py:25
  5.3 14.7 %collective-permute-start.14 = (f32[192,128]{1,0:T(8,128)S(1)}, f32[192,128]{1,0:T(8,128)S(1)}, u32[]{:S(2)}, u32[]{:S(2)}) collective-permute-start(f32[192,128]{1,0:T(8,128)S(1)} %pad_maximum_fusion), channel_id=1, source_target_pairs={{0,4},{1,5},{2,6},{3,7},{16,20},{17,21},{18,22},{19,23}} | collective-permute-start | bytes 294920 | tf_op jit(solution)/shard_map/ppermute | solution.py:25
  5.9 14.1 %collective-permute-start.15 = (f32[192,128]{1,0:T(8,128)S(1)}, f32[192,128]{1,0:T(8,128)S(1)}, u32[]{:S(2)}, u32[]{:S(2)}) collective-permute-start(f32[192,128]{1,0:T(8,128)S(1)} %pad_maximum_fusion), channel_id=1, source_target_pairs={{0,8},{1,9},{2,10},{3,11},{16,24},{17,25},{18,26},{19,27}} | collective-permute-start | bytes 294920 | tf_op jit(solution)/shard_map/ppermute | solution.py:25
  17.3 5.6 %collective-permute-start.8 = (f32[512,128]{1,0:T(8,128)S(1)}, f32[512,128]{1,0:T(8,128)S(1)}, u32[]{:S(2)}, u32[]{:S(2)}) collective-permute-start(f32[512,128]{1,0:T(8,128)S(1)} %broadcast_select_fusion), channel_id=1, source_target_pairs={{32,160},{33,161},{34,162},{35,163},{36,164},{37,165},{38,166},{39... | collective-permute-start | bytes 786440 | tf_op jit(solution)/shard_map/ppermute | solution.py:25
  18.7 5.6 %collective-permute-start.3 = (f32[256,128]{1,0:T(8,128)S(1)}, f32[256,128]{1,0:T(8,128)S(1)}, u32[]{:S(2)}, u32[]{:S(2)}) collective-permute-start(f32[256,128]{1,0:T(8,128)S(1)} %get-tuple-element.17), channel_id=1, source_target_pairs={{0,3},{1,2},{16,19},{17,18},{32,35},{33,34},{48,51},{49,50},{64,67... | collective-permute-start | bytes 393224 | tf_op jit(solution)/shard_map/ppermute | solution.py:25
  20.0 8.0 %collective-permute-start.16 = (f32[192,128]{1,0:T(8,128)S(1)}, f32[192,128]{1,0:T(8,128)S(1)}, u32[]{:S(2)}, u32[]{:S(2)}) collective-permute-start(f32[192,128]{1,0:T(8,128)S(1)} %select_select_fusion.3), channel_id=1, source_target_pairs={{0,64},{1,65},{2,66},{3,67},{4,68},{5,69},{6,70},{7,71},{8,72},{9,... | collective-permute-start | bytes 294920 | tf_op jit(solution)/shard_map/ppermute | solution.py:25
  20.7 7.4 %collective-permute-start.17 = (f32[192,128]{1,0:T(8,128)S(1)}, f32[192,128]{1,0:T(8,128)S(1)}, u32[]{:S(2)}, u32[]{:S(2)}) collective-permute-start(f32[192,128]{1,0:T(8,128)S(1)} %select_select_fusion.3), channel_id=1, source_target_pairs={{0,384},{1,385},{2,386},{3,387},{4,388},{5,389},{6,390},{7,391},{8... | collective-permute-start | bytes 294920 | tf_op jit(solution)/shard_map/ppermute | solution.py:25
  21.4 6.7 %collective-permute-start.18 = (f32[192,128]{1,0:T(8,128)S(1)}, f32[192,128]{1,0:T(8,128)S(1)}, u32[]{:S(2)}, u32[]{:S(2)}) collective-permute-start(f32[192,128]{1,0:T(8,128)S(1)} %select_select_fusion.3), channel_id=1, source_target_pairs={{0,128},{1,129},{2,130},{3,131},{4,132},{5,133},{6,134},{7,135},{8... | collective-permute-start | bytes 294920 | tf_op jit(solution)/shard_map/ppermute | solution.py:25
  22.9 7.9 %collective-permute-start.9 = (f32[512,128]{1,0:T(8,128)S(1)}, f32[512,128]{1,0:T(8,128)S(1)}, u32[]{:S(2)}, u32[]{:S(2)}) collective-permute-start(f32[512,128]{1,0:T(8,128)S(1)} %broadcast_select_fusion.1), channel_id=1, source_target_pairs={{32,416},{33,417},{34,418},{35,419},{36,420},{37,421},{38,422},{39... | collective-permute-start | bytes 786440 | tf_op jit(solution)/shard_map/ppermute | solution.py:25
  24.3 19.4 %collective-permute-start.4 = (f32[256,128]{1,0:T(8,128)S(1)}, f32[256,128]{1,0:T(8,128)S(1)}, u32[]{:S(2)}, u32[]{:S(2)}) collective-permute-start(f32[256,128]{1,0:T(8,128)S(1)} %broadcast_select_fusion.3), channel_id=1, source_target_pairs={{0,8},{1,9},{2,10},{3,11},{16,24},{17,25},{18,26},{19,27},{32,40},... | collective-permute-start | bytes 393224 | tf_op jit(solution)/shard_map/ppermute | solution.py:25
  28.1 6.5 %collective-permute-start.19 = (f32[192,128]{1,0:T(8,128)S(1)}, f32[192,128]{1,0:T(8,128)S(1)}, u32[]{:S(2)}, u32[]{:S(2)}) collective-permute-start(f32[192,128]{1,0:T(8,128)S(1)} %select_select_fusion.2), channel_id=1, source_target_pairs={{0,480},{1,481},{2,482},{3,483},{4,484},{5,485},{6,486},{7,487},{8... | collective-permute-start | bytes 294920 | tf_op jit(solution)/shard_map/ppermute | solution.py:25
  29.4 6.5 %collective-permute-start.20 = (f32[192,128]{1,0:T(8,128)S(1)}, f32[192,128]{1,0:T(8,128)S(1)}, u32[]{:S(2)}, u32[]{:S(2)}) collective-permute-start(f32[192,128]{1,0:T(8,128)S(1)} %select_select_fusion.2), channel_id=1, source_target_pairs={{0,448},{1,449},{2,450},{3,451},{4,452},{5,453},{6,454},{7,455},{8... | collective-permute-start | bytes 294920 | tf_op jit(solution)/shard_map/ppermute | solution.py:25
  30.1 11.6 %collective-permute-start.21 = (f32[192,128]{1,0:T(8,128)S(1)}, f32[192,128]{1,0:T(8,128)S(1)}, u32[]{:S(2)}, u32[]{:S(2)}) collective-permute-start(f32[192,128]{1,0:T(8,128)S(1)} %select_select_fusion.2), channel_id=1, source_target_pairs={{0,416},{1,417},{2,418},{3,419},{4,420},{5,421},{6,422},{7,423},{8... | collective-permute-start | bytes 294920 | tf_op jit(solution)/shard_map/ppermute | solution.py:25
  30.8 18.4 %collective-permute-start.10 = (f32[512,128]{1,0:T(8,128)S(1)}, f32[512,128]{1,0:T(8,128)S(1)}, u32[]{:S(2)}, u32[]{:S(2)}) collective-permute-start(f32[512,128]{1,0:T(8,128)S(1)} %broadcast_select_fusion.2), channel_id=1, source_target_pairs={{160,224},{161,225},{162,226},{163,227},{164,228},{165,229},{166,2... | collective-permute-start | bytes 786440 | tf_op jit(solution)/shard_map/ppermute | solution.py:25
  34.6 14.6 %collective-permute-start.11 = (f32[512,128]{1,0:T(8,128)S(1)}, f32[512,128]{1,0:T(8,128)S(1)}, u32[]{:S(2)}, u32[]{:S(2)}) collective-permute-start(f32[512,128]{1,0:T(8,128)S(1)} %broadcast_select_fusion.2), channel_id=1, source_target_pairs={{32,96},{33,97},{34,98},{35,99},{36,100},{37,101},{38,102},{39,103... | collective-permute-start | bytes 786440 | tf_op jit(solution)/shard_map/ppermute | solution.py:25
  36.0 13.3 %collective-permute-start.12 = (f32[512,128]{1,0:T(8,128)S(1)}, f32[512,128]{1,0:T(8,128)S(1)}, u32[]{:S(2)}, u32[]{:S(2)}) collective-permute-start(f32[512,128]{1,0:T(8,128)S(1)} %broadcast_select_fusion.2), channel_id=1, source_target_pairs={{32,64},{33,65},{34,66},{35,67},{36,68},{37,69},{38,70},{39,71},{4... | collective-permute-start | bytes 786440 | tf_op jit(solution)/shard_map/ppermute | solution.py:25
  41.8 4.3 %collective-permute-start.22 = (f32[192,128]{1,0:T(8,128)S(1)}, f32[192,128]{1,0:T(8,128)S(1)}, u32[]{:S(2)}, u32[]{:S(2)}) collective-permute-start(f32[192,128]{1,0:T(8,128)S(1)} %select_select_fusion.1.mine), channel_id=1, source_target_pairs={{0,16},{1,17},{2,18},{3,19},{4,20},{5,21},{6,22},{7,23},{8,24},{9,... | collective-permute-start | bytes 294920 | tf_op jit(solution)/shard_map/ppermute | solution.py:25
  43.7 7.8 %collective-permute-start.5 = (f32[256,128]{1,0:T(8,128)S(1)}, f32[256,128]{1,0:T(8,128)S(1)}, u32[]{:S(2)}, u32[]{:S(2)}) collective-permute-start(f32[256,128]{1,0:T(8,128)S(1)} %broadcast_select_fusion.4), channel_id=1, source_target_pairs={{0,4},{1,5},{2,6},{3,7},{8,12},{9,13},{10,14},{11,15},{16,20},{17,... | collective-permute-start | bytes 393224 | tf_op jit(solution)/shard_map/ppermute | solution.py:25
  49.3 9.8 %collective-permute-start.23 = (f32[512,128]{1,0:T(8,128)S(1)}, f32[512,128]{1,0:T(8,128)S(1)}, u32[]{:S(2)}, u32[]{:S(2)}) collective-permute-start(f32[512,128]{1,0:T(8,128)S(1)} %select_select_fusion.cols_a), channel_id=1, source_target_pairs={{0,16},{1,17},{2,18},{3,19},{4,20},{5,21},{6,22},{7,23},{8,24},{9,... | collective-permute-start | bytes 786440 | tf_op jit(solution)/shard_map/ppermute | solution.py:25
  51.5 7.6 %collective-permute-start.6 = (f32[256,128]{1,0:T(8,128)S(1)}, f32[256,128]{1,0:T(8,128)S(1)}, u32[]{:S(2)}, u32[]{:S(2)}) collective-permute-start(f32[256,128]{1,0:T(8,128)S(1)} %broadcast_select_fusion.5.rows_a), channel_id=1, source_target_pairs={{0,1},{1,0},{2,3},{3,2},{4,5},{5,4},{6,7},{7,6},{8,9},{9,8},{10,11... | collective-permute-start | bytes 393224 | tf_op jit(solution)/shard_map/ppermute | solution.py:25
  (2 other events, 6.7 us)

commit v6 on v5

--- a/solution.py
+++ b/solution.py
@@ -259,8 +259,8 @@
         return [along_z(value, each) for each in sends]
 
     r3 = move(tile, [((c, a), (c, b)) for c in cores for a, b in ((0, 1), (1, 0))])
+    r2 = move(tile, [((c, a), (c, b)) for c in cores for a, b in ((0, 3), (1, 2))])
     r1 = move(tile, [((c, a), (c, b)) for c in cores for a, b in ((0, 2), (1, 3))])
-    r2 = move(tile, [((c, a), (c, b)) for c in cores for a, b in ((0, 3), (1, 2))])
     for sends in ([(0, 1)], [(1, 5)]):
         cols = take(cols, z, lift(cols, [sends]), [sends])
     c_sends = [[(1, 13), (5, 9)]]
@@ -275,7 +275,7 @@
         axis=0,
     )
 
-    got = [move(diag, [((c, a), (c, b)) for c in cores for a, b in along_x(0, d)]) for d in (2, 1, 3)]
+    got = [move(diag, [((c, a), (c, b)) for c in cores for a, b in along_x(0, d)]) for d in (3, 1, 2)]
     cols = take(cols, z, c_got, c_sends)
     cols = tied((cols, diag))[0]
     q_sends = [[(1, 2), (5, 4), (13, 12), (9, 8)]]
@@ -283,10 +283,10 @@
     r_got = in_row(tied((rows, diag))[0], [(0, 3), (1, 2)])
     rows = jnp.where((y >= 2) & (x == 0), r_got, rows)
     far = in_row(tied((rows, diag))[0], along_x(0, 2))
-    diag = take(diag, x, got, [[(0, 2)], [(0, 1)], [(0, 3)]])
+    diag = take(diag, x, got, [[(0, 3)], [(0, 1)], [(0, 2)]])
     diag, mark = tied((diag, token(diag, diag, r_got)))
 
-    d_sends = [[(0, 4)], [(0, 12)], [(0, 2)]]
+    d_sends = [[(0, 4)], [(0, 2)], [(0, 12)]]
     got = lift(diag, d_sends)
     rows = jnp.where(x == 2, far, rows)
     r_got = in_row(tied((rows, mark))[0], along_x(0, 1) + along_x(2, 3))
@@ -295,11 +295,11 @@
 
     d_sends = [
         [(0, 13), (2, 5), (4, 8), (12, 9)],
+        [(0, 15), (2, 1), (4, 6), (12, 11)],
         [(0, 14), (2, 3), (4, 7), (12, 10)],
-        [(0, 15), (2, 1), (4, 6), (12, 11)],
     ]
     got = lift(diag, d_sends)
-    late_sends = [[(1, 3), (5, 6), (9, 10), (13, 14)], [(5, 7), (9, 11), (13, 15)]]
+    late_sends = [[(5, 7), (9, 11), (13, 15)], [(1, 3), (5, 6), (9, 10), (13, 14)]]
     late_got = [along_z(tied((cols, mark))[0], each) for each in late_sends]
     diag = take(diag, z, got, d_sends)
     diag, mark = tied((diag, token(diag, mark, *late_got)))

time: 62.7 us -> 63.1 us (level)
  the two profiles are of different devices: /device:TPU:40 before, /device:TPU:32 now
where the time goes in v6:
time: 63.1 us; the launch traced here: 62.6 us
  starting transfers between devices  34.7 us (55%)
  waiting for transfers between devices  16.9 us (27%)
  Pallas kernels  9.08 us (14%)
  local copies, waits for them, and re-layouts  1.05 us (2%)
    ppermute x24, starting transfers between devices, move(): return lax.ppermute(value, ('row', 'col'), flat)  34.7 us
    ppermute x24, waiting for transfers between devices, move(): return lax.ppermute(value, ('row', 'col'), flat)  16.9 us
    pallas_call x4, Pallas kernels, call(): pl.pallas_call(body, out_shape=shapes, in_specs=[VMEM] * len(args), out_s...  9.08 us
  transfers between devices with their start and end apart: 24, of which 4 were waited for; matrix products, arithmetic and copies ran while one was open for 0% of the time, Pallas kernels for 9%

profile of v6, /device:TPU:32, one launch (start us, length us, event | category | flops | bytes accessed | tf_op | source)
XLA Modules:
  0.0 62.6 jit_solution(16062139687867870470)
XLA Ops:
  0.0 1.0 %copy-done = f32[2,128,4,128]{3,2,1,0:T(4,128)S(1)} copy-done((f32[2,128,4,128]{3,2,1,0:T(4,128)S(1)}, f32[2,128,4,128]{3,2,1,0:T(4,128)}, u32[]{:S(2)}) %copy-start) | copy-done | bytes 524312
  3.2 1.3 %collective-permute-start.7 = (f32[512,128]{1,0:T(8,128)S(1)}, f32[512,128]{1,0:T(8,128)S(1)}, u32[]{:S(2)}, u32[]{:S(2)}) collective-permute-start(f32[512,128]{1,0:T(8,128)S(1)} %get-tuple-element.19), channel_id=1, source_target_pairs={{0,32},{1,33},{2,34},{3,35},{4,36},{5,37},{6,38},{7,39},{8,40},{9,... | collective-permute-start | bytes 786440 | tf_op jit(solution)/shard_map/ppermute | solution.py:25
  4.6 0.7 %collective-permute-start.13 = (f32[192,128]{1,0:T(8,128)S(1)}, f32[192,128]{1,0:T(8,128)S(1)}, u32[]{:S(2)}, u32[]{:S(2)}) collective-permute-start(f32[192,128]{1,0:T(8,128)S(1)} %pad_maximum_fusion), channel_id=1, source_target_pairs={{0,8},{1,9},{2,10},{3,11},{16,24},{17,25},{18,26},{19,27}} | collective-permute-start | bytes 294920 | tf_op jit(solution)/shard_map/ppermute | solution.py:25
  5.3 0.7 %collective-permute-start.14 = (f32[192,128]{1,0:T(8,128)S(1)}, f32[192,128]{1,0:T(8,128)S(1)}, u32[]{:S(2)}, u32[]{:S(2)}) collective-permute-start(f32[192,128]{1,0:T(8,128)S(1)} %pad_maximum_fusion), channel_id=1, source_target_pairs={{0,4},{1,5},{2,6},{3,7},{16,20},{17,21},{18,22},{19,23}} | collective-permute-start | bytes 294920 | tf_op jit(solution)/shard_map/ppermute | solution.py:25
  5.9 0.7 %collective-permute-start.15 = (f32[192,128]{1,0:T(8,128)S(1)}, f32[192,128]{1,0:T(8,128)S(1)}, u32[]{:S(2)}, u32[]{:S(2)}) collective-permute-start(f32[192,128]{1,0:T(8,128)S(1)} %pad_maximum_fusion), channel_id=1, source_target_pairs={{0,12},{1,13},{2,14},{3,15},{16,28},{17,29},{18,30},{19,31}} | collective-permute-start | bytes 294920 | tf_op jit(solution)/shard_map/ppermute | solution.py:25
  6.6 10.2 %collective-permute-done.7 = f32[512,128]{1,0:T(8,128)S(1)} collective-permute-done((f32[512,128]{1,0:T(8,128)S(1)}, f32[512,128]{1,0:T(8,128)S(1)}, u32[]{:S(2)}, u32[]{:S(2)}) %collective-permute-start.7) | collective-permute-done | bytes 262176 | tf_op jit(solution)/shard_map/ppermute | solution.py:25
  16.8 1.3 %collective-permute-start.8 = (f32[512,128]{1,0:T(8,128)S(1)}, f32[512,128]{1,0:T(8,128)S(1)}, u32[]{:S(2)}, u32[]{:S(2)}) collective-permute-start(f32[512,128]{1,0:T(8,128)S(1)} %broadcast_select_fusion), channel_id=1, source_target_pairs={{32,160},{33,161},{34,162},{35,163},{36,164},{37,165},{38,166},{39... | collective-permute-start | bytes 786440 | tf_op jit(solution)/shard_map/ppermute | solution.py:25
  18.2 1.9 %collective-permute-start.3 = (f32[256,128]{1,0:T(8,128)S(1)}, f32[256,128]{1,0:T(8,128)S(1)}, u32[]{:S(2)}, u32[]{:S(2)}) collective-permute-start(f32[256,128]{1,0:T(8,128)S(1)} %get-tuple-element.17), channel_id=1, source_target_pairs={{0,3},{1,2},{16,19},{17,18},{32,35},{33,34},{48,51},{49,50},{64,67... | collective-permute-start | bytes 393224 | tf_op jit(solution)/shard_map/ppermute | solution.py:25
  22.3 3.4 %collective-permute-start.9 = (f32[512,128]{1,0:T(8,128)S(1)}, f32[512,128]{1,0:T(8,128)S(1)}, u32[]{:S(2)}, u32[]{:S(2)}) collective-permute-start(f32[512,128]{1,0:T(8,128)S(1)} %broadcast_select_fusion.1), channel_id=1, source_target_pairs={{32,416},{33,417},{34,418},{35,419},{36,420},{37,421},{38,422},{39... | collective-permute-start | bytes 786440 | tf_op jit(solution)/shard_map/ppermute | solution.py:25
  25.8 1.3 %collective-permute-start.4 = (f32[256,128]{1,0:T(8,128)S(1)}, f32[256,128]{1,0:T(8,128)S(1)}, u32[]{:S(2)}, u32[]{:S(2)}) collective-permute-start(f32[256,128]{1,0:T(8,128)S(1)} %broadcast_select_fusion.3), channel_id=1, source_target_pairs={{0,8},{1,9},{2,10},{3,11},{16,24},{17,25},{18,26},{19,27},{32,40},... | collective-permute-start | bytes 393224 | tf_op jit(solution)/shard_map/ppermute | solution.py:25
  27.8 1.3 %collective-permute-start.20 = (f32[192,128]{1,0:T(8,128)S(1)}, f32[192,128]{1,0:T(8,128)S(1)}, u32[]{:S(2)}, u32[]{:S(2)}) collective-permute-start(f32[192,128]{1,0:T(8,128)S(1)} %select_select_fusion.2), channel_id=1, source_target_pairs={{0,480},{1,481},{2,482},{3,483},{4,484},{5,485},{6,486},{7,487},{8... | collective-permute-start | bytes 294920 | tf_op jit(solution)/shard_map/ppermute | solution.py:25
  29.8 1.2 %collective-permute-done.9 = f32[512,128]{1,0:T(8,128)S(1)} collective-permute-done((f32[512,128]{1,0:T(8,128)S(1)}, f32[512,128]{1,0:T(8,128)S(1)}, u32[]{:S(2)}, u32[]{:S(2)}) %collective-permute-start.9) | collective-permute-done | bytes 262176 | tf_op jit(solution)/shard_map/ppermute | solution.py:25
  31.1 1.3 %collective-permute-start.10 = (f32[512,128]{1,0:T(8,128)S(1)}, f32[512,128]{1,0:T(8,128)S(1)}, u32[]{:S(2)}, u32[]{:S(2)}) collective-permute-start(f32[512,128]{1,0:T(8,128)S(1)} %broadcast_select_fusion.2), channel_id=1, source_target_pairs={{32,96},{33,97},{34,98},{35,99},{36,100},{37,101},{38,102},{39,103... | collective-permute-start | bytes 786440 | tf_op jit(solution)/shard_map/ppermute | solution.py:25
  32.4 0.7 %collective-permute-start.11 = (f32[512,128]{1,0:T(8,128)S(1)}, f32[512,128]{1,0:T(8,128)S(1)}, u32[]{:S(2)}, u32[]{:S(2)}) collective-permute-start(f32[512,128]{1,0:T(8,128)S(1)} %broadcast_select_fusion.2), channel_id=1, source_target_pairs={{160,224},{161,225},{162,226},{163,227},{164,228},{165,229},{166,2... | collective-permute-start | bytes 786440 | tf_op jit(solution)/shard_map/ppermute | solution.py:25
  33.1 3.1 %collective-permute-done.20 = f32[192,128]{1,0:T(8,128)S(1)} collective-permute-done((f32[192,128]{1,0:T(8,128)S(1)}, f32[192,128]{1,0:T(8,128)S(1)}, u32[]{:S(2)}, u32[]{:S(2)}) %collective-permute-start.20) | collective-permute-done | bytes 98336 | tf_op jit(solution)/shard_map/ppermute | solution.py:25
  36.1 7.0 %collective-permute-start.12 = (f32[512,128]{1,0:T(8,128)S(1)}, f32[512,128]{1,0:T(8,128)S(1)}, u32[]{:S(2)}, u32[]{:S(2)}) collective-permute-start(f32[512,128]{1,0:T(8,128)S(1)} %broadcast_select_fusion.2), channel_id=1, source_target_pairs={{32,64},{33,65},{34,66},{35,67},{36,68},{37,69},{38,70},{39,71},{4... | collective-permute-start | bytes 786440 | tf_op jit(solution)/shard_map/ppermute | solution.py:25
  43.2 1.9 %collective-permute-start.22 = (f32[192,128]{1,0:T(8,128)S(1)}, f32[192,128]{1,0:T(8,128)S(1)}, u32[]{:S(2)}, u32[]{:S(2)}) collective-permute-start(f32[192,128]{1,0:T(8,128)S(1)} %select_select_fusion.1.mine), channel_id=1, source_target_pairs={{0,16},{1,17},{2,18},{3,19},{4,20},{5,21},{6,22},{7,23},{8,24},{9,... | collective-permute-start | bytes 294920 | tf_op jit(solution)/shard_map/ppermute | solution.py:25
  45.1 1.3 %collective-permute-start.5 = (f32[256,128]{1,0:T(8,128)S(1)}, f32[256,128]{1,0:T(8,128)S(1)}, u32[]{:S(2)}, u32[]{:S(2)}) collective-permute-start(f32[256,128]{1,0:T(8,128)S(1)} %broadcast_select_fusion.4), channel_id=1, source_target_pairs={{0,4},{1,5},{2,6},{3,7},{8,12},{9,13},{10,14},{11,15},{16,20},{17,... | collective-permute-start | bytes 393224 | tf_op jit(solution)/shard_map/ppermute | solution.py:25
  46.5 3.2 %shard_map.18 = (f32[128,128]{1,0:T(8,128)S(1)}, f32[128,128]{1,0:T(8,128)S(1)}, f32[128,128]{1,0:T(8,128)S(1)}) custom-call(f32[192,128]{1,0:T(8,128)S(1)} %select_select_fusion.1.mine, f32[192,128]{1,0:T(8,128)S(1)} %collective-permute-done.22.other), custom_call_target="tpu_custom_call" | custom-call | tf_op jit(solution)/shard_map/pallas_call | solution.py:195
  49.8 2.4 %collective-permute-start.23 = (f32[512,128]{1,0:T(8,128)S(1)}, f32[512,128]{1,0:T(8,128)S(1)}, u32[]{:S(2)}, u32[]{:S(2)}) collective-permute-start(f32[512,128]{1,0:T(8,128)S(1)} %select_select_fusion.cols_a), channel_id=1, source_target_pairs={{0,16},{1,17},{2,18},{3,19},{4,20},{5,21},{6,22},{7,23},{8,24},{9,... | collective-permute-start | bytes 786440 | tf_op jit(solution)/shard_map/ppermute | solution.py:25
  52.2 2.2 %collective-permute-start.6 = (f32[256,128]{1,0:T(8,128)S(1)}, f32[256,128]{1,0:T(8,128)S(1)}, u32[]{:S(2)}, u32[]{:S(2)}) collective-permute-start(f32[256,128]{1,0:T(8,128)S(1)} %broadcast_select_fusion.5.rows_a), channel_id=1, source_target_pairs={{0,1},{1,0},{2,3},{3,2},{4,5},{5,4},{6,7},{7,6},{8,9},{9,8},{10,11... | collective-permute-start | bytes 393224 | tf_op jit(solution)/shard_map/ppermute | solution.py:25
  54.5 2.7 %shard_map.19.w1 = f32[128,128]{1,0:T(8,128)S(1)} custom-call(f32[128,128]{1,0:T(8,128)S(1)} %get-tuple-element.21.s11, f32[8,128]{1,0:T(8,128)S(1)} %slice.11.mark), custom_call_target="tpu_custom_call" | custom-call | flops 1000000000 | bytes 1000000000 | tf_op jit(solution)/shard_map/pallas_call | solution.py:195
  57.2 2.3 %collective-permute-done.6.rows_b = f32[256,128]{1,0:T(8,128)S(1)} collective-permute-done((f32[256,128]{1,0:T(8,128)S(1)}, f32[256,128]{1,0:T(8,128)S(1)}, u32[]{:S(2)}, u32[]{:S(2)}) %collective-permute-start.6) | collective-permute-done | bytes 131104 | tf_op jit(solution)/shard_map/ppermute | solution.py:25
  59.5 3.1 %shard_map.20 = f32[1024,128]{1,0:T(8,128)} custom-call(f32[1024,128]{1,0:T(8,128)S(1)} %bitcast.3, f32[256,128]{1,0:T(8,128)S(1)} %broadcast_select_fusion.5.rows_a, f32[256,128]{1,0:T(8,128)S(1)} %collective-permute-done.6.rows_b, f32[512,128]{1,0:T(8,128)S(1)} %select_select_fusion.cols_a, f32[512,128]{1,0:T(8,128)S(1)} %collective-permute-done.23.cols_b, ...), custom_call_target="tpu_custom_call" | custom-call | tf_op jit(solution)/shard_map/pallas_call | solution.py:195
  (46 shorter events, 5.8 us)
Async XLA Ops:
  1.2 3.3 %collective-permute-start = (f32[128,128]{1,0:T(8,128)S(1)}, f32[128,128]{1,0:T(8,128)S(1)}, u32[]{:S(2)}, u32[]{:S(2)}) collective-permute-start(f32[128,128]{1,0:T(8,128)S(1)} %get-tuple-element.16), channel_id=1, source_target_pairs={{0,1},{1,0},{16,17},{17,16}} | collective-permute-start | bytes 196616 | tf_op jit(solution)/shard_map/ppermute | solution.py:25
  1.8 2.7 %collective-permute-start.2 = (f32[128,128]{1,0:T(8,128)S(1)}, f32[128,128]{1,0:T(8,128)S(1)}, u32[]{:S(2)}, u32[]{:S(2)}) collective-permute-start(f32[128,128]{1,0:T(8,128)S(1)} %get-tuple-element.16), channel_id=1, source_target_pairs={{0,2},{1,3},{16,18},{17,19}} | collective-permute-start | bytes 196616 | tf_op jit(solution)/shard_map/ppermute | solution.py:25
  2.5 2.0 %collective-permute-start.1 = (f32[128,128]{1,0:T(8,128)S(1)}, f32[128,128]{1,0:T(8,128)S(1)}, u32[]{:S(2)}, u32[]{:S(2)}) collective-permute-start(f32[128,128]{1,0:T(8,128)S(1)} %get-tuple-element.16), channel_id=1, source_target_pairs={{0,3},{1,2},{16,19},{17,18}} | collective-permute-start | bytes 196616 | tf_op jit(solution)/shard_map/ppermute | solution.py:25
  3.2 13.6 %collective-permute-start.7 = (f32[512,128]{1,0:T(8,128)S(1)}, f32[512,128]{1,0:T(8,128)S(1)}, u32[]{:S(2)}, u32[]{:S(2)}) collective-permute-start(f32[512,128]{1,0:T(8,128)S(1)} %get-tuple-element.19), channel_id=1, source_target_pairs={{0,32},{1,33},{2,34},{3,35},{4,36},{5,37},{6,38},{7,39},{8,40},{9,... | collective-permute-start | bytes 786440 | tf_op jit(solution)/shard_map/ppermute | solution.py:25
  4.6 15.6 %collective-permute-start.13 = (f32[192,128]{1,0:T(8,128)S(1)}, f32[192,128]{1,0:T(8,128)S(1)}, u32[]{:S(2)}, u32[]{:S(2)}) collective-permute-start(f32[192,128]{1,0:T(8,128)S(1)} %pad_maximum_fusion), channel_id=1, source_target_pairs={{0,8},{1,9},{2,10},{3,11},{16,24},{17,25},{18,26},{19,27}} | collective-permute-start | bytes 294920 | tf_op jit(solution)/shard_map/ppermute | solution.py:25
  5.3 14.9 %collective-permute-start.14 = (f32[192,128]{1,0:T(8,128)S(1)}, f32[192,128]{1,0:T(8,128)S(1)}, u32[]{:S(2)}, u32[]{:S(2)}) collective-permute-start(f32[192,128]{1,0:T(8,128)S(1)} %pad_maximum_fusion), channel_id=1, source_target_pairs={{0,4},{1,5},{2,6},{3,7},{16,20},{17,21},{18,22},{19,23}} | collective-permute-start | bytes 294920 | tf_op jit(solution)/shard_map/ppermute | solution.py:25
  5.9 14.3 %collective-permute-start.15 = (f32[192,128]{1,0:T(8,128)S(1)}, f32[192,128]{1,0:T(8,128)S(1)}, u32[]{:S(2)}, u32[]{:S(2)}) collective-permute-start(f32[192,128]{1,0:T(8,128)S(1)} %pad_maximum_fusion), channel_id=1, source_target_pairs={{0,12},{1,13},{2,14},{3,15},{16,28},{17,29},{18,30},{19,31}} | collective-permute-start | bytes 294920 | tf_op jit(solution)/shard_map/ppermute | solution.py:25
  16.8 5.4 %collective-permute-start.8 = (f32[512,128]{1,0:T(8,128)S(1)}, f32[512,128]{1,0:T(8,128)S(1)}, u32[]{:S(2)}, u32[]{:S(2)}) collective-permute-start(f32[512,128]{1,0:T(8,128)S(1)} %broadcast_select_fusion), channel_id=1, source_target_pairs={{32,160},{33,161},{34,162},{35,163},{36,164},{37,165},{38,166},{39... | collective-permute-start | bytes 786440 | tf_op jit(solution)/shard_map/ppermute | solution.py:25
  18.2 7.5 %collective-permute-start.3 = (f32[256,128]{1,0:T(8,128)S(1)}, f32[256,128]{1,0:T(8,128)S(1)}, u32[]{:S(2)}, u32[]{:S(2)}) collective-permute-start(f32[256,128]{1,0:T(8,128)S(1)} %get-tuple-element.17), channel_id=1, source_target_pairs={{0,3},{1,2},{16,19},{17,18},{32,35},{33,34},{48,51},{49,50},{64,67... | collective-permute-start | bytes 393224 | tf_op jit(solution)/shard_map/ppermute | solution.py:25
  20.2 6.8 %collective-permute-start.16 = (f32[192,128]{1,0:T(8,128)S(1)}, f32[192,128]{1,0:T(8,128)S(1)}, u32[]{:S(2)}, u32[]{:S(2)}) collective-permute-start(f32[192,128]{1,0:T(8,128)S(1)} %select_select_fusion.3), channel_id=1, source_target_pairs={{0,384},{1,385},{2,386},{3,387},{4,388},{5,389},{6,390},{7,391},{8... | collective-permute-start | bytes 294920 | tf_op jit(solution)/shard_map/ppermute | solution.py:25
  20.9 6.2 %collective-permute-start.17 = (f32[192,128]{1,0:T(8,128)S(1)}, f32[192,128]{1,0:T(8,128)S(1)}, u32[]{:S(2)}, u32[]{:S(2)}) collective-permute-start(f32[192,128]{1,0:T(8,128)S(1)} %select_select_fusion.3), channel_id=1, source_target_pairs={{0,64},{1,65},{2,66},{3,67},{4,68},{5,69},{6,70},{7,71},{8,72},{9,... | collective-permute-start | bytes 294920 | tf_op jit(solution)/shard_map/ppermute | solution.py:25
  21.6 5.5 %collective-permute-start.18 = (f32[192,128]{1,0:T(8,128)S(1)}, f32[192,128]{1,0:T(8,128)S(1)}, u32[]{:S(2)}, u32[]{:S(2)}) collective-permute-start(f32[192,128]{1,0:T(8,128)S(1)} %select_select_fusion.3), channel_id=1, source_target_pairs={{0,128},{1,129},{2,130},{3,131},{4,132},{5,133},{6,134},{7,135},{8... | collective-permute-start | bytes 294920 | tf_op jit(solution)/shard_map/ppermute | solution.py:25
  22.3 8.7 %collective-permute-start.9 = (f32[512,128]{1,0:T(8,128)S(1)}, f32[512,128]{1,0:T(8,128)S(1)}, u32[]{:S(2)}, u32[]{:S(2)}) collective-permute-start(f32[512,128]{1,0:T(8,128)S(1)} %broadcast_select_fusion.1), channel_id=1, source_target_pairs={{32,416},{33,417},{34,418},{35,419},{36,420},{37,421},{38,422},{39... | collective-permute-start | bytes 786440 | tf_op jit(solution)/shard_map/ppermute | solution.py:25
  25.8 19.3 %collective-permute-start.4 = (f32[256,128]{1,0:T(8,128)S(1)}, f32[256,128]{1,0:T(8,128)S(1)}, u32[]{:S(2)}, u32[]{:S(2)}) collective-permute-start(f32[256,128]{1,0:T(8,128)S(1)} %broadcast_select_fusion.3), channel_id=1, source_target_pairs={{0,8},{1,9},{2,10},{3,11},{16,24},{17,25},{18,26},{19,27},{32,40},... | collective-permute-start | bytes 393224 | tf_op jit(solution)/shard_map/ppermute | solution.py:25
  27.1 5.2 %collective-permute-start.19 = (f32[192,128]{1,0:T(8,128)S(1)}, f32[192,128]{1,0:T(8,128)S(1)}, u32[]{:S(2)}, u32[]{:S(2)}) collective-permute-start(f32[192,128]{1,0:T(8,128)S(1)} %select_select_fusion.2), channel_id=1, source_target_pairs={{0,448},{1,449},{2,450},{3,451},{4,452},{5,453},{6,454},{7,455},{8... | collective-permute-start | bytes 294920 | tf_op jit(solution)/shard_map/ppermute | solution.py:25
  27.8 8.3 %collective-permute-start.20 = (f32[192,128]{1,0:T(8,128)S(1)}, f32[192,128]{1,0:T(8,128)S(1)}, u32[]{:S(2)}, u32[]{:S(2)}) collective-permute-start(f32[192,128]{1,0:T(8,128)S(1)} %select_select_fusion.2), channel_id=1, source_target_pairs={{0,480},{1,481},{2,482},{3,483},{4,484},{5,485},{6,486},{7,487},{8... | collective-permute-start | bytes 294920 | tf_op jit(solution)/shard_map/ppermute | solution.py:25
  29.1 14.0 %collective-permute-start.21 = (f32[192,128]{1,0:T(8,128)S(1)}, f32[192,128]{1,0:T(8,128)S(1)}, u32[]{:S(2)}, u32[]{:S(2)}) collective-permute-start(f32[192,128]{1,0:T(8,128)S(1)} %select_select_fusion.2), channel_id=1, source_target_pairs={{0,416},{1,417},{2,418},{3,419},{4,420},{5,421},{6,422},{7,423},{8... | collective-permute-start | bytes 294920 | tf_op jit(solution)/shard_map/ppermute | solution.py:25
  31.1 18.6 %collective-permute-start.10 = (f32[512,128]{1,0:T(8,128)S(1)}, f32[512,128]{1,0:T(8,128)S(1)}, u32[]{:S(2)}, u32[]{:S(2)}) collective-permute-start(f32[512,128]{1,0:T(8,128)S(1)} %broadcast_select_fusion.2), channel_id=1, source_target_pairs={{32,96},{33,97},{34,98},{35,99},{36,100},{37,101},{38,102},{39,103... | collective-permute-start | bytes 786440 | tf_op jit(solution)/shard_map/ppermute | solution.py:25
  32.4 17.3 %collective-permute-start.11 = (f32[512,128]{1,0:T(8,128)S(1)}, f32[512,128]{1,0:T(8,128)S(1)}, u32[]{:S(2)}, u32[]{:S(2)}) collective-permute-start(f32[512,128]{1,0:T(8,128)S(1)} %broadcast_select_fusion.2), channel_id=1, source_target_pairs={{160,224},{161,225},{162,226},{163,227},{164,228},{165,229},{166,2... | collective-permute-start | bytes 786440 | tf_op jit(solution)/shard_map/ppermute | solution.py:25
  36.1 13.6 %collective-permute-start.12 = (f32[512,128]{1,0:T(8,128)S(1)}, f32[512,128]{1,0:T(8,128)S(1)}, u32[]{:S(2)}, u32[]{:S(2)}) collective-permute-start(f32[512,128]{1,0:T(8,128)S(1)} %broadcast_select_fusion.2), channel_id=1, source_target_pairs={{32,64},{33,65},{34,66},{35,67},{36,68},{37,69},{38,70},{39,71},{4... | collective-permute-start | bytes 786440 | tf_op jit(solution)/shard_map/ppermute | solution.py:25
  43.2 3.3 %collective-permute-start.22 = (f32[192,128]{1,0:T(8,128)S(1)}, f32[192,128]{1,0:T(8,128)S(1)}, u32[]{:S(2)}, u32[]{:S(2)}) collective-permute-start(f32[192,128]{1,0:T(8,128)S(1)} %select_select_fusion.1.mine), channel_id=1, source_target_pairs={{0,16},{1,17},{2,18},{3,19},{4,20},{5,21},{6,22},{7,23},{8,24},{9,... | collective-permute-start | bytes 294920 | tf_op jit(solution)/shard_map/ppermute | solution.py:25
  45.1 7.0 %collective-permute-start.5 = (f32[256,128]{1,0:T(8,128)S(1)}, f32[256,128]{1,0:T(8,128)S(1)}, u32[]{:S(2)}, u32[]{:S(2)}) collective-permute-start(f32[256,128]{1,0:T(8,128)S(1)} %broadcast_select_fusion.4), channel_id=1, source_target_pairs={{0,4},{1,5},{2,6},{3,7},{8,12},{9,13},{10,14},{11,15},{16,20},{17,... | collective-permute-start | bytes 393224 | tf_op jit(solution)/shard_map/ppermute | solution.py:25
  49.8 9.8 %collective-permute-start.23 = (f32[512,128]{1,0:T(8,128)S(1)}, f32[512,128]{1,0:T(8,128)S(1)}, u32[]{:S(2)}, u32[]{:S(2)}) collective-permute-start(f32[512,128]{1,0:T(8,128)S(1)} %select_select_fusion.cols_a), channel_id=1, source_target_pairs={{0,16},{1,17},{2,18},{3,19},{4,20},{5,21},{6,22},{7,23},{8,24},{9,... | collective-permute-start | bytes 786440 | tf_op jit(solution)/shard_map/ppermute | solution.py:25
  52.2 7.3 %collective-permute-start.6 = (f32[256,128]{1,0:T(8,128)S(1)}, f32[256,128]{1,0:T(8,128)S(1)}, u32[]{:S(2)}, u32[]{:S(2)}) collective-permute-start(f32[256,128]{1,0:T(8,128)S(1)} %broadcast_select_fusion.5.rows_a), channel_id=1, source_target_pairs={{0,1},{1,0},{2,3},{3,2},{4,5},{5,4},{6,7},{7,6},{8,9},{9,8},{10,11... | collective-permute-start | bytes 393224 | tf_op jit(solution)/shard_map/ppermute | solution.py:25
  (2 other events, 6.1 us)

commit v7 on v5

--- a/solution.py
+++ b/solution.py
@@ -104,11 +104,14 @@
     return i, lax.broadcasted_iota(jnp.int32, (NB, NB), 1)
 
 
-def pick_body(x, tile, rows, cols):
+def corner_body(x, tile):
     first = x[pl.ds(0, NB, stride=4), :]
     odd = (lax.axis_index("row") & 1) == 1
     tile[...] = jnp.where(odd, first.T, first)
-    rows[0:NB, :] = first
+
+
+def pick_body(x, rows, cols):
+    rows[0:NB, :] = x[pl.ds(0, NB, stride=4), :]
     rows[NB:, :] = x[pl.ds(4 * NB, NB, stride=4), :]
     for m in range(4):
         cols[NB * m : NB * (m + 1), :] = x[pl.ds(m, NB, stride=4), :]
@@ -224,7 +227,15 @@
     y = q & 3
     odd = (p & 1) == 1
     local = covariance.reshape(2 * NB * 4, NB)
-    tile, rows, cols = call(pick_body, tile_of(NB, 2 * NB, 4 * NB), 0, local)
+    tile = pl.pallas_call(
+        corner_body,
+        grid=(1,),
+        out_shape=tile_of(NB)[0],
+        in_specs=[pl.BlockSpec((4 * NB, NB), lambda i: (0, 0))],
+        out_specs=pl.BlockSpec((NB, NB), lambda i: (0, 0)),
+        compiler_params=PARAMS,
+    )(local[: 4 * NB])
+    rows, cols = call(pick_body, tile_of(2 * NB, 4 * NB), 0, local)
 
     cores = (0, 1)
     every = range(COLS)

time: 62.7 us -> 62.8 us (level)
    unnamed x4 -> x2, local copies, waits for them, and re-layouts: 1.05 us -> 0.01 us
    slice x0 -> x1, local copies, waits for them, and re-layouts: none -> 1.04 us  [per_device(): local[:4 * NB]]
where the time goes in v7:
time: 62.8 us; the launch traced here: 62.2 us
  starting transfers between devices  34.1 us (54%)
  waiting for transfers between devices  17.1 us (27%)
  Pallas kernels  9.1 us (14%)
  local copies, waits for them, and re-layouts  1.05 us (2%)
    ppermute x24, starting transfers between devices, move(): return lax.ppermute(value, ('row', 'col'), flat)  34.1 us
    ppermute x24, waiting for transfers between devices, move(): return lax.ppermute(value, ('row', 'col'), flat)  17.1 us
    pallas_call x4, Pallas kernels, call(): pl.pallas_call(body, out_shape=shapes, in_specs=[VMEM] * len(args), out_s...  9.01 us
  transfers between devices with their start and end apart: 24, of which 4 were waited for; matrix products, arithmetic and copies ran while one was open for 1% of the time, Pallas kernels for 10%

profile of v7, /device:TPU:40, one launch (start us, length us, event | category | flops | bytes accessed | tf_op | source)
XLA Modules:
  0.0 62.2 jit_solution(9353400422887828440)
XLA Ops:
  0.0 1.0 %slice.15 = f32[1,128,4,128]{3,2,1,0:T(4,128)S(1)} slice(f32[2,128,4,128]{3,2,1,0:T(4,128)} %param.1), slice={[0:1], [0:128], [0:4], [0:128]} | slice | bytes 524288 | tf_op jit(solution)/shard_map/slice | solution.py:237
  3.2 1.3 %collective-permute-start.7 = (f32[512,128]{1,0:T(8,128)S(1)}, f32[512,128]{1,0:T(8,128)S(1)}, u32[]{:S(2)}, u32[]{:S(2)}) collective-permute-start(f32[512,128]{1,0:T(8,128)S(1)} %get-tuple-element.17), channel_id=1, source_target_pairs={{0,32},{1,33},{2,34},{3,35},{4,36},{5,37},{6,38},{7,39},{8,40},{9,... | collective-permute-start | bytes 786440 | tf_op jit(solution)/shard_map/ppermute | solution.py:25
  4.6 0.7 %collective-permute-start.13 = (f32[192,128]{1,0:T(8,128)S(1)}, f32[192,128]{1,0:T(8,128)S(1)}, u32[]{:S(2)}, u32[]{:S(2)}) collective-permute-start(f32[192,128]{1,0:T(8,128)S(1)} %pad_maximum_fusion), channel_id=1, source_target_pairs={{0,12},{1,13},{2,14},{3,15},{16,28},{17,29},{18,30},{19,31}} | collective-permute-start | bytes 294920 | tf_op jit(solution)/shard_map/ppermute | solution.py:25
  5.3 0.7 %collective-permute-start.14 = (f32[192,128]{1,0:T(8,128)S(1)}, f32[192,128]{1,0:T(8,128)S(1)}, u32[]{:S(2)}, u32[]{:S(2)}) collective-permute-start(f32[192,128]{1,0:T(8,128)S(1)} %pad_maximum_fusion), channel_id=1, source_target_pairs={{0,4},{1,5},{2,6},{3,7},{16,20},{17,21},{18,22},{19,23}} | collective-permute-start | bytes 294920 | tf_op jit(solution)/shard_map/ppermute | solution.py:25
  6.0 0.7 %collective-permute-start.15 = (f32[192,128]{1,0:T(8,128)S(1)}, f32[192,128]{1,0:T(8,128)S(1)}, u32[]{:S(2)}, u32[]{:S(2)}) collective-permute-start(f32[192,128]{1,0:T(8,128)S(1)} %pad_maximum_fusion), channel_id=1, source_target_pairs={{0,8},{1,9},{2,10},{3,11},{16,24},{17,25},{18,26},{19,27}} | collective-permute-start | bytes 294920 | tf_op jit(solution)/shard_map/ppermute | solution.py:25
  6.6 10.6 %collective-permute-done.7 = f32[512,128]{1,0:T(8,128)S(1)} collective-permute-done((f32[512,128]{1,0:T(8,128)S(1)}, f32[512,128]{1,0:T(8,128)S(1)}, u32[]{:S(2)}, u32[]{:S(2)}) %collective-permute-start.7) | collective-permute-done | bytes 262176 | tf_op jit(solution)/shard_map/ppermute | solution.py:25
  17.3 1.3 %collective-permute-start.8 = (f32[512,128]{1,0:T(8,128)S(1)}, f32[512,128]{1,0:T(8,128)S(1)}, u32[]{:S(2)}, u32[]{:S(2)}) collective-permute-start(f32[512,128]{1,0:T(8,128)S(1)} %broadcast_select_fusion), channel_id=1, source_target_pairs={{32,160},{33,161},{34,162},{35,163},{36,164},{37,165},{38,166},{39... | collective-permute-start | bytes 786440 | tf_op jit(solution)/shard_map/ppermute | solution.py:25
  18.7 1.3 %collective-permute-start.3 = (f32[256,128]{1,0:T(8,128)S(1)}, f32[256,128]{1,0:T(8,128)S(1)}, u32[]{:S(2)}, u32[]{:S(2)}) collective-permute-start(f32[256,128]{1,0:T(8,128)S(1)} %get-tuple-element.15), channel_id=1, source_target_pairs={{0,3},{1,2},{16,19},{17,18},{32,35},{33,34},{48,51},{49,50},{64,67... | collective-permute-start | bytes 393224 | tf_op jit(solution)/shard_map/ppermute | solution.py:25
  22.1 0.8 %collective-permute-done.8 = f32[512,128]{1,0:T(8,128)S(1)} collective-permute-done((f32[512,128]{1,0:T(8,128)S(1)}, f32[512,128]{1,0:T(8,128)S(1)}, u32[]{:S(2)}, u32[]{:S(2)}) %collective-permute-start.8) | collective-permute-done | bytes 262176 | tf_op jit(solution)/shard_map/ppermute | solution.py:25
  22.9 1.4 %collective-permute-start.9 = (f32[512,128]{1,0:T(8,128)S(1)}, f32[512,128]{1,0:T(8,128)S(1)}, u32[]{:S(2)}, u32[]{:S(2)}) collective-permute-start(f32[512,128]{1,0:T(8,128)S(1)} %broadcast_select_fusion.1), channel_id=1, source_target_pairs={{32,416},{33,417},{34,418},{35,419},{36,420},{37,421},{38,422},{39... | collective-permute-start | bytes 786440 | tf_op jit(solution)/shard_map/ppermute | solution.py:25
  24.4 3.7 %collective-permute-start.4 = (f32[256,128]{1,0:T(8,128)S(1)}, f32[256,128]{1,0:T(8,128)S(1)}, u32[]{:S(2)}, u32[]{:S(2)}) collective-permute-start(f32[256,128]{1,0:T(8,128)S(1)} %broadcast_select_fusion.3), channel_id=1, source_target_pairs={{0,8},{1,9},{2,10},{3,11},{16,24},{17,25},{18,26},{19,27},{32,40},... | collective-permute-start | bytes 393224 | tf_op jit(solution)/shard_map/ppermute | solution.py:25
  28.2 1.3 %collective-permute-start.19 = (f32[192,128]{1,0:T(8,128)S(1)}, f32[192,128]{1,0:T(8,128)S(1)}, u32[]{:S(2)}, u32[]{:S(2)}) collective-permute-start(f32[192,128]{1,0:T(8,128)S(1)} %select_select_fusion.2), channel_id=1, source_target_pairs={{0,480},{1,481},{2,482},{3,483},{4,484},{5,485},{6,486},{7,487},{8... | collective-permute-start | bytes 294920 | tf_op jit(solution)/shard_map/ppermute | solution.py:25
  30.9 0.7 %collective-permute-start.10 = (f32[512,128]{1,0:T(8,128)S(1)}, f32[512,128]{1,0:T(8,128)S(1)}, u32[]{:S(2)}, u32[]{:S(2)}) collective-permute-start(f32[512,128]{1,0:T(8,128)S(1)} %broadcast_select_fusion.2), channel_id=1, source_target_pairs={{160,224},{161,225},{162,226},{163,227},{164,228},{165,229},{166,2... | collective-permute-start | bytes 786440 | tf_op jit(solution)/shard_map/ppermute | solution.py:25
  31.6 3.1 %collective-permute-done.19 = f32[192,128]{1,0:T(8,128)S(1)} collective-permute-done((f32[192,128]{1,0:T(8,128)S(1)}, f32[192,128]{1,0:T(8,128)S(1)}, u32[]{:S(2)}, u32[]{:S(2)}) %collective-permute-start.19) | collective-permute-done | bytes 98336 | tf_op jit(solution)/shard_map/ppermute | solution.py:25
  34.7 1.3 %collective-permute-start.11 = (f32[512,128]{1,0:T(8,128)S(1)}, f32[512,128]{1,0:T(8,128)S(1)}, u32[]{:S(2)}, u32[]{:S(2)}) collective-permute-start(f32[512,128]{1,0:T(8,128)S(1)} %broadcast_select_fusion.2), channel_id=1, source_target_pairs={{32,96},{33,97},{34,98},{35,99},{36,100},{37,101},{38,102},{39,103... | collective-permute-start | bytes 786440 | tf_op jit(solution)/shard_map/ppermute | solution.py:25
  36.0 5.8 %collective-permute-start.12 = (f32[512,128]{1,0:T(8,128)S(1)}, f32[512,128]{1,0:T(8,128)S(1)}, u32[]{:S(2)}, u32[]{:S(2)}) collective-permute-start(f32[512,128]{1,0:T(8,128)S(1)} %broadcast_select_fusion.2), channel_id=1, source_target_pairs={{32,64},{33,65},{34,66},{35,67},{36,68},{37,69},{38,70},{39,71},{4... | collective-permute-start | bytes 786440 | tf_op jit(solution)/shard_map/ppermute | solution.py:25
  41.8 1.9 %collective-permute-start.22 = (f32[192,128]{1,0:T(8,128)S(1)}, f32[192,128]{1,0:T(8,128)S(1)}, u32[]{:S(2)}, u32[]{:S(2)}) collective-permute-start(f32[192,128]{1,0:T(8,128)S(1)} %select_select_fusion.1.mine), channel_id=1, source_target_pairs={{0,16},{1,17},{2,18},{3,19},{4,20},{5,21},{6,22},{7,23},{8,24},{9,... | collective-permute-start | bytes 294920 | tf_op jit(solution)/shard_map/ppermute | solution.py:25
  43.8 2.3 %collective-permute-start.5 = (f32[256,128]{1,0:T(8,128)S(1)}, f32[256,128]{1,0:T(8,128)S(1)}, u32[]{:S(2)}, u32[]{:S(2)}) collective-permute-start(f32[256,128]{1,0:T(8,128)S(1)} %broadcast_select_fusion.4), channel_id=1, source_target_pairs={{0,4},{1,5},{2,6},{3,7},{8,12},{9,13},{10,14},{11,15},{16,20},{17,... | collective-permute-start | bytes 393224 | tf_op jit(solution)/shard_map/ppermute | solution.py:25
  46.1 3.2 %shard_map.19 = (f32[128,128]{1,0:T(8,128)S(1)}, f32[128,128]{1,0:T(8,128)S(1)}, f32[128,128]{1,0:T(8,128)S(1)}) custom-call(f32[192,128]{1,0:T(8,128)S(1)} %select_select_fusion.1.mine, f32[192,128]{1,0:T(8,128)S(1)} %collective-permute-done.22.other), custom_call_target="tpu_custom_call" | custom-call | tf_op jit(solution)/shard_map/pallas_call | solution.py:198
  49.4 2.1 %collective-permute-start.23 = (f32[512,128]{1,0:T(8,128)S(1)}, f32[512,128]{1,0:T(8,128)S(1)}, u32[]{:S(2)}, u32[]{:S(2)}) collective-permute-start(f32[512,128]{1,0:T(8,128)S(1)} %select_select_fusion.cols_a), channel_id=1, source_target_pairs={{0,16},{1,17},{2,18},{3,19},{4,20},{5,21},{6,22},{7,23},{8,24},{9,... | collective-permute-start | bytes 786440 | tf_op jit(solution)/shard_map/ppermute | solution.py:25
  51.6 2.4 %collective-permute-start.6 = (f32[256,128]{1,0:T(8,128)S(1)}, f32[256,128]{1,0:T(8,128)S(1)}, u32[]{:S(2)}, u32[]{:S(2)}) collective-permute-start(f32[256,128]{1,0:T(8,128)S(1)} %broadcast_select_fusion.5.rows_a), channel_id=1, source_target_pairs={{0,1},{1,0},{2,3},{3,2},{4,5},{5,4},{6,7},{7,6},{8,9},{9,8},{10,11... | collective-permute-start | bytes 393224 | tf_op jit(solution)/shard_map/ppermute | solution.py:25
  53.9 2.7 %shard_map.20.w1 = f32[128,128]{1,0:T(8,128)S(1)} custom-call(f32[128,128]{1,0:T(8,128)S(1)} %get-tuple-element.19.s11, f32[8,128]{1,0:T(8,128)S(1)} %slice.19.mark), custom_call_target="tpu_custom_call" | custom-call | flops 1000000000 | bytes 1000000000 | tf_op jit(solution)/shard_map/pallas_call | solution.py:198
  56.7 2.5 %collective-permute-done.6.rows_b = f32[256,128]{1,0:T(8,128)S(1)} collective-permute-done((f32[256,128]{1,0:T(8,128)S(1)}, f32[256,128]{1,0:T(8,128)S(1)}, u32[]{:S(2)}, u32[]{:S(2)}) %collective-permute-start.6) | collective-permute-done | bytes 131104 | tf_op jit(solution)/shard_map/ppermute | solution.py:25
  59.2 3.1 %shard_map.21 = f32[1024,128]{1,0:T(8,128)} custom-call(f32[1024,128]{1,0:T(8,128)S(1)} %bitcast.4, f32[256,128]{1,0:T(8,128)S(1)} %broadcast_select_fusion.5.rows_a, f32[256,128]{1,0:T(8,128)S(1)} %collective-permute-done.6.rows_b, f32[512,128]{1,0:T(8,128)S(1)} %select_select_fusion.cols_a, f32[512,128]{1,0:T(8,128)S(1)} %collective-permute-done.23.cols_b, ...), custom_call_target="tpu_custom_call" | custom-call | tf_op jit(solution)/shard_map/pallas_call | solution.py:198
  (46 shorter events, 5.8 us)
Async XLA Ops:
  1.1 3.4 %collective-permute-start = (f32[128,128]{1,0:T(8,128)S(1)}, f32[128,128]{1,0:T(8,128)S(1)}, u32[]{:S(2)}, u32[]{:S(2)}) collective-permute-start(f32[128,128]{1,0:T(8,128)S(1)} %shard_map.18), channel_id=1, source_target_pairs={{0,1},{1,0},{16,17},{17,16}} | collective-permute-start | bytes 196616 | tf_op jit(solution)/shard_map/ppermute | solution.py:25
  1.8 2.7 %collective-permute-start.2 = (f32[128,128]{1,0:T(8,128)S(1)}, f32[128,128]{1,0:T(8,128)S(1)}, u32[]{:S(2)}, u32[]{:S(2)}) collective-permute-start(f32[128,128]{1,0:T(8,128)S(1)} %shard_map.18), channel_id=1, source_target_pairs={{0,2},{1,3},{16,18},{17,19}} | collective-permute-start | bytes 196616 | tf_op jit(solution)/shard_map/ppermute | solution.py:25
  2.5 2.1 %collective-permute-start.1 = (f32[128,128]{1,0:T(8,128)S(1)}, f32[128,128]{1,0:T(8,128)S(1)}, u32[]{:S(2)}, u32[]{:S(2)}) collective-permute-start(f32[128,128]{1,0:T(8,128)S(1)} %shard_map.18), channel_id=1, source_target_pairs={{0,3},{1,2},{16,19},{17,18}} | collective-permute-start | bytes 196616 | tf_op jit(solution)/shard_map/ppermute | solution.py:25
  3.2 14.1 %collective-permute-start.7 = (f32[512,128]{1,0:T(8,128)S(1)}, f32[512,128]{1,0:T(8,128)S(1)}, u32[]{:S(2)}, u32[]{:S(2)}) collective-permute-start(f32[512,128]{1,0:T(8,128)S(1)} %get-tuple-element.17), channel_id=1, source_target_pairs={{0,32},{1,33},{2,34},{3,35},{4,36},{5,37},{6,38},{7,39},{8,40},{9,... | collective-permute-start | bytes 786440 | tf_op jit(solution)/shard_map/ppermute | solution.py:25
  4.6 15.4 %collective-permute-start.13 = (f32[192,128]{1,0:T(8,128)S(1)}, f32[192,128]{1,0:T(8,128)S(1)}, u32[]{:S(2)}, u32[]{:S(2)}) collective-permute-start(f32[192,128]{1,0:T(8,128)S(1)} %pad_maximum_fusion), channel_id=1, source_target_pairs={{0,12},{1,13},{2,14},{3,15},{16,28},{17,29},{18,30},{19,31}} | collective-permute-start | bytes 294920 | tf_op jit(solution)/shard_map/ppermute | solution.py:25
  5.3 14.7 %collective-permute-start.14 = (f32[192,128]{1,0:T(8,128)S(1)}, f32[192,128]{1,0:T(8,128)S(1)}, u32[]{:S(2)}, u32[]{:S(2)}) collective-permute-start(f32[192,128]{1,0:T(8,128)S(1)} %pad_maximum_fusion), channel_id=1, source_target_pairs={{0,4},{1,5},{2,6},{3,7},{16,20},{17,21},{18,22},{19,23}} | collective-permute-start | bytes 294920 | tf_op jit(solution)/shard_map/ppermute | solution.py:25
  6.0 14.1 %collective-permute-start.15 = (f32[192,128]{1,0:T(8,128)S(1)}, f32[192,128]{1,0:T(8,128)S(1)}, u32[]{:S(2)}, u32[]{:S(2)}) collective-permute-start(f32[192,128]{1,0:T(8,128)S(1)} %pad_maximum_fusion), channel_id=1, source_target_pairs={{0,8},{1,9},{2,10},{3,11},{16,24},{17,25},{18,26},{19,27}} | collective-permute-start | bytes 294920 | tf_op jit(solution)/shard_map/ppermute | solution.py:25
  17.3 5.6 %collective-permute-start.8 = (f32[512,128]{1,0:T(8,128)S(1)}, f32[512,128]{1,0:T(8,128)S(1)}, u32[]{:S(2)}, u32[]{:S(2)}) collective-permute-start(f32[512,128]{1,0:T(8,128)S(1)} %broadcast_select_fusion), channel_id=1, source_target_pairs={{32,160},{33,161},{34,162},{35,163},{36,164},{37,165},{38,166},{39... | collective-permute-start | bytes 786440 | tf_op jit(solution)/shard_map/ppermute | solution.py:25
  18.7 5.6 %collective-permute-start.3 = (f32[256,128]{1,0:T(8,128)S(1)}, f32[256,128]{1,0:T(8,128)S(1)}, u32[]{:S(2)}, u32[]{:S(2)}) collective-permute-start(f32[256,128]{1,0:T(8,128)S(1)} %get-tuple-element.15), channel_id=1, source_target_pairs={{0,3},{1,2},{16,19},{17,18},{32,35},{33,34},{48,51},{49,50},{64,67... | collective-permute-start | bytes 393224 | tf_op jit(solution)/shard_map/ppermute | solution.py:25
  20.1 8.0 %collective-permute-start.16 = (f32[192,128]{1,0:T(8,128)S(1)}, f32[192,128]{1,0:T(8,128)S(1)}, u32[]{:S(2)}, u32[]{:S(2)}) collective-permute-start(f32[192,128]{1,0:T(8,128)S(1)} %select_select_fusion.3), channel_id=1, source_target_pairs={{0,64},{1,65},{2,66},{3,67},{4,68},{5,69},{6,70},{7,71},{8,72},{9,... | collective-permute-start | bytes 294920 | tf_op jit(solution)/shard_map/ppermute | solution.py:25
  20.7 7.4 %collective-permute-start.17 = (f32[192,128]{1,0:T(8,128)S(1)}, f32[192,128]{1,0:T(8,128)S(1)}, u32[]{:S(2)}, u32[]{:S(2)}) collective-permute-start(f32[192,128]{1,0:T(8,128)S(1)} %select_select_fusion.3), channel_id=1, source_target_pairs={{0,384},{1,385},{2,386},{3,387},{4,388},{5,389},{6,390},{7,391},{8... | collective-permute-start | bytes 294920 | tf_op jit(solution)/shard_map/ppermute | solution.py:25
  21.4 6.7 %collective-permute-start.18 = (f32[192,128]{1,0:T(8,128)S(1)}, f32[192,128]{1,0:T(8,128)S(1)}, u32[]{:S(2)}, u32[]{:S(2)}) collective-permute-start(f32[192,128]{1,0:T(8,128)S(1)} %select_select_fusion.3), channel_id=1, source_target_pairs={{0,128},{1,129},{2,130},{3,131},{4,132},{5,133},{6,134},{7,135},{8... | collective-permute-start | bytes 294920 | tf_op jit(solution)/shard_map/ppermute | solution.py:25
  22.9 7.9 %collective-permute-start.9 = (f32[512,128]{1,0:T(8,128)S(1)}, f32[512,128]{1,0:T(8,128)S(1)}, u32[]{:S(2)}, u32[]{:S(2)}) collective-permute-start(f32[512,128]{1,0:T(8,128)S(1)} %broadcast_select_fusion.1), channel_id=1, source_target_pairs={{32,416},{33,417},{34,418},{35,419},{36,420},{37,421},{38,422},{39... | collective-permute-start | bytes 786440 | tf_op jit(solution)/shard_map/ppermute | solution.py:25
  24.4 19.4 %collective-permute-start.4 = (f32[256,128]{1,0:T(8,128)S(1)}, f32[256,128]{1,0:T(8,128)S(1)}, u32[]{:S(2)}, u32[]{:S(2)}) collective-permute-start(f32[256,128]{1,0:T(8,128)S(1)} %broadcast_select_fusion.3), channel_id=1, source_target_pairs={{0,8},{1,9},{2,10},{3,11},{16,24},{17,25},{18,26},{19,27},{32,40},... | collective-permute-start | bytes 393224 | tf_op jit(solution)/shard_map/ppermute | solution.py:25
  28.2 6.5 %collective-permute-start.19 = (f32[192,128]{1,0:T(8,128)S(1)}, f32[192,128]{1,0:T(8,128)S(1)}, u32[]{:S(2)}, u32[]{:S(2)}) collective-permute-start(f32[192,128]{1,0:T(8,128)S(1)} %select_select_fusion.2), channel_id=1, source_target_pairs={{0,480},{1,481},{2,482},{3,483},{4,484},{5,485},{6,486},{7,487},{8... | collective-permute-start | bytes 294920 | tf_op jit(solution)/shard_map/ppermute | solution.py:25
  29.5 6.5 %collective-permute-start.20 = (f32[192,128]{1,0:T(8,128)S(1)}, f32[192,128]{1,0:T(8,128)S(1)}, u32[]{:S(2)}, u32[]{:S(2)}) collective-permute-start(f32[192,128]{1,0:T(8,128)S(1)} %select_select_fusion.2), channel_id=1, source_target_pairs={{0,448},{1,449},{2,450},{3,451},{4,452},{5,453},{6,454},{7,455},{8... | collective-permute-start | bytes 294920 | tf_op jit(solution)/shard_map/ppermute | solution.py:25
  30.1 11.6 %collective-permute-start.21 = (f32[192,128]{1,0:T(8,128)S(1)}, f32[192,128]{1,0:T(8,128)S(1)}, u32[]{:S(2)}, u32[]{:S(2)}) collective-permute-start(f32[192,128]{1,0:T(8,128)S(1)} %select_select_fusion.2), channel_id=1, source_target_pairs={{0,416},{1,417},{2,418},{3,419},{4,420},{5,421},{6,422},{7,423},{8... | collective-permute-start | bytes 294920 | tf_op jit(solution)/shard_map/ppermute | solution.py:25
  30.9 18.4 %collective-permute-start.10 = (f32[512,128]{1,0:T(8,128)S(1)}, f32[512,128]{1,0:T(8,128)S(1)}, u32[]{:S(2)}, u32[]{:S(2)}) collective-permute-start(f32[512,128]{1,0:T(8,128)S(1)} %broadcast_select_fusion.2), channel_id=1, source_target_pairs={{160,224},{161,225},{162,226},{163,227},{164,228},{165,229},{166,2... | collective-permute-start | bytes 786440 | tf_op jit(solution)/shard_map/ppermute | solution.py:25
  34.7 14.6 %collective-permute-start.11 = (f32[512,128]{1,0:T(8,128)S(1)}, f32[512,128]{1,0:T(8,128)S(1)}, u32[]{:S(2)}, u32[]{:S(2)}) collective-permute-start(f32[512,128]{1,0:T(8,128)S(1)} %broadcast_select_fusion.2), channel_id=1, source_target_pairs={{32,96},{33,97},{34,98},{35,99},{36,100},{37,101},{38,102},{39,103... | collective-permute-start | bytes 786440 | tf_op jit(solution)/shard_map/ppermute | solution.py:25
  36.0 13.3 %collective-permute-start.12 = (f32[512,128]{1,0:T(8,128)S(1)}, f32[512,128]{1,0:T(8,128)S(1)}, u32[]{:S(2)}, u32[]{:S(2)}) collective-permute-start(f32[512,128]{1,0:T(8,128)S(1)} %broadcast_select_fusion.2), channel_id=1, source_target_pairs={{32,64},{33,65},{34,66},{35,67},{36,68},{37,69},{38,70},{39,71},{4... | collective-permute-start | bytes 786440 | tf_op jit(solution)/shard_map/ppermute | solution.py:25
  41.8 4.3 %collective-permute-start.22 = (f32[192,128]{1,0:T(8,128)S(1)}, f32[192,128]{1,0:T(8,128)S(1)}, u32[]{:S(2)}, u32[]{:S(2)}) collective-permute-start(f32[192,128]{1,0:T(8,128)S(1)} %select_select_fusion.1.mine), channel_id=1, source_target_pairs={{0,16},{1,17},{2,18},{3,19},{4,20},{5,21},{6,22},{7,23},{8,24},{9,... | collective-permute-start | bytes 294920 | tf_op jit(solution)/shard_map/ppermute | solution.py:25
  43.8 7.8 %collective-permute-start.5 = (f32[256,128]{1,0:T(8,128)S(1)}, f32[256,128]{1,0:T(8,128)S(1)}, u32[]{:S(2)}, u32[]{:S(2)}) collective-permute-start(f32[256,128]{1,0:T(8,128)S(1)} %broadcast_select_fusion.4), channel_id=1, source_target_pairs={{0,4},{1,5},{2,6},{3,7},{8,12},{9,13},{10,14},{11,15},{16,20},{17,... | collective-permute-start | bytes 393224 | tf_op jit(solution)/shard_map/ppermute | solution.py:25
  49.4 9.8 %collective-permute-start.23 = (f32[512,128]{1,0:T(8,128)S(1)}, f32[512,128]{1,0:T(8,128)S(1)}, u32[]{:S(2)}, u32[]{:S(2)}) collective-permute-start(f32[512,128]{1,0:T(8,128)S(1)} %select_select_fusion.cols_a), channel_id=1, source_target_pairs={{0,16},{1,17},{2,18},{3,19},{4,20},{5,21},{6,22},{7,23},{8,24},{9,... | collective-permute-start | bytes 786440 | tf_op jit(solution)/shard_map/ppermute | solution.py:25
  51.6 7.6 %collective-permute-start.6 = (f32[256,128]{1,0:T(8,128)S(1)}, f32[256,128]{1,0:T(8,128)S(1)}, u32[]{:S(2)}, u32[]{:S(2)}) collective-permute-start(f32[256,128]{1,0:T(8,128)S(1)} %broadcast_select_fusion.5.rows_a), channel_id=1, source_target_pairs={{0,1},{1,0},{2,3},{3,2},{4,5},{5,4},{6,7},{7,6},{8,9},{9,8},{10,11... | collective-permute-start | bytes 393224 | tf_op jit(solution)/shard_map/ppermute | solution.py:25
  (1 other events, 3.2 us)
